TPU v7x, 32 devices: a whole 2x2x4 slice. The times are simulated.
32 devices in a mesh: batch: 2 (over y), grp: 16 (over z, x, core).
Axes of the slice: x: 2, y: 2, z: 4, core: 2. Of those that a mesh axis runs over, the one named last changes fastest.
Arguments:
- amps: bfloat16 [6, 16, 1024, 128], P('batch', None, 'grp'), may hold values from -6 to 6
- cycle_inter: bfloat16 [6, 1024, 8, 128], P('batch', 'grp'), may hold values from -0.21875 to 0.21875
- k_irrep: int32 [6], replicated, may hold values from 0 to 7
- i_irrep: int32 [16], replicated, may hold values from 0 to 7
- j_irrep: int32 [8], replicated, may hold values from 0 to 7
- virt_count: int32 [8], replicated, may hold values from 64 to 128, as said below
Outputs:
- cycle_term: bfloat16 [16, 8, 1024, 128], P(None, 'batch', 'grp')
Inputs may be any that keep to these rules, and one draw needn't show every extreme that they name: `virt_count`: together the counts are 800.
All inputs are finite; a program needn't handle non-finite values.
Results may differ from a plain program's by a relative error of at most 0.013.
Values may be sent and summed in bfloat16 or wider, within the bound.
No kernel may reach another device: no remote copies, remote signals or barrier semaphores. Data moves between devices by JAX's collectives and lax.ppermute only.
A program may use at most 64 MiB of HBM per device.

v0:
```python
import jax
import jax.numpy as jnp
from jax import lax
from jax.sharding import PartitionSpec as P


def shards(amps, cycle_inter, k_irrep, i_irrep, j_irrep, virt_count):
    k_local = amps.shape[0]
    slab_size = amps.shape[2]
    width = amps.shape[3]
    n_irrep = virt_count.shape[0]
    j_total = cycle_inter.shape[2]
    irreps = jnp.arange(n_irrep, dtype=jnp.int32)
    slot_pos = jnp.arange(width, dtype=jnp.int32)

    def count_of(labels):
        return jnp.sum(jnp.where(labels[..., None] == irreps, virt_count, 0), axis=-1)

    k_first = lax.axis_index("batch") * k_local
    k_labels = lax.dynamic_slice_in_dim(k_irrep, k_first, k_local)
    c_index = lax.axis_index("grp") * slab_size + jnp.arange(slab_size, dtype=jnp.int32)
    c_labels = c_index // width
    c_live = c_index % width < count_of(c_labels)
    a_labels = jnp.bitwise_xor(
        jnp.bitwise_xor(k_labels[:, None, None], i_irrep[None, :, None]), c_labels[None, None, :]
    )
    amp_mask = c_live[None, None, :, None] & (slot_pos < count_of(a_labels)[..., None])
    masked_amps = jnp.where(amp_mask, amps, jnp.zeros((), amps.dtype))
    b_labels = jnp.bitwise_xor(
        jnp.bitwise_xor(k_labels[:, None, None], c_labels[None, :, None]), j_irrep[None, None, :]
    )
    inter_mask = c_live[None, :, None, None] & (slot_pos < count_of(b_labels)[..., None])
    masked_inter = jnp.where(inter_mask, cycle_inter, jnp.zeros((), cycle_inter.dtype))
    sorted_amps = lax.all_to_all(masked_amps, "grp", split_axis=1, concat_axis=2, tiled=True)
    whole_inter = lax.all_gather(masked_inter, "grp", axis=1, tiled=True)
    i_count = sorted_amps.shape[1]
    i_labels = lax.dynamic_slice_in_dim(i_irrep, lax.axis_index("grp") * i_count, i_count)
    k_source = jnp.bitwise_xor(irreps[None, :], k_labels[:, None])
    amp_blocks = sorted_amps.reshape(k_local, i_count, n_irrep, width, width)
    amp_perm = jnp.take_along_axis(amp_blocks, k_source[:, None, :, None, None], axis=2)
    inter_blocks = whole_inter.reshape(k_local, n_irrep, width, j_total, width)
    inter_perm = jnp.take_along_axis(inter_blocks, k_source[:, :, None, None, None], axis=1)
    products = jnp.einsum(
        "kiqca,kqcjb->iqajb", amp_perm, inter_perm, preferred_element_type=jnp.float32
    )
    i_source = jnp.bitwise_xor(irreps[None, :], i_labels[:, None])
    partial_value = jnp.take_along_axis(products, i_source[:, :, None, None, None], axis=1)
    partial_value = jnp.transpose(partial_value, (0, 3, 1, 2, 4)).reshape(
        i_count, j_total, n_irrep * width, width
    )
    rounded = partial_value.astype(jnp.bfloat16)
    resorted = lax.all_to_all(rounded, "grp", split_axis=2, concat_axis=0, tiled=True)
    return lax.psum_scatter(
        resorted.astype(jnp.float32).astype(jnp.bfloat16), "batch", scatter_dimension=1, tiled=True
    )


def solution(mesh):
    return jax.shard_map(
        shards,
        mesh=mesh,
        in_specs=(P("batch", None, "grp", None), P("batch", "grp", None, None), P(), P(), P(), P()),
        out_specs=P(None, "batch", "grp", None),
        check_vma=False,
    )
```

profile of v0, /device:TPU:1, one launch (start us, length us, event | category | flops | bytes accessed | tf_op | source)
XLA Modules:
  0.0 206.1 jit_solution(5988143826144996087)
XLA Ops:
  6.6 0.7 dynamic_slice.7
  7.3 0.1 broadcast_xor_fusion.3
  7.4 0.7 select_reduce_fusion.2
  8.1 0.7 broadcast_xor_fusion.1
  8.8 0.8 select_reduce_fusion.1
  9.6 0.1 copy.26
  9.7 2.1 %fusion.11 = bf16[3,64,8,128]{3,2,1,0:T(8,128)(2,1)} fusion(bf16[3,64,8,128]{3,2,1,0:T(8,128)(2,1)} %param.7, s32[3,64,8]{2,1,0:T(8,128)S(1)} %copy.26, pred[64]{0:T(512)(128)(4,1)S(1)} %fusion.18), kind=kLoop, calls=%fused_computation.17 | loop fusion | flops 589824 | bytes 792640 | tf_op jit(solution)/shard_map/jit(_where)/select_n | solution.py:33
  11.8 0.7 broadcast_xor_fusion.2
  12.6 0.1 broadcast_xor_fusion
  12.6 0.8 select_reduce_fusion
  13.5 2.3 %fusion.8 = bf16[3,16,64,128]{3,2,0,1:T(8,128)(2,1)} fusion(bf16[3,16,64,128]{3,2,1,0:T(8,128)(2,1)} %param.6, s32[3,16,64]{2,0,1:T(4,128)S(1)} %copy.27, pred[64]{0:T(512)(128)(4,1)S(1)} %fusion.18), kind=kLoop, calls=%fused_computation.12 | loop fusion | flops 1179648 | bytes 1585216 | tf_op jit(solution)/shard_map/jit(_where)/select_n | solution.py:28
  15.8 7.3 %all-to-all-start = ((bf16[3,16,64,128]{3,2,0,1:T(8,128)(2,1)}), bf16[3,16,64,128]{3,2,0,1:T(8,128)(2,1)S(1)}, u32[]{:S(2)}, u32[]{:S(2)}) async-start(bf16[3,16,64,128]{3,2,0,1:T(8,128)(2,1)} %fusion.8), calls=%async_computation | async-start | bytes 1572864 | tf_op jit(solution)/shard_map/all_to_all | solution.py:34
  23.2 0.1 fusion.14
  23.2 0.1 reshape.379
  23.3 0.7 dynamic_slice.6
  24.0 0.7 fusion.19
  24.7 0.7 compare_and_fusion
  25.4 0.1 fusion.17
  25.5 27.7 %all-to-all-done = bf16[3,16,64,128]{3,2,0,1:T(8,128)(2,1)S(1)} async-done(((bf16[3,16,64,128]{3,2,0,1:T(8,128)(2,1)}), bf16[3,16,64,128]{3,2,0,1:T(8,128)(2,1)S(1)}, u32[]{:S(2)}, u32[]{:S(2)}) %all-to-all-start) | async-done | bytes 786464 | tf_op jit(solution)/shard_map/all_to_all | solution.py:34
  53.2 0.1 copy.29
  53.2 0.8 gather_fusion.2
  54.0 36.8 %all-gather.2.cloned.1.call-done = bf16[3,1024,8,128]{3,2,1,0:T(8,128)(2,1)} async-done(((bf16[3,64,8,128]{3,2,1,0:T(8,128)(2,1)}), bf16[3,1024,8,128]{3,2,1,0:T(8,128)(2,1)}) %all-gather.2.cloned.1.call-update) | async-done | bytes 6291472 | tf_op jit(solution)/shard_map/all_gather | solution.py:35
  90.8 7.4 %gather_fusion.1 = bf16[24,128,8,128]{3,2,1,0:T(8,128)(2,1)} fusion(bf16[3,8,128,8,128]{4,3,2,1,0:T(8,128)(2,1)} %bitcast.39, s32[24]{0:T(128)S(1)} %reshape.379), kind=kCustom, calls=%fused_computation.1 | custom fusion | bytes 12583104 | tf_op jit(solution)/shard_map/jit(take_along_axis)/gather | solution.py:42
  98.1 3.4 %broadcast_select_fusion = bf16[3,8,128,8,128]{4,3,2,1,0:T(8,128)(2,1)S(1)} fusion(bf16[3,8,128,8,128]{4,3,2,1,0:T(8,128)(2,1)} %bitcast.36, pred[3,8]{1,0:T(4,128)(4,1)S(1)} %fusion.17), kind=kLoop, calls=%fused_computation.5 | loop fusion | flops 3145728 | bytes 12582936 | tf_op jit(solution)/shard_map/jit(take_along_axis)/select_n | solution.py:42
  101.6 3.5 %fusion.3 = bf16[8,128,8,128]{1,3,2,0:T(8,128)(2,1)} fusion(bf16[3,8,128,8,128]{4,3,2,1,0:T(8,128)(2,1)S(1)} %broadcast_select_fusion, bf16[3,8,128,128]{3,2,1,0:T(8,128)(2,1)S(1)} %bitcast.41, pred[3,8]{1,0:T(4,128)(4,1)S(1)} %fusion.17), kind=kOutput, calls=%fused_computation.8 | convolution fusion | flops 805699584 | bytes 9175064 | tf_op jit(solution)/shard_map/kiqca,kqcjb->iqajb/dot_general | solution.py:43
  105.1 2.5 %gather_fusion = bf16[8,128,8,128]{1,3,2,0:T(8,128)(2,1)S(1)} fusion(bf16[8,128,8,128]{1,3,2,0:T(8,128)(2,1)} %fusion.3, s32[1024]{0:T(1024)S(1)} %pad_clamp_fusion), kind=kCustom, calls=%fused_computation | custom fusion | bytes 4194336 | tf_op jit(solution)/shard_map/jit(take_along_axis)/gather | solution.py:47
  107.7 2.0 fusion.6
  109.7 3.2 %copy.40 = bf16[1,8,8,128,128]{4,1,3,2,0:T(8,128)(2,1)S(1)} copy(bf16[1,8,8,128,128]{3,4,1,2,0:T(8,128)(2,1)} %fusion.6) | data formatting | bytes 4194304 | tf_op jit(solution)/shard_map/convert_element_type | solution.py:51
  112.9 51.0 %all_to_all.27 = bf16[1,8,1024,128]{3,1,0,2:T(8,128)(2,1)S(1)} all-to-all(bf16[1,8,1024,128]{3,1,0,2:T(8,128)(2,1)S(1)} %bitcast.38), channel_id=1, replica_groups=mesh['batch'=2,'grp'=16] {'grp'}, dimensions={2} | all-to-all | bytes 4194304 | tf_op jit(solution)/shard_map/all_to_all | solution.py:52
  163.9 1.7 copy.34
  165.6 31.4 %reduce-scatter.2.cloned.1.call-done = bf16[16,4,64,128]{3,2,0,1:T(8,128)(2,1)} async-done(((bf16[16,8,64,128]{3,2,0,1:T(8,128)(2,1)}), bf16[16,4,64,128]{3,2,0,1:T(8,128)(2,1)}) %reduce-scatter.2.cloned.1.call-update) | async-done | bytes 1048592 | tf_op jit(solution)/shard_map/reduce_scatter | solution.py:53
  197.0 2.3 %copy.35 = bf16[16,4,64,128]{3,2,1,0:T(8,128)(2,1)} copy(bf16[16,4,64,128]{3,2,0,1:T(8,128)(2,1)} %reduce-scatter.2.cloned.1.call-done) | data formatting | bytes 2097152 | tf_op jit(solution)/shard_map/reduce_scatter | solution.py:53
  (10 shorter events, 0.1 us)
Async XLA Ops:
  6.5 16.8 %copy-start = (s32[16]{0:T(128)S(1)}, s32[16]{0:T(128)}, u32[]{:S(2)}) copy-start(s32[16]{0:T(128)} %param.9) | copy-start | bytes 196
  6.5 84.2 %all-gather.2.cloned.1.call-start = ((), (), s32[]{:S(2)}) async-start(), calls=%async_computation.3 | async-start | bytes 6684672 | tf_op jit(solution)/shard_map/all_gather | solution.py:35
  15.8 37.4 %all-to-all-start = ((bf16[3,16,64,128]{3,2,0,1:T(8,128)(2,1)}), bf16[3,16,64,128]{3,2,0,1:T(8,128)(2,1)S(1)}, u32[]{:S(2)}, u32[]{:S(2)}) async-start(bf16[3,16,64,128]{3,2,0,1:T(8,128)(2,1)} %fusion.8), calls=%async_computation | async-start | bytes 1572864 | tf_op jit(solution)/shard_map/all_to_all | solution.py:34
  23.1 173.9 %reduce-scatter.2.cloned.1.call-start = ((), (), s32[]{:S(2)}) async-start(), calls=%async_computation.4 | async-start | bytes 3145728 | tf_op jit(solution)/shard_map/reduce_scatter | solution.py:53
Sparse Core Ops, SparseCore 0:
  12.0 78.7 all-gather.1
  165.7 31.2 reduce-scatter.1
where the time goes:
time: 207 us; the launch traced here: 206 us
  waiting for transfers between devices  95.9 us (46%)
  blocking collectives  51 us (25%)
  local copies, waits for them, and re-layouts  19.5 us (9%)
  other arithmetic  15.4 us (7%)
  between operations  13.5 us (7%)
  starting transfers between devices  7.36 us (4%)
  matrix products  3.53 us (2%)
    all_to_all x1, blocking collectives, shards(): lax.all_to_all(rounded, 'grp', split_axis=2, concat_axis=0, tiled=True)  51 us
    all_gather x1, waiting for transfers between devices, shards(): whole_inter = lax.all_gather(masked_inter, 'grp', axis=1, tiled=True)  36.8 us
    reduce_scatter x1, waiting for transfers between devices, shards(): lax.psum_scatter(resorted.astype(jnp.float32).astype(jnp.bfloat16), 'batc...  31.4 us
    all_to_all x1, waiting for transfers between devices, shards(): lax.all_to_all(masked_amps, 'grp', split_axis=1, concat_axis=2, tiled=True)  27.7 us
    gather x2, local copies, waits for them, and re-layouts, shards(): jnp.take_along_axis(inter_blocks, k_source[:, :, None, None, None], axis=1)  7.46 us
    all_to_all x1, starting transfers between devices, shards(): lax.all_to_all(masked_amps, 'grp', split_axis=1, concat_axis=2, tiled=True)  7.32 us
  transfers between devices with their start and end apart: 3, of which 3 were waited for; matrix products, arithmetic and copies ran while one was open for 3% of the time, Pallas kernels for 0%

commit v1 on v0

v1 whole, which is shorter than its diff:
```python
import functools

import jax
import jax.numpy as jnp
from jax import lax
from jax.experimental import pallas as pl
from jax.experimental.pallas import tpu as pltpu
from jax.sharding import PartitionSpec as P


def contract_kernel(n_k, width, labels_ref, *refs):
    amp_refs = refs[:n_k]
    inter_refs = refs[n_k:2 * n_k]
    out_ref = refs[2 * n_k]
    p = pl.program_id(0)
    n_irrep = pl.num_programs(0)
    j_count = out_ref.shape[1]
    i_label = labels_ref[n_k]
    j_first = n_k + 1
    count_first = j_first + j_count
    row = lax.broadcasted_iota(jnp.int32, (width, width), 0)
    col = lax.broadcasted_iota(jnp.int32, (width, width), 1)
    acc = None
    for k in range(n_k):
        c_count = labels_ref[count_first + (labels_ref[k] ^ i_label ^ p)]
        amp = amp_refs[k][...].reshape(width, width)
        amp = jnp.where(row < c_count, amp, jnp.zeros((), amp.dtype))
        inter = inter_refs[k][...].reshape(width, j_count * width)
        term = lax.dot_general(amp, inter, (((0,), (0,)), ((), ())), preferred_element_type=jnp.float32)
        acc = term if acc is None else acc + term
    a_count = labels_ref[count_first + p]
    parts, rows = out_ref.shape[0], out_ref.shape[2]
    for j in range(j_count):
        b_count = labels_ref[count_first + (p ^ i_label ^ labels_ref[j_first + j])]
        live = (row < a_count) & (col < b_count)
        block = jnp.where(live, acc[:, j * width:(j + 1) * width], 0.0).astype(out_ref.dtype)
        out_ref[:, j] = block.reshape(parts, rows, width)


def contract(labels, amps, inter, n_irrep, j_count):
    devices, _, slab, width = amps[0].shape
    parts = devices // n_irrep
    n_k = sum(x.shape[1] for x in amps)

    def block_of(k, at):
        def index(p, labels):
            return (labels[k] ^ labels[n_k] ^ p, at, 0, 0)
        return index

    amp_ops, amp_specs, inter_specs = [], [], []
    for a in amps:
        for at in range(a.shape[1]):
            amp_specs.append(pl.BlockSpec((parts, 1, slab, width), block_of(len(amp_ops), at)))
            amp_ops.append(a)
    for k in range(n_k):
        inter_specs.append(pl.BlockSpec((parts, 1, slab, j_count * width), block_of(k, k)))
    flops = 2 * n_k * n_irrep * width ** 3 * j_count
    return pl.pallas_call(
        functools.partial(contract_kernel, n_k, width),
        grid_spec=pltpu.PrefetchScalarGridSpec(
            num_scalar_prefetch=1,
            grid=(n_irrep,),
            in_specs=amp_specs + inter_specs,
            out_specs=pl.BlockSpec((parts, j_count, slab, width), lambda p, labels: (p, 0, 0, 0)),
        ),
        out_shape=jax.ShapeDtypeStruct((devices, j_count, slab, width), jnp.bfloat16),
        compiler_params=pltpu.CompilerParams(vmem_limit_bytes=48 * 2 ** 20),
        cost_estimate=pl.CostEstimate(flops=flops, bytes_accessed=flops // 128, transcendentals=0),
    )(labels, *amp_ops, *([inter] * n_k))


def shards(n_batch, n_grp, amps, cycle_inter, k_irrep, i_irrep, j_irrep, virt_count):
    k_local, i_total, slab, width = amps.shape
    n_irrep = virt_count.shape[0]
    j_total = cycle_inter.shape[2]
    j_count = j_total // n_batch
    me_b = lax.axis_index("batch")
    me_g = lax.axis_index("grp")
    i_count = i_total // n_grp

    split = cycle_inter.reshape(k_local, slab, n_batch, j_count * width)
    if n_batch == 2:
        swap = [(0, 1), (1, 0)]
        own = lax.dynamic_index_in_dim(split, me_b, 2, keepdims=False)
        away = lax.dynamic_index_in_dim(split, 1 - me_b, 2, keepdims=False)
        mine = jnp.concatenate([own, lax.ppermute(away, "batch", swap)])
        k_labels = jnp.concatenate([
            lax.dynamic_slice_in_dim(k_irrep, me_b * k_local, k_local),
            lax.dynamic_slice_in_dim(k_irrep, (1 - me_b) * k_local, k_local),
        ])
    else:
        mine = lax.all_to_all(split.transpose(2, 0, 1, 3), "batch", split_axis=0, concat_axis=0, tiled=True)
        mine = mine.reshape(n_batch * k_local, slab, j_count * width)
        k_labels = k_irrep
    inter_all = lax.all_gather(mine, "grp", axis=0, tiled=False)

    sends = amps.transpose(1, 0, 2, 3).reshape(n_grp, i_count, k_local, slab, width)
    got = lax.all_to_all(sends, "grp", split_axis=0, concat_axis=0, tiled=True)
    if n_batch == 2:
        amp_parts = [got, lax.ppermute(got, "batch", swap)]
    else:
        gathered = lax.all_gather(got, "batch", axis=0, tiled=False)
        amp_parts = [gathered[b] for b in range(n_batch)]

    j_labels = lax.dynamic_slice_in_dim(j_irrep, me_b * j_count, j_count)
    outs = []
    for i in range(i_count):
        i_label = lax.dynamic_slice_in_dim(i_irrep, me_g * i_count + i, 1)
        labels = jnp.concatenate([k_labels, i_label, j_labels, virt_count])
        outs.append(contract(labels, [a[:, i] for a in amp_parts], inter_all, n_irrep, j_count))
    partial = outs[0][:, None] if i_count == 1 else jnp.stack(outs, axis=1)
    result = lax.all_to_all(partial, "grp", split_axis=0, concat_axis=0, tiled=True)
    return result.reshape(i_total, j_count, slab, width)


def solution(mesh):
    return jax.shard_map(
        functools.partial(shards, mesh.shape["batch"], mesh.shape["grp"]),
        mesh=mesh,
        in_specs=(P("batch", None, "grp", None), P("batch", "grp", None, None), P(), P(), P(), P()),
        out_specs=P(None, "batch", "grp", None),
        check_vma=False,
    )
```

time: 207 us -> 138 us (0.67)
  waiting for transfers between devices: 95.9 us -> 37.7 us
  blocking collectives: 51 us -> 68.8 us
  other arithmetic: 15.4 us -> 0.78 us
  local copies, waits for them, and re-layouts: 19.5 us -> 5.65 us
  Pallas kernels: 0 us -> 8.27 us
  starting transfers between devices: 7.36 us -> 3.41 us
  matrix products: 3.53 us -> 0 us
    reduce_scatter x1 -> x0, waiting for transfers between devices: 31.4 us -> none  [shards(): lax.psum_scatter(resorted.astype(jnp.float32).astype(jnp.bfloat16), 'batc...]
    all_to_all x1 -> x0, waiting for transfers between devices: 27.7 us -> none  [shards(): lax.all_to_all(masked_amps, 'grp', split_axis=1, concat_axis=2, tiled=True)]
    ppermute x0 -> x2, waiting for transfers between devices: none -> 21.3 us  [the longest x1 16.7 us: shards(): amp_parts = [got, lax.ppermute(got, 'batch', swap)]]
    all_gather x1, waiting for transfers between devices: 36.8 us -> 16.4 us  [shards(): inter_all = lax.all_gather(mine, 'grp', axis=0, tiled=False)]
    all_to_all x1 -> x2, blocking collectives: 51 us -> 68.8 us  [the longest x1 40.3 us: shards(): got = lax.all_to_all(sends, 'grp', split_axis=0, concat_axis=0, tiled=True)]
    gather x4 -> x0, local copies, waits for them, and re-layouts: 10.8 us -> none  [the longest x2 7.46 us: shards(): jnp.take_along_axis(inter_blocks, k_source[:, :, None, None, None], axis=1)]
    select_n x5 -> x0, other arithmetic: 8.6 us -> none  [the longest x1 3.45 us: shards(): jnp.take_along_axis(inter_blocks, k_source[:, :, None, None, None], axis=1)]
    pallas_call x0 -> x1, Pallas kernels: none -> 8.27 us  [contract(): pl.pallas_call(functools.partial(contract_kernel, n_k, width), grid_spec=...]
  transfers between devices with their start and end apart: 3 -> 3, of which waited for: 3 -> 3; matrix products, arithmetic and copies ran while one was open for 3% -> 2% of each run, Pallas kernels for 0% -> 0%
where the time goes in v1:
time: 138 us
  blocking collectives  68.8 us (50%)
  waiting for transfers between devices  37.7 us (27%)
  between operations  13.4 us (10%)
  Pallas kernels  8.27 us (6%)
  local copies, waits for them, and re-layouts  5.65 us (4%)
  starting transfers between devices  3.41 us (2%)
    all_to_all x1, blocking collectives, shards(): got = lax.all_to_all(sends, 'grp', split_axis=0, concat_axis=0, tiled=True)  40.3 us
    all_to_all x1, blocking collectives, shards(): lax.all_to_all(partial, 'grp', split_axis=0, concat_axis=0, tiled=True)  28.5 us
    ppermute x1, waiting for transfers between devices, shards(): amp_parts = [got, lax.ppermute(got, 'batch', swap)]  16.7 us
    all_gather x1, waiting for transfers between devices, shards(): inter_all = lax.all_gather(mine, 'grp', axis=0, tiled=False)  16.4 us
    pallas_call x1, Pallas kernels, contract(): pl.pallas_call(functools.partial(contract_kernel, n_k, width), grid_spec=...  8.27 us
    ppermute x1, waiting for transfers between devices, shards(): mine = jnp.concatenate([own, lax.ppermute(away, 'batch', swap)])  4.6 us
  transfers between devices with their start and end apart: 3, of which 3 were waited for; matrix products, arithmetic and copies ran while one was open for 2% of the time, Pallas kernels for 0%

profile of v1, /device:TPU:1, one launch (start us, length us, event | category | flops | bytes accessed | tf_op | source)
XLA Modules:
  0.0 138.1 jit_solution(15461976339059749688)
XLA Ops:
  6.5 0.0 copy-start.2
  6.5 0.0 copy-start.3
  6.5 0.0 copy-start
  6.5 0.0 copy-start.1
  6.5 0.0 all-gather.3.cloned.1.call-start
  6.6 1.2 reshape.10
  7.7 0.8 constant_dynamic-slice_fusion.1
  8.6 2.1 %collective-permute-start.1 = (bf16[3,64,512]{2,1,0:T(8,128)(2,1)S(1)}, bf16[3,64,512]{2,1,0:T(8,128)(2,1)S(1)}, u32[]{:S(2)}, u32[]{:S(2)}) collective-permute-start(bf16[3,64,512]{2,1,0:T(8,128)(2,1)S(1)} %bitcast.38), channel_id=1, source_target_pairs={{0,16},{16,0},{1,17},{17,1},{2,18},{18,2},{3,19},{19,3},{4,20},{20... | collective-permute-start | bytes 589832 | tf_op jit(solution)/shard_map/ppermute | solution.py:86
  10.8 4.6 %collective-permute-done.1 = bf16[3,64,512]{2,1,0:T(8,128)(2,1)S(1)} collective-permute-done((bf16[3,64,512]{2,1,0:T(8,128)(2,1)S(1)}, bf16[3,64,512]{2,1,0:T(8,128)(2,1)S(1)}, u32[]{:S(2)}, u32[]{:S(2)}) %collective-permute-start.1) | collective-permute-done | bytes 196640 | tf_op jit(solution)/shard_map/ppermute | solution.py:86
  15.4 0.8 pad_maximum_fusion
  16.2 0.0 all-gather.3.cloned.1.call-update
  16.2 1.2 copy.18
  17.4 40.3 %all_to_all.10 = bf16[16,1,3,64,128]{4,3,2,1,0:T(8,128)(2,1)S(1)} all-to-all(bf16[16,1,3,64,128]{4,3,2,1,0:T(8,128)(2,1)S(1)} %bitcast.36), channel_id=1, replica_groups=mesh['batch'=2,'grp'=16] {'grp'}, dimensions={0} | all-to-all | bytes 1572864 | tf_op jit(solution)/shard_map/all_to_all | solution.py:98
  57.7 1.2 collective-permute-start
  58.9 0.0 copy-done.2
  58.9 0.1 dynamic_slice.22
  59.0 0.0 copy-done.3
  59.0 0.6 dynamic_slice.21
  59.6 0.0 copy-done
  59.6 0.1 fusion
  59.7 0.0 copy-done.1
  59.7 0.7 concatenate.6.labels_ref
  60.4 16.7 %collective-permute-done = bf16[16,1,3,64,128]{4,3,2,0,1:T(8,128)(2,1)S(1)} collective-permute-done((bf16[16,1,3,64,128]{4,3,2,0,1:T(8,128)(2,1)S(1)}, bf16[16,1,3,64,128]{4,3,2,0,1:T(8,128)(2,1)S(1)}, u32[]{:S(2)}, u32[]{:S(2)}) %collective-permute-start) | collective-permute-done | bytes 786464 | tf_op jit(solution)/shard_map/ppermute | solution.py:100
  77.1 16.4 %all-gather.3.cloned.1.call-done = bf16[96,64,512]{2,1,0:T(8,128)(2,1)} async-done(((bf16[6,64,512]{2,1,0:T(8,128)(2,1)}), bf16[96,64,512]{2,1,0:T(8,128)(2,1)}) %all-gather.3.cloned.1.call-update) | async-done | bytes 6291472 | tf_op jit(solution)/shard_map/all_gather | solution.py:95
  93.5 8.3 %shard_map.64 = bf16[16,4,64,128]{3,2,1,0:T(8,128)(2,1)S(1)} custom-call(s32[19]{0:T(128)S(1)} %concatenate.6.labels_ref, bf16[16,3,64,128]{3,2,1,0:T(8,128)(2,1)S(1)} %bitcast.22, bf16[16,3,64,128]{3,2,1,0:T(8,128)(2,1)S(1)} %bitcast.23, bf16[16,3,64,128]{3,2,1,0:T(8,128)(2,1)S(1)} %bitcast.24, bf16[16,3,64,128]{3,2,1,0:T(8,128)(2,1)S(1)} %bitcast.25, ...), custom_call_target="tpu_custom_call" | custom-call | flops 805306368 | bytes 6291456 | tf_op jit(solution)/shard_map/pallas_call | solution.py:58
  101.8 28.5 %all_to_all.11 = bf16[16,1,4,64,128]{4,3,2,1,0:T(8,128)(2,1)S(1)} all-to-all(bf16[16,1,4,64,128]{4,3,2,1,0:T(8,128)(2,1)S(1)} %bitcast.28), channel_id=1, replica_groups=mesh['batch'=2,'grp'=16] {'grp'}, dimensions={0} | all-to-all | bytes 2097152 | tf_op jit(solution)/shard_map/all_to_all | solution.py:112
  130.3 1.0 copy.22
  (2 shorter events, 0.1 us)
Async XLA Ops:
  6.5 52.4 %copy-start.2 = (s32[8]{0:T(128)S(1)}, s32[8]{0:T(128)}, u32[]{:S(2)}) copy-start(s32[8]{0:T(128)} %param.10) | copy-start | bytes 100
  6.5 52.5 %copy-start.3 = (s32[16]{0:T(128)S(1)}, s32[16]{0:T(128)}, u32[]{:S(2)}) copy-start(s32[16]{0:T(128)} %param.9) | copy-start | bytes 196
  6.5 53.1 %copy-start = (s32[6]{0:T(128)S(1)}, s32[6]{0:T(128)}, u32[]{:S(2)}) copy-start(s32[6]{0:T(128)} %param.8) | copy-start | bytes 76
  6.5 53.2 %copy-start.1 = (s32[8]{0:T(128)S(1)}, s32[8]{0:T(128)}, u32[]{:S(2)}) copy-start(s32[8]{0:T(128)} %param.11) | copy-start | bytes 100
  6.5 87.0 %all-gather.3.cloned.1.call-start = ((), (), s32[]{:S(2)}) async-start(), calls=%async_computation.2 | async-start | bytes 6684672 | tf_op jit(solution)/shard_map/all_gather | solution.py:95
  8.6 6.8 %collective-permute-start.1 = (bf16[3,64,512]{2,1,0:T(8,128)(2,1)S(1)}, bf16[3,64,512]{2,1,0:T(8,128)(2,1)S(1)}, u32[]{:S(2)}, u32[]{:S(2)}) collective-permute-start(bf16[3,64,512]{2,1,0:T(8,128)(2,1)S(1)} %bitcast.38), channel_id=1, source_target_pairs={{0,16},{16,0},{1,17},{17,1},{2,18},{18,2},{3,19},{19,3},{4,20},{20... | collective-permute-start | bytes 589832 | tf_op jit(solution)/shard_map/ppermute | solution.py:86
  57.7 19.4 %collective-permute-start = (bf16[16,1,3,64,128]{4,3,2,0,1:T(8,128)(2,1)S(1)}, bf16[16,1,3,64,128]{4,3,2,0,1:T(8,128)(2,1)S(1)}, u32[]{:S(2)}, u32[]{:S(2)}) collective-permute-start(bf16[16,1,3,64,128]{4,3,2,0,1:T(8,128)(2,1)S(1)} %bitcast.21), channel_id=1, source_target_pairs={{0,16},{16,0},{1,17},{17,1},{2,18},{18,2},{3,19},{19,3},{4,20},{20... | collective-permute-start | bytes 2359304 | tf_op jit(solution)/shard_map/ppermute | solution.py:100
Sparse Core Ops, SparseCore 0:
  16.3 77.1 all-gather.2

commit v2 on v1

--- a/solution.py
+++ b/solution.py
@@ -69,7 +69,7 @@
     )(labels, *amp_ops, *([inter] * n_k))
 
 
-def shards(n_batch, n_grp, amps, cycle_inter, k_irrep, i_irrep, j_irrep, virt_count):
+def shards_any(n_batch, n_grp, amps, cycle_inter, k_irrep, i_irrep, j_irrep, virt_count):
     k_local, i_total, slab, width = amps.shape
     n_irrep = virt_count.shape[0]
     j_total = cycle_inter.shape[2]
@@ -113,6 +113,139 @@
     return result.reshape(i_total, j_count, slab, width)
 
 
+def tile_kernel(n_place, k_half, width, j_count, k_irrep, i_irrep, j_irrep, virt_count, *refs):
+    own_refs, twin_refs = refs[:n_place], refs[n_place:2 * n_place]
+    near_refs = refs[2 * n_place:3 * n_place]
+    far_first, far_rest = refs[3 * n_place:3 * n_place + 2]
+    far_refs = [far_first] + [far_rest.at[at] for at in range(n_place - 1)]
+    out_ref, own, twin, near, far, total, sems = refs[3 * n_place + 2:]
+    n_irrep = total.shape[1]
+    me_b, me_g = lax.axis_index("batch"), lax.axis_index("grp")
+    core, first_c = me_g % 2, me_g // 2
+    i_labels = [i_irrep[2 * (me_g % (2 * n_place)) + i] for i in range(2)]
+    k_labels = [k_irrep[(me_b ^ half) * k_half + k] for half in range(2) for k in range(k_half)]
+    copies = []
+    for at in range(n_place):
+        here = []
+        for which, (src, dst) in enumerate(((own_refs, own), (twin_refs, twin), (near_refs, near), (far_refs, far))):
+            here.append(pltpu.make_async_copy(src[at], dst.at[at], sems.at[which, at]))
+        copies.append(here)
+    for here in copies:
+        for copy in here:
+            copy.start()
+    total[...] = jnp.zeros_like(total)
+    row = lax.broadcasted_iota(jnp.int32, (width, width), 0)
+    col = lax.broadcasted_iota(jnp.int32, (width, width), 1)
+    slot = (row + core * (width // 2)) & (width - 1)
+    for at in range(n_place):
+        for copy in copies[at]:
+            copy.wait()
+        c = first_c ^ at
+        live = slot < virt_count[c]
+        for half, side in enumerate((near, far)):
+            for k in range(k_half):
+                amps = []
+                for i in range(2):
+                    amp = side[at, :, k, i].reshape(width, width)
+                    amps.append(jnp.where(live, amp, jnp.zeros((), amp.dtype)))
+                inter = jnp.concatenate([own[at, half * k_half + k], twin[at, half * k_half + k]], axis=0)
+                term = lax.dot_general(
+                    jnp.concatenate(amps, axis=1), inter,
+                    (((0,), (0,)), ((), ())), preferred_element_type=jnp.float32,
+                )
+                for i in range(2):
+                    p = c ^ k_labels[half * k_half + k] ^ i_labels[i]
+                    total[i, p] += term[i * width:(i + 1) * width]
+
+    @pl.loop(0, n_irrep)
+    def _(p):
+        a_live = row < virt_count[p]
+        for i in range(2):
+            for j in range(j_count):
+                b = p ^ i_labels[i] ^ j_irrep[me_b * j_count + j]
+                live = a_live & (col < virt_count[b])
+                block = jnp.where(live, total[i, p, :, j * width:(j + 1) * width], 0.0).astype(out_ref.dtype)
+                for side in range(2):
+                    out_ref[2 * p + side, i, j] = block[side * width // 2:(side + 1) * width // 2]
+
+
+def shards_tiled(amps, cycle_inter, k_irrep, i_irrep, j_irrep, virt_count):
+    k_half, i_total, slab, width = amps.shape
+    n_irrep = virt_count.shape[0]
+    j_count = cycle_inter.shape[2] // 2
+    n_place = n_irrep // 2
+    n_grp = 4 * n_place
+    me_b = lax.axis_index("batch")
+    me_g = lax.axis_index("grp")
+    core, place = me_g % 2, (me_g // 2) % n_place
+    swap = [(0, 1), (1, 0)]
+
+    def flip(x, bits):
+        return lax.ppermute(x, "grp", [(d, d ^ bits) for d in range(n_grp)])
+
+    def hold(*xs):
+        return lax.optimization_barrier(xs)
+
+    def over(x):
+        return lax.ppermute(x, "batch", swap)
+
+    low, high = cycle_inter[:, :, :j_count], cycle_inter[:, :, j_count:]
+    mine = jnp.where(me_b == 0, low, high).reshape(k_half, slab, j_count * width)
+    away = jnp.where(me_b == 0, high, low).reshape(k_half, slab, j_count * width)
+    parts = amps.reshape(k_half, n_place, 2, 2, slab, width)
+    keep = lax.dynamic_index_in_dim(parts, core, 2, keepdims=False)
+    take = flip(lax.dynamic_index_in_dim(parts, 1 - core, 2, keepdims=False), 1)
+    i_parts = jnp.stack([keep, take])
+
+    def i_part(at):
+        return lax.dynamic_index_in_dim(i_parts, at, 2, keepdims=False)
+
+    i_parts, away, mine = hold(i_parts, away, mine)
+    other = over(away)
+    near0, near1, near2, near3 = i_part(place), *(flip(i_part(place ^ m), 2 * m) for m in range(1, n_place))
+    far0 = over(near0)
+    own0 = jnp.concatenate([mine, other])
+    own1, own2, twin0 = flip(own0, 2), flip(own0, 4), flip(own0, 1)
+    far123 = over(jnp.stack([near1, near2, near3]))
+    own1, own2, twin0, far0 = hold(own1, own2, twin0, far0)
+    own3 = flip(own1[:k_half], 4), flip(own2[k_half:], 2)
+    twin1, twin2 = flip(own1, 1), flip(own2, 1)
+    far123, twin1, twin2, *own3 = hold(far123, twin1, twin2, *own3)
+    own3 = jnp.concatenate(own3)
+    near, far = [near0, near1, near2, near3], [far0, far123]
+    own, twin = [own0, own1, own2, own3], [twin0, twin1, twin2, flip(own3, 1)]
+
+    any_spec = pl.BlockSpec(memory_space=pl.ANY)
+    flops = 2 * 2 * k_half * 2 * n_place * width ** 3 * j_count
+    tile = pl.pallas_call(
+        functools.partial(tile_kernel, n_place, k_half, width, j_count),
+        in_specs=[pl.BlockSpec(memory_space=pltpu.SMEM)] * 4 + [any_spec] * (3 * n_place + 2),
+        out_specs=pl.BlockSpec(memory_space=pltpu.VMEM),
+        out_shape=jax.ShapeDtypeStruct((n_grp, 2, j_count, slab, width), jnp.bfloat16),
+        scratch_shapes=[
+            pltpu.VMEM((n_place, 2 * k_half, slab, j_count * width), jnp.bfloat16),
+            pltpu.VMEM((n_place, 2 * k_half, slab, j_count * width), jnp.bfloat16),
+            pltpu.VMEM((n_place, 2, k_half, 2, slab, width), jnp.bfloat16),
+            pltpu.VMEM((n_place, 2, k_half, 2, slab, width), jnp.bfloat16),
+            pltpu.VMEM((2, n_irrep, width, j_count * width), jnp.float32),
+            pltpu.SemaphoreType.DMA((4, n_place)),
+        ],
+        compiler_params=pltpu.CompilerParams(vmem_limit_bytes=24 * 2 ** 20),
+        cost_estimate=pl.CostEstimate(flops=flops, bytes_accessed=8 * 2 ** 20, transcendentals=0),
+    )(k_irrep, i_irrep, j_irrep, virt_count, *own, *twin, *near, *far)
+    result = lax.all_to_all(tile, "grp", split_axis=0, concat_axis=0, tiled=True)
+    result = result.reshape(2, i_total, j_count, slab, width).astype(jnp.float32)
+    return (result[0] + result[1]).astype(jnp.bfloat16)
+
+
+def shards(n_batch, n_grp, amps, cycle_inter, k_irrep, i_irrep, j_irrep, virt_count):
+    operands = (amps, cycle_inter, k_irrep, i_irrep, j_irrep, virt_count)
+    n_irrep = virt_count.shape[0]
+    if n_batch == 2 and n_grp == 2 * n_irrep and n_irrep == 8 and amps.shape[1] == n_grp:
+        return shards_tiled(*operands)
+    return shards_any(n_batch, n_grp, *operands)
+
+
 def solution(mesh):
     return jax.shard_map(
         functools.partial(shards, mesh.shape["batch"], mesh.shape["grp"]),

time: 138 us -> 101 us (0.73)
  waiting for transfers between devices: 37.7 us -> 17.8 us
  blocking collectives: 68.8 us -> 52.7 us
  starting transfers between devices: 3.41 us -> 18.4 us
  between operations: 13.4 us -> 0.2 us
  local copies, waits for them, and re-layouts: 5.65 us -> 1.62 us
  other arithmetic: 0.78 us -> 2.3 us
    all_gather x1 -> x0, waiting for transfers between devices: 16.4 us -> none  [shards(): inter_all = lax.all_gather(mine, 'grp', axis=0, tiled=False)]
    all_to_all x2 -> x1, blocking collectives: 68.8 us -> 52.7 us  [shards_tiled(): lax.all_to_all(tile, 'grp', split_axis=0, concat_axis=0, tiled=True)]
    ppermute x2 -> x15, starting transfers between devices: 3.37 us -> 18.4 us  [the longest x12 14.5 us: flip(): return lax.ppermute(x, 'grp', [(d, d ^ bits) for d in range(n_grp)])]
    ppermute x2 -> x15, waiting for transfers between devices: 21.3 us -> 17.8 us  [the longest x12 12.5 us: flip(): return lax.ppermute(x, 'grp', [(d, d ^ bits) for d in range(n_grp)])]
    unnamed x12, local copies, waits for them, and re-layouts: 2.23 us -> 0.06 us
    convert_element_type x0 -> x2, other arithmetic: none -> 1.92 us  [the longest x1 1.45 us: shards_tiled(): return (result[0] + result[1]).astype(jnp.bfloat16)]
  transfers between devices with their start and end apart: 3 -> 15, of which waited for: 3 -> 8; matrix products, arithmetic and copies ran while one was open for 2% -> 1% of each run, Pallas kernels for 0% -> 0%
where the time goes in v2:
time: 101 us
  blocking collectives  52.7 us (52%)
  starting transfers between devices  18.4 us (18%)
  waiting for transfers between devices  17.8 us (18%)
  Pallas kernels  7.48 us (7%)
  other arithmetic  2.3 us (2%)
  local copies, waits for them, and re-layouts  1.62 us (2%)
    all_to_all x1, blocking collectives, shards_tiled(): lax.all_to_all(tile, 'grp', split_axis=0, concat_axis=0, tiled=True)  52.7 us
    ppermute x12, starting transfers between devices, flip(): return lax.ppermute(x, 'grp', [(d, d ^ bits) for d in range(n_grp)])  14.5 us
    ppermute x12, waiting for transfers between devices, flip(): return lax.ppermute(x, 'grp', [(d, d ^ bits) for d in range(n_grp)])  12.5 us
    pallas_call x1, Pallas kernels, shards_tiled(): pl.pallas_call(functools.partial(tile_kernel, n_place, k_half, width, j_c...  7.48 us
    ppermute x3, waiting for transfers between devices, over(): return lax.ppermute(x, 'batch', swap)  5.34 us
    ppermute x3, starting transfers between devices, over(): return lax.ppermute(x, 'batch', swap)  3.97 us
  transfers between devices with their start and end apart: 15, of which 8 were waited for; matrix products, arithmetic and copies ran while one was open for 1% of the time, Pallas kernels for 0%

profile of v2, /device:TPU:1, one launch (start us, length us, event | category | flops | bytes accessed | tf_op | source)
XLA Modules:
  0.0 100.6 jit_solution(1825983809783912743)
XLA Ops:
  0.0 1.2 %constant_dynamic-slice_fusion.1 = (bf16[3,4,1,2,64,128]{5,4,3,2,1,0:T(8,128)(2,1)S(1)}, bf16[3,4,1,2,64,128]{5,4,3,2,1,0:T(8,128)(2,1)S(1)}) fusion(bf16[3,4,2,2,64,128]{5,4,3,2,1,0:T(8,128)(2,1)} %bitcast.24, s32[]{:T(128)S(6)} %select_n.48, s32[]{:T(128)S(6)} %select_n.49), kind=kLoop, calls=%fused_computation.17 | loop fusion | bytes 1572872 | tf_op jit(solution)/shard_map/jit(dynamic_index_in_dim)/dynamic_slice | solution.py:196
  1.3 0.1 collective-permute-start
  1.4 0.2 broadcast_select_fusion
  1.7 0.1 reshape.21
  1.7 0.1 reshape.20
  1.9 1.2 %collective-permute-done = bf16[3,4,2,64,128]{4,3,2,0,1:T(8,128)(2,1)S(1)} collective-permute-done((bf16[3,4,2,64,128]{4,3,2,0,1:T(8,128)(2,1)S(1)}, bf16[3,4,2,64,128]{4,3,2,0,1:T(8,128)(2,1)S(1)}, u32[]{:S(2)}, u32[]{:S(2)}) %collective-permute-start) | collective-permute-done | bytes 393248 | tf_op jit(solution)/shard_map/ppermute | solution.py:184
  3.1 0.1 pad_maximum_fusion
  3.1 2.4 %collective-permute-start.1 = (bf16[3,64,512]{2,1,0:T(8,128)(2,1)S(1)}, bf16[3,64,512]{2,1,0:T(8,128)(2,1)S(1)}, u32[]{:S(2)}, u32[]{:S(2)}) collective-permute-start(bf16[3,64,512]{2,1,0:T(8,128)(2,1)S(1)} %reshape.20), channel_id=1, source_target_pairs={{0,16},{16,0},{1,17},{17,1},{2,18},{18,2},{3,19},{19,3},{4,20},{20... | collective-permute-start | bytes 589832 | tf_op jit(solution)/shard_map/ppermute | solution.py:190
  5.7 1.3 %collective-permute-start.6 = (bf16[2,3,2,64,128]{4,3,2,1,0:T(8,128)(2,1)S(1)}, bf16[2,3,2,64,128]{4,3,2,1,0:T(8,128)(2,1)S(1)}, u32[]{:S(2)}, u32[]{:S(2)}) collective-permute-start(bf16[2,3,2,64,128]{4,3,2,1,0:T(8,128)(2,1)S(1)} %get-tuple-element.29), channel_id=1, source_target_pairs={{0,2},{1,3},{2,0},{3,1},{4,6},{5,7},{6,4},{7,5},{8,10},{9,11},{10,... | collective-permute-start | bytes 589832 | tf_op jit(solution)/shard_map/ppermute | solution.py:184
  7.0 1.3 %collective-permute-start.8 = (bf16[2,3,2,64,128]{4,3,2,1,0:T(8,128)(2,1)S(1)}, bf16[2,3,2,64,128]{4,3,2,1,0:T(8,128)(2,1)S(1)}, u32[]{:S(2)}, u32[]{:S(2)}) collective-permute-start(bf16[2,3,2,64,128]{4,3,2,1,0:T(8,128)(2,1)S(1)} %get-tuple-element.30), channel_id=1, source_target_pairs={{0,6},{1,7},{2,4},{3,5},{4,2},{5,3},{6,0},{7,1},{8,14},{9,15},{10,... | collective-permute-start | bytes 589832 | tf_op jit(solution)/shard_map/ppermute | solution.py:184
  8.2 0.2 collective-permute-start.7
  8.4 2.1 %collective-permute-done.1 = bf16[3,64,512]{2,1,0:T(8,128)(2,1)S(1)} collective-permute-done((bf16[3,64,512]{2,1,0:T(8,128)(2,1)S(1)}, bf16[3,64,512]{2,1,0:T(8,128)(2,1)S(1)}, u32[]{:S(2)}, u32[]{:S(2)}) %collective-permute-start.1) | collective-permute-done | bytes 196640 | tf_op jit(solution)/shard_map/ppermute | solution.py:190
  10.6 0.9 collective-permute-start.4
  11.5 1.5 %collective-permute-start.3 = (bf16[6,64,512]{2,1,0:T(8,128)(2,1)S(1)}, bf16[6,64,512]{2,1,0:T(8,128)(2,1)S(1)}, u32[]{:S(2)}, u32[]{:S(2)}) collective-permute-start(bf16[6,64,512]{2,1,0:T(8,128)(2,1)S(1)} %constant_dynamic-update-slice_fusion.refs_0_), channel_id=1, source_target_pairs={{0,4},{1,5},{2,6},{3,7},{4,0},{5,1},{6,2},{7,3},{8,12},{9,13},{10,... | collective-permute-start | bytes 1179656 | tf_op jit(solution)/shard_map/ppermute | solution.py:184
  13.0 2.2 %collective-permute-done.6.refs_9_ = bf16[2,3,2,64,128]{4,3,2,1,0:T(8,128)(2,1)S(1)} collective-permute-done((bf16[2,3,2,64,128]{4,3,2,1,0:T(8,128)(2,1)S(1)}, bf16[2,3,2,64,128]{4,3,2,1,0:T(8,128)(2,1)S(1)}, u32[]{:S(2)}, u32[]{:S(2)}) %collective-permute-start.6) | collective-permute-done | bytes 196640 | tf_op jit(solution)/shard_map/ppermute | solution.py:184
  15.3 1.7 %collective-permute-start.2 = (bf16[6,64,512]{2,1,0:T(8,128)(2,1)S(1)}, bf16[6,64,512]{2,1,0:T(8,128)(2,1)S(1)}, u32[]{:S(2)}, u32[]{:S(2)}) collective-permute-start(bf16[6,64,512]{2,1,0:T(8,128)(2,1)S(1)} %constant_dynamic-update-slice_fusion.refs_0_), channel_id=1, source_target_pairs={{0,2},{1,3},{2,0},{3,1},{4,6},{5,7},{6,4},{7,5},{8,10},{9,11},{10,... | collective-permute-start | bytes 1179656 | tf_op jit(solution)/shard_map/ppermute | solution.py:184
  17.0 0.2 collective-permute-start.5
  17.2 0.1 pad_maximum_fusion.1
  17.3 1.3 %collective-permute-start.9 = (bf16[3,2,3,2,64,128]{5,4,3,2,1,0:T(8,128)(2,1)S(1)}, bf16[3,2,3,2,64,128]{5,4,3,2,1,0:T(8,128)(2,1)S(1)}, u32[]{:S(2)}, u32[]{:S(2)}) collective-permute-start(bf16[3,2,3,2,64,128]{5,4,3,2,1,0:T(8,128)(2,1)S(1)} %pad_maximum_fusion.1), channel_id=1, source_target_pairs={{0,16},{16,0},{1,17},{17,1},{2,18},{18,2},{3,19},{19,3},{4,20},{20... | collective-permute-start | bytes 1769480 | tf_op jit(solution)/shard_map/ppermute | solution.py:190
  18.6 3.2 %collective-permute-done.5.refs_12_ = bf16[2,3,2,64,128]{4,3,2,1,0:T(8,128)(2,1)S(1)} collective-permute-done((bf16[2,3,2,64,128]{4,3,2,1,0:T(8,128)(2,1)S(1)}, bf16[2,3,2,64,128]{4,3,2,1,0:T(8,128)(2,1)S(1)}, u32[]{:S(2)}, u32[]{:S(2)}) %collective-permute-start.5) | collective-permute-done | bytes 196640 | tf_op jit(solution)/shard_map/ppermute | solution.py:190
  21.8 3.3 %collective-permute-done.3.refs_2_ = bf16[6,64,512]{2,1,0:T(8,128)(2,1)S(1)} collective-permute-done((bf16[6,64,512]{2,1,0:T(8,128)(2,1)S(1)}, bf16[6,64,512]{2,1,0:T(8,128)(2,1)S(1)}, u32[]{:S(2)}, u32[]{:S(2)}) %collective-permute-start.3) | collective-permute-done | bytes 393248 | tf_op jit(solution)/shard_map/ppermute | solution.py:184
  25.1 1.9 %collective-permute-start.10 = (bf16[6,64,512]{2,1,0:T(8,128)(2,1)S(1)}, bf16[6,64,512]{2,1,0:T(8,128)(2,1)S(1)}, u32[]{:S(2)}, u32[]{:S(2)}) collective-permute-start(bf16[6,64,512]{2,1,0:T(8,128)(2,1)S(1)} %collective-permute-done.2.refs_1_), channel_id=1, source_target_pairs={{0,1},{1,0},{2,3},{3,2},{4,5},{5,4},{6,7},{7,6},{8,9},{9,8},{10,11... | collective-permute-start | bytes 1179656 | tf_op jit(solution)/shard_map/ppermute | solution.py:184
  27.1 1.5 %collective-permute-start.13 = (bf16[3,64,512]{2,1,0:T(8,128)(2,1)S(1)}, bf16[3,64,512]{2,1,0:T(8,128)(2,1)S(1)}, u32[]{:S(2)}, u32[]{:S(2)}) collective-permute-start(bf16[3,64,512]{2,1,0:T(8,128)(2,1)S(1)} %slice.23), channel_id=1, source_target_pairs={{0,2},{1,3},{2,0},{3,1},{4,6},{5,7},{6,4},{7,5},{8,10},{9,11},{10,... | collective-permute-start | bytes 589832 | tf_op jit(solution)/shard_map/ppermute | solution.py:184
  28.6 1.3 %collective-permute-start.12 = (bf16[3,64,512]{2,1,0:T(8,128)(2,1)S(1)}, bf16[3,64,512]{2,1,0:T(8,128)(2,1)S(1)}, u32[]{:S(2)}, u32[]{:S(2)}) collective-permute-start(bf16[3,64,512]{2,1,0:T(8,128)(2,1)S(1)} %slice.22), channel_id=1, source_target_pairs={{0,4},{1,5},{2,6},{3,7},{4,0},{5,1},{6,2},{7,3},{8,12},{9,13},{10,... | collective-permute-start | bytes 589832 | tf_op jit(solution)/shard_map/ppermute | solution.py:184
  29.9 3.2 %collective-permute-done.13 = bf16[3,64,512]{2,1,0:T(8,128)(2,1)S(1)} collective-permute-done((bf16[3,64,512]{2,1,0:T(8,128)(2,1)S(1)}, bf16[3,64,512]{2,1,0:T(8,128)(2,1)S(1)}, u32[]{:S(2)}, u32[]{:S(2)}) %collective-permute-start.13) | collective-permute-done | bytes 196640 | tf_op jit(solution)/shard_map/ppermute | solution.py:184
  33.1 1.1 %collective-permute-done.12 = bf16[3,64,512]{2,1,0:T(8,128)(2,1)S(1)} collective-permute-done((bf16[3,64,512]{2,1,0:T(8,128)(2,1)S(1)}, bf16[3,64,512]{2,1,0:T(8,128)(2,1)S(1)}, u32[]{:S(2)}, u32[]{:S(2)}) %collective-permute-start.12) | collective-permute-done | bytes 196640 | tf_op jit(solution)/shard_map/ppermute | solution.py:184
  34.3 2.7 %collective-permute-start.14 = (bf16[6,64,512]{2,1,0:T(8,128)(2,1)S(1)}, bf16[6,64,512]{2,1,0:T(8,128)(2,1)S(1)}, u32[]{:S(2)}, u32[]{:S(2)}) collective-permute-start(bf16[6,64,512]{2,1,0:T(8,128)(2,1)S(1)} %constant_dynamic-update-slice_fusion.2.refs_3_), channel_id=1, source_target_pairs={{0,1},{1,0},{2,3},{3,2},{4,5},{5,4},{6,7},{7,6},{8,9},{9,8},{10,11... | collective-permute-start | bytes 1179656 | tf_op jit(solution)/shard_map/ppermute | solution.py:184
  37.1 1.3 %collective-permute-done.14.refs_7_ = bf16[6,64,512]{2,1,0:T(8,128)(2,1)S(1)} collective-permute-done((bf16[6,64,512]{2,1,0:T(8,128)(2,1)S(1)}, bf16[6,64,512]{2,1,0:T(8,128)(2,1)S(1)}, u32[]{:S(2)}, u32[]{:S(2)}) %collective-permute-start.14) | collective-permute-done | bytes 393248 | tf_op jit(solution)/shard_map/ppermute | solution.py:184
  38.4 7.5 %shard_map.64 = bf16[16,2,4,64,128]{4,3,2,1,0:T(8,128)(2,1)S(1)} custom-call(s32[6]{0:T(128)S(1)} %copy-done, s32[16]{0:T(128)S(1)} %copy-done.1, s32[8]{0:T(128)S(1)} %copy-done.2, s32[8]{0:T(128)S(1)} %copy-done.3, bf16[6,64,512]{2,1,0:T(8,128)(2,1)S(1)} %constant_dynamic-update-slice_fusion.refs_0_, ...), custom_call_target="tpu_custom_call" | custom-call | flops 805306368 | bytes 8388608 | tf_op jit(solution)/shard_map/pallas_call | solution.py:220
  45.9 52.7 %all_to_all.5 = bf16[16,2,4,64,128]{4,3,2,1,0:T(8,128)(2,1)S(1)} all-to-all(bf16[16,2,4,64,128]{4,3,2,1,0:T(8,128)(2,1)S(1)} %shard_map.64), channel_id=1, replica_groups=mesh['batch'=2,'grp'=16] {'grp'}, dimensions={0} | all-to-all | bytes 4194304 | tf_op jit(solution)/shard_map/all_to_all | solution.py:236
  98.6 0.5 convert_element_type.11
  99.1 1.4 %fusion = bf16[8,2,4,64,128]{4,3,2,1,0:T(8,128)(2,1)} fusion(f32[16,2,4,64,128]{4,3,2,1,0:T(8,128)S(1)} %convert_element_type.11), kind=kLoop, calls=%fused_computation.1 | loop fusion | flops 1048576 | bytes 5242880 | tf_op jit(solution)/shard_map/convert_element_type | solution.py:238
  (27 shorter events, 0.2 us)
Async XLA Ops:
  0.0 1.4 %copy-start.4 = (bf16[3,64,8,128]{3,2,1,0:T(8,128)(2,1)S(1)}, bf16[3,64,8,128]{3,2,1,0:T(8,128)(2,1)}, u32[]{:S(2)}) copy-start(bf16[3,64,8,128]{3,2,1,0:T(8,128)(2,1)} %param.7) | copy-start | bytes 1179652
  1.3 1.8 %collective-permute-start = (bf16[3,4,2,64,128]{4,3,2,0,1:T(8,128)(2,1)S(1)}, bf16[3,4,2,64,128]{4,3,2,0,1:T(8,128)(2,1)S(1)}, u32[]{:S(2)}, u32[]{:S(2)}) collective-permute-start(bf16[3,4,2,64,128]{4,3,2,0,1:T(8,128)(2,1)S(1)} %bitcast.25), channel_id=1, source_target_pairs={{0,1},{1,0},{2,3},{3,2},{4,5},{5,4},{6,7},{7,6},{8,9},{9,8},{10,11... | collective-permute-start | bytes 1179656 | tf_op jit(solution)/shard_map/ppermute | solution.py:184
  3.1 7.4 %collective-permute-start.1 = (bf16[3,64,512]{2,1,0:T(8,128)(2,1)S(1)}, bf16[3,64,512]{2,1,0:T(8,128)(2,1)S(1)}, u32[]{:S(2)}, u32[]{:S(2)}) collective-permute-start(bf16[3,64,512]{2,1,0:T(8,128)(2,1)S(1)} %reshape.20), channel_id=1, source_target_pairs={{0,16},{16,0},{1,17},{17,1},{2,18},{18,2},{3,19},{19,3},{4,20},{20... | collective-permute-start | bytes 589832 | tf_op jit(solution)/shard_map/ppermute | solution.py:190
  5.6 32.8 %copy-start = (s32[6]{0:T(128)S(1)}, s32[6]{0:T(128)}, u32[]{:S(2)}) copy-start(s32[6]{0:T(128)} %k_irrep.1) | copy-start | bytes 76
  5.7 32.7 %copy-start.1 = (s32[16]{0:T(128)S(1)}, s32[16]{0:T(128)}, u32[]{:S(2)}) copy-start(s32[16]{0:T(128)} %i_irrep.1) | copy-start | bytes 196
  5.7 32.7 %copy-start.2 = (s32[8]{0:T(128)S(1)}, s32[8]{0:T(128)}, u32[]{:S(2)}) copy-start(s32[8]{0:T(128)} %j_irrep.1) | copy-start | bytes 100
  5.7 32.7 %copy-start.3 = (s32[8]{0:T(128)S(1)}, s32[8]{0:T(128)}, u32[]{:S(2)}) copy-start(s32[8]{0:T(128)} %virt_count.1) | copy-start | bytes 100
  5.7 9.6 %collective-permute-start.6 = (bf16[2,3,2,64,128]{4,3,2,1,0:T(8,128)(2,1)S(1)}, bf16[2,3,2,64,128]{4,3,2,1,0:T(8,128)(2,1)S(1)}, u32[]{:S(2)}, u32[]{:S(2)}) collective-permute-start(bf16[2,3,2,64,128]{4,3,2,1,0:T(8,128)(2,1)S(1)} %get-tuple-element.29), channel_id=1, source_target_pairs={{0,2},{1,3},{2,0},{3,1},{4,6},{5,7},{6,4},{7,5},{8,10},{9,11},{10,... | collective-permute-start | bytes 589832 | tf_op jit(solution)/shard_map/ppermute | solution.py:184
  7.0 10.0 %collective-permute-start.8 = (bf16[2,3,2,64,128]{4,3,2,1,0:T(8,128)(2,1)S(1)}, bf16[2,3,2,64,128]{4,3,2,1,0:T(8,128)(2,1)S(1)}, u32[]{:S(2)}, u32[]{:S(2)}) collective-permute-start(bf16[2,3,2,64,128]{4,3,2,1,0:T(8,128)(2,1)S(1)} %get-tuple-element.30), channel_id=1, source_target_pairs={{0,6},{1,7},{2,4},{3,5},{4,2},{5,3},{6,0},{7,1},{8,14},{9,15},{10,... | collective-permute-start | bytes 589832 | tf_op jit(solution)/shard_map/ppermute | solution.py:184
  8.2 9.0 %collective-permute-start.7 = (bf16[2,3,2,64,128]{4,3,2,1,0:T(8,128)(2,1)S(1)}, bf16[2,3,2,64,128]{4,3,2,1,0:T(8,128)(2,1)S(1)}, u32[]{:S(2)}, u32[]{:S(2)}) collective-permute-start(bf16[2,3,2,64,128]{4,3,2,1,0:T(8,128)(2,1)S(1)} %get-tuple-element.31), channel_id=1, source_target_pairs={{0,4},{1,5},{2,6},{3,7},{4,0},{5,1},{6,2},{7,3},{8,12},{9,13},{10,... | collective-permute-start | bytes 589832 | tf_op jit(solution)/shard_map/ppermute | solution.py:184
  10.6 11.2 %collective-permute-start.4 = (bf16[6,64,512]{2,1,0:T(8,128)(2,1)S(1)}, bf16[6,64,512]{2,1,0:T(8,128)(2,1)S(1)}, u32[]{:S(2)}, u32[]{:S(2)}) collective-permute-start(bf16[6,64,512]{2,1,0:T(8,128)(2,1)S(1)} %constant_dynamic-update-slice_fusion.refs_0_), channel_id=1, source_target_pairs={{0,1},{1,0},{2,3},{3,2},{4,5},{5,4},{6,7},{7,6},{8,9},{9,8},{10,11... | collective-permute-start | bytes 1179656 | tf_op jit(solution)/shard_map/ppermute | solution.py:184
  11.5 13.6 %collective-permute-start.3 = (bf16[6,64,512]{2,1,0:T(8,128)(2,1)S(1)}, bf16[6,64,512]{2,1,0:T(8,128)(2,1)S(1)}, u32[]{:S(2)}, u32[]{:S(2)}) collective-permute-start(bf16[6,64,512]{2,1,0:T(8,128)(2,1)S(1)} %constant_dynamic-update-slice_fusion.refs_0_), channel_id=1, source_target_pairs={{0,4},{1,5},{2,6},{3,7},{4,0},{5,1},{6,2},{7,3},{8,12},{9,13},{10,... | collective-permute-start | bytes 1179656 | tf_op jit(solution)/shard_map/ppermute | solution.py:184
  15.3 9.9 %collective-permute-start.2 = (bf16[6,64,512]{2,1,0:T(8,128)(2,1)S(1)}, bf16[6,64,512]{2,1,0:T(8,128)(2,1)S(1)}, u32[]{:S(2)}, u32[]{:S(2)}) collective-permute-start(bf16[6,64,512]{2,1,0:T(8,128)(2,1)S(1)} %constant_dynamic-update-slice_fusion.refs_0_), channel_id=1, source_target_pairs={{0,2},{1,3},{2,0},{3,1},{4,6},{5,7},{6,4},{7,5},{8,10},{9,11},{10,... | collective-permute-start | bytes 1179656 | tf_op jit(solution)/shard_map/ppermute | solution.py:184
  17.0 4.8 %collective-permute-start.5 = (bf16[2,3,2,64,128]{4,3,2,1,0:T(8,128)(2,1)S(1)}, bf16[2,3,2,64,128]{4,3,2,1,0:T(8,128)(2,1)S(1)}, u32[]{:S(2)}, u32[]{:S(2)}) collective-permute-start(bf16[2,3,2,64,128]{4,3,2,1,0:T(8,128)(2,1)S(1)} %get-tuple-element.32.refs_8_), channel_id=1, source_target_pairs={{0,16},{16,0},{1,17},{17,1},{2,18},{18,2},{3,19},{19,3},{4,20},{20... | collective-permute-start | bytes 589832 | tf_op jit(solution)/shard_map/ppermute | solution.py:190
  17.3 17.0 %collective-permute-start.9 = (bf16[3,2,3,2,64,128]{5,4,3,2,1,0:T(8,128)(2,1)S(1)}, bf16[3,2,3,2,64,128]{5,4,3,2,1,0:T(8,128)(2,1)S(1)}, u32[]{:S(2)}, u32[]{:S(2)}) collective-permute-start(bf16[3,2,3,2,64,128]{5,4,3,2,1,0:T(8,128)(2,1)S(1)} %pad_maximum_fusion.1), channel_id=1, source_target_pairs={{0,16},{16,0},{1,17},{17,1},{2,18},{18,2},{3,19},{19,3},{4,20},{20... | collective-permute-start | bytes 1769480 | tf_op jit(solution)/shard_map/ppermute | solution.py:190
  25.1 9.1 %collective-permute-start.10 = (bf16[6,64,512]{2,1,0:T(8,128)(2,1)S(1)}, bf16[6,64,512]{2,1,0:T(8,128)(2,1)S(1)}, u32[]{:S(2)}, u32[]{:S(2)}) collective-permute-start(bf16[6,64,512]{2,1,0:T(8,128)(2,1)S(1)} %collective-permute-done.2.refs_1_), channel_id=1, source_target_pairs={{0,1},{1,0},{2,3},{3,2},{4,5},{5,4},{6,7},{7,6},{8,9},{9,8},{10,11... | collective-permute-start | bytes 1179656 | tf_op jit(solution)/shard_map/ppermute | solution.py:184
  27.0 7.2 %collective-permute-start.11 = (bf16[6,64,512]{2,1,0:T(8,128)(2,1)S(1)}, bf16[6,64,512]{2,1,0:T(8,128)(2,1)S(1)}, u32[]{:S(2)}, u32[]{:S(2)}) collective-permute-start(bf16[6,64,512]{2,1,0:T(8,128)(2,1)S(1)} %collective-permute-done.3.refs_2_), channel_id=1, source_target_pairs={{0,1},{1,0},{2,3},{3,2},{4,5},{5,4},{6,7},{7,6},{8,9},{9,8},{10,11... | collective-permute-start | bytes 1179656 | tf_op jit(solution)/shard_map/ppermute | solution.py:184
  27.1 6.0 %collective-permute-start.13 = (bf16[3,64,512]{2,1,0:T(8,128)(2,1)S(1)}, bf16[3,64,512]{2,1,0:T(8,128)(2,1)S(1)}, u32[]{:S(2)}, u32[]{:S(2)}) collective-permute-start(bf16[3,64,512]{2,1,0:T(8,128)(2,1)S(1)} %slice.23), channel_id=1, source_target_pairs={{0,2},{1,3},{2,0},{3,1},{4,6},{5,7},{6,4},{7,5},{8,10},{9,11},{10,... | collective-permute-start | bytes 589832 | tf_op jit(solution)/shard_map/ppermute | solution.py:184
  28.6 5.6 %collective-permute-start.12 = (bf16[3,64,512]{2,1,0:T(8,128)(2,1)S(1)}, bf16[3,64,512]{2,1,0:T(8,128)(2,1)S(1)}, u32[]{:S(2)}, u32[]{:S(2)}) collective-permute-start(bf16[3,64,512]{2,1,0:T(8,128)(2,1)S(1)} %slice.22), channel_id=1, source_target_pairs={{0,4},{1,5},{2,6},{3,7},{4,0},{5,1},{6,2},{7,3},{8,12},{9,13},{10,... | collective-permute-start | bytes 589832 | tf_op jit(solution)/shard_map/ppermute | solution.py:184
  34.3 4.1 %collective-permute-start.14 = (bf16[6,64,512]{2,1,0:T(8,128)(2,1)S(1)}, bf16[6,64,512]{2,1,0:T(8,128)(2,1)S(1)}, u32[]{:S(2)}, u32[]{:S(2)}) collective-permute-start(bf16[6,64,512]{2,1,0:T(8,128)(2,1)S(1)} %constant_dynamic-update-slice_fusion.2.refs_3_), channel_id=1, source_target_pairs={{0,1},{1,0},{2,3},{3,2},{4,5},{5,4},{6,7},{7,6},{8,9},{9,8},{10,11... | collective-permute-start | bytes 1179656 | tf_op jit(solution)/shard_map/ppermute | solution.py:184

commit v3 on v2

--- a/solution.py
+++ b/solution.py
@@ -114,41 +114,28 @@
 
 
 def tile_kernel(n_place, k_half, width, j_count, k_irrep, i_irrep, j_irrep, virt_count, *refs):
-    own_refs, twin_refs = refs[:n_place], refs[n_place:2 * n_place]
-    near_refs = refs[2 * n_place:3 * n_place]
-    far_first, far_rest = refs[3 * n_place:3 * n_place + 2]
-    far_refs = [far_first] + [far_rest.at[at] for at in range(n_place - 1)]
-    out_ref, own, twin, near, far, total, sems = refs[3 * n_place + 2:]
+    own, twin, near = refs[:n_place], refs[n_place:2 * n_place], refs[2 * n_place:3 * n_place]
+    far_first, far_rest, out_ref, total = refs[3 * n_place:]
+    far = [far_first] + [far_rest.at[at] for at in range(n_place - 1)]
     n_irrep = total.shape[1]
     me_b, me_g = lax.axis_index("batch"), lax.axis_index("grp")
     core, first_c = me_g % 2, me_g // 2
     i_labels = [i_irrep[2 * (me_g % (2 * n_place)) + i] for i in range(2)]
     k_labels = [k_irrep[(me_b ^ half) * k_half + k] for half in range(2) for k in range(k_half)]
-    copies = []
-    for at in range(n_place):
-        here = []
-        for which, (src, dst) in enumerate(((own_refs, own), (twin_refs, twin), (near_refs, near), (far_refs, far))):
-            here.append(pltpu.make_async_copy(src[at], dst.at[at], sems.at[which, at]))
-        copies.append(here)
-    for here in copies:
-        for copy in here:
-            copy.start()
     total[...] = jnp.zeros_like(total)
     row = lax.broadcasted_iota(jnp.int32, (width, width), 0)
     col = lax.broadcasted_iota(jnp.int32, (width, width), 1)
     slot = (row + core * (width // 2)) & (width - 1)
     for at in range(n_place):
-        for copy in copies[at]:
-            copy.wait()
         c = first_c ^ at
         live = slot < virt_count[c]
         for half, side in enumerate((near, far)):
             for k in range(k_half):
                 amps = []
                 for i in range(2):
-                    amp = side[at, :, k, i].reshape(width, width)
+                    amp = side[at][:, k, i].reshape(width, width)
                     amps.append(jnp.where(live, amp, jnp.zeros((), amp.dtype)))
-                inter = jnp.concatenate([own[at, half * k_half + k], twin[at, half * k_half + k]], axis=0)
+                inter = jnp.concatenate([own[at][half * k_half + k], twin[at][half * k_half + k]], axis=0)
                 term = lax.dot_general(
                     jnp.concatenate(amps, axis=1), inter,
                     (((0,), (0,)), ((), ())), preferred_element_type=jnp.float32,
@@ -215,22 +202,15 @@
     near, far = [near0, near1, near2, near3], [far0, far123]
     own, twin = [own0, own1, own2, own3], [twin0, twin1, twin2, flip(own3, 1)]
 
-    any_spec = pl.BlockSpec(memory_space=pl.ANY)
+    here = pl.BlockSpec(memory_space=pltpu.VMEM)
     flops = 2 * 2 * k_half * 2 * n_place * width ** 3 * j_count
     tile = pl.pallas_call(
         functools.partial(tile_kernel, n_place, k_half, width, j_count),
-        in_specs=[pl.BlockSpec(memory_space=pltpu.SMEM)] * 4 + [any_spec] * (3 * n_place + 2),
-        out_specs=pl.BlockSpec(memory_space=pltpu.VMEM),
+        in_specs=[pl.BlockSpec(memory_space=pltpu.SMEM)] * 4 + [here] * (3 * n_place + 2),
+        out_specs=here,
         out_shape=jax.ShapeDtypeStruct((n_grp, 2, j_count, slab, width), jnp.bfloat16),
-        scratch_shapes=[
-            pltpu.VMEM((n_place, 2 * k_half, slab, j_count * width), jnp.bfloat16),
-            pltpu.VMEM((n_place, 2 * k_half, slab, j_count * width), jnp.bfloat16),
-            pltpu.VMEM((n_place, 2, k_half, 2, slab, width), jnp.bfloat16),
-            pltpu.VMEM((n_place, 2, k_half, 2, slab, width), jnp.bfloat16),
-            pltpu.VMEM((2, n_irrep, width, j_count * width), jnp.float32),
-            pltpu.SemaphoreType.DMA((4, n_place)),
-        ],
-        compiler_params=pltpu.CompilerParams(vmem_limit_bytes=24 * 2 ** 20),
+        scratch_shapes=[pltpu.VMEM((2, n_irrep, width, j_count * width), jnp.float32)],
+        compiler_params=pltpu.CompilerParams(vmem_limit_bytes=16 * 2 ** 20),
         cost_estimate=pl.CostEstimate(flops=flops, bytes_accessed=8 * 2 ** 20, transcendentals=0),
     )(k_irrep, i_irrep, j_irrep, virt_count, *own, *twin, *near, *far)
     result = lax.all_to_all(tile, "grp", split_axis=0, concat_axis=0, tiled=True)

time: 101 us -> 96.4 us (0.954)
  Pallas kernels: 7.48 us -> 3.12 us
    pallas_call x1, Pallas kernels: 7.48 us -> 3.12 us  [shards_tiled(): pl.pallas_call(functools.partial(tile_kernel, n_place, k_half, width, j_c...]
where the time goes in v3:
time: 96.4 us; the launch traced here: 96.2 us
  blocking collectives  52.7 us (55%)
  starting transfers between devices  18.4 us (19%)
  waiting for transfers between devices  17.8 us (18%)
  Pallas kernels  3.12 us (3%)
  other arithmetic  2.3 us (2%)
  local copies, waits for them, and re-layouts  1.62 us (2%)
    all_to_all x1, blocking collectives, shards_tiled(): lax.all_to_all(tile, 'grp', split_axis=0, concat_axis=0, tiled=True)  52.7 us
    ppermute x12, starting transfers between devices, flip(): return lax.ppermute(x, 'grp', [(d, d ^ bits) for d in range(n_grp)])  14.5 us
    ppermute x12, waiting for transfers between devices, flip(): return lax.ppermute(x, 'grp', [(d, d ^ bits) for d in range(n_grp)])  12.5 us
    ppermute x3, waiting for transfers between devices, over(): return lax.ppermute(x, 'batch', swap)  5.34 us
    ppermute x3, starting transfers between devices, over(): return lax.ppermute(x, 'batch', swap)  3.97 us
    pallas_call x1, Pallas kernels, shards_tiled(): pl.pallas_call(functools.partial(tile_kernel, n_place, k_half, width, j_c...  3.12 us
  transfers between devices with their start and end apart: 15, of which 8 were waited for; matrix products, arithmetic and copies ran while one was open for 1% of the time, Pallas kernels for 0%

profile of v3, /device:TPU:1, one launch (start us, length us, event | category | flops | bytes accessed | tf_op | source)
XLA Modules:
  0.0 96.2 jit_solution(3246867593616407375)
XLA Ops:
  0.0 1.2 %constant_dynamic-slice_fusion.1 = (bf16[3,4,1,2,64,128]{5,4,3,2,1,0:T(8,128)(2,1)S(1)}, bf16[3,4,1,2,64,128]{5,4,3,2,1,0:T(8,128)(2,1)S(1)}) fusion(bf16[3,4,2,2,64,128]{5,4,3,2,1,0:T(8,128)(2,1)} %bitcast.24, s32[]{:T(128)S(6)} %select_n.48, s32[]{:T(128)S(6)} %select_n.49), kind=kLoop, calls=%fused_computation.17 | loop fusion | bytes 1572872 | tf_op jit(solution)/shard_map/jit(dynamic_index_in_dim)/dynamic_slice | solution.py:183
  1.3 0.1 collective-permute-start
  1.4 0.2 broadcast_select_fusion
  1.7 0.1 reshape.21
  1.7 0.1 reshape.20
  1.9 1.2 %collective-permute-done = bf16[3,4,2,64,128]{4,3,2,0,1:T(8,128)(2,1)S(1)} collective-permute-done((bf16[3,4,2,64,128]{4,3,2,0,1:T(8,128)(2,1)S(1)}, bf16[3,4,2,64,128]{4,3,2,0,1:T(8,128)(2,1)S(1)}, u32[]{:S(2)}, u32[]{:S(2)}) %collective-permute-start) | collective-permute-done | bytes 393248 | tf_op jit(solution)/shard_map/ppermute | solution.py:171
  3.1 0.1 pad_maximum_fusion
  3.1 2.4 %collective-permute-start.1 = (bf16[3,64,512]{2,1,0:T(8,128)(2,1)S(1)}, bf16[3,64,512]{2,1,0:T(8,128)(2,1)S(1)}, u32[]{:S(2)}, u32[]{:S(2)}) collective-permute-start(bf16[3,64,512]{2,1,0:T(8,128)(2,1)S(1)} %reshape.20), channel_id=1, source_target_pairs={{0,16},{16,0},{1,17},{17,1},{2,18},{18,2},{3,19},{19,3},{4,20},{20... | collective-permute-start | bytes 589832 | tf_op jit(solution)/shard_map/ppermute | solution.py:177
  5.7 1.3 %collective-permute-start.6 = (bf16[2,3,2,64,128]{4,3,2,1,0:T(8,128)(2,1)S(1)}, bf16[2,3,2,64,128]{4,3,2,1,0:T(8,128)(2,1)S(1)}, u32[]{:S(2)}, u32[]{:S(2)}) collective-permute-start(bf16[2,3,2,64,128]{4,3,2,1,0:T(8,128)(2,1)S(1)} %get-tuple-element.29), channel_id=1, source_target_pairs={{0,2},{1,3},{2,0},{3,1},{4,6},{5,7},{6,4},{7,5},{8,10},{9,11},{10,... | collective-permute-start | bytes 589832 | tf_op jit(solution)/shard_map/ppermute | solution.py:171
  7.0 1.3 %collective-permute-start.8 = (bf16[2,3,2,64,128]{4,3,2,1,0:T(8,128)(2,1)S(1)}, bf16[2,3,2,64,128]{4,3,2,1,0:T(8,128)(2,1)S(1)}, u32[]{:S(2)}, u32[]{:S(2)}) collective-permute-start(bf16[2,3,2,64,128]{4,3,2,1,0:T(8,128)(2,1)S(1)} %get-tuple-element.30), channel_id=1, source_target_pairs={{0,6},{1,7},{2,4},{3,5},{4,2},{5,3},{6,0},{7,1},{8,14},{9,15},{10,... | collective-permute-start | bytes 589832 | tf_op jit(solution)/shard_map/ppermute | solution.py:171
  8.2 0.2 collective-permute-start.7
  8.4 2.1 %collective-permute-done.1 = bf16[3,64,512]{2,1,0:T(8,128)(2,1)S(1)} collective-permute-done((bf16[3,64,512]{2,1,0:T(8,128)(2,1)S(1)}, bf16[3,64,512]{2,1,0:T(8,128)(2,1)S(1)}, u32[]{:S(2)}, u32[]{:S(2)}) %collective-permute-start.1) | collective-permute-done | bytes 196640 | tf_op jit(solution)/shard_map/ppermute | solution.py:177
  10.6 0.9 collective-permute-start.4
  11.5 1.5 %collective-permute-start.3 = (bf16[6,64,512]{2,1,0:T(8,128)(2,1)S(1)}, bf16[6,64,512]{2,1,0:T(8,128)(2,1)S(1)}, u32[]{:S(2)}, u32[]{:S(2)}) collective-permute-start(bf16[6,64,512]{2,1,0:T(8,128)(2,1)S(1)} %constant_dynamic-update-slice_fusion.refs_0_), channel_id=1, source_target_pairs={{0,4},{1,5},{2,6},{3,7},{4,0},{5,1},{6,2},{7,3},{8,12},{9,13},{10,... | collective-permute-start | bytes 1179656 | tf_op jit(solution)/shard_map/ppermute | solution.py:171
  13.0 2.2 %collective-permute-done.6.refs_9_ = bf16[2,3,2,64,128]{4,3,2,1,0:T(8,128)(2,1)S(1)} collective-permute-done((bf16[2,3,2,64,128]{4,3,2,1,0:T(8,128)(2,1)S(1)}, bf16[2,3,2,64,128]{4,3,2,1,0:T(8,128)(2,1)S(1)}, u32[]{:S(2)}, u32[]{:S(2)}) %collective-permute-start.6) | collective-permute-done | bytes 196640 | tf_op jit(solution)/shard_map/ppermute | solution.py:171
  15.3 1.7 %collective-permute-start.2 = (bf16[6,64,512]{2,1,0:T(8,128)(2,1)S(1)}, bf16[6,64,512]{2,1,0:T(8,128)(2,1)S(1)}, u32[]{:S(2)}, u32[]{:S(2)}) collective-permute-start(bf16[6,64,512]{2,1,0:T(8,128)(2,1)S(1)} %constant_dynamic-update-slice_fusion.refs_0_), channel_id=1, source_target_pairs={{0,2},{1,3},{2,0},{3,1},{4,6},{5,7},{6,4},{7,5},{8,10},{9,11},{10,... | collective-permute-start | bytes 1179656 | tf_op jit(solution)/shard_map/ppermute | solution.py:171
  17.0 0.2 collective-permute-start.5
  17.2 0.1 pad_maximum_fusion.1
  17.3 1.3 %collective-permute-start.9 = (bf16[3,2,3,2,64,128]{5,4,3,2,1,0:T(8,128)(2,1)S(1)}, bf16[3,2,3,2,64,128]{5,4,3,2,1,0:T(8,128)(2,1)S(1)}, u32[]{:S(2)}, u32[]{:S(2)}) collective-permute-start(bf16[3,2,3,2,64,128]{5,4,3,2,1,0:T(8,128)(2,1)S(1)} %pad_maximum_fusion.1), channel_id=1, source_target_pairs={{0,16},{16,0},{1,17},{17,1},{2,18},{18,2},{3,19},{19,3},{4,20},{20... | collective-permute-start | bytes 1769480 | tf_op jit(solution)/shard_map/ppermute | solution.py:177
  18.6 3.2 %collective-permute-done.5.refs_12_ = bf16[2,3,2,64,128]{4,3,2,1,0:T(8,128)(2,1)S(1)} collective-permute-done((bf16[2,3,2,64,128]{4,3,2,1,0:T(8,128)(2,1)S(1)}, bf16[2,3,2,64,128]{4,3,2,1,0:T(8,128)(2,1)S(1)}, u32[]{:S(2)}, u32[]{:S(2)}) %collective-permute-start.5) | collective-permute-done | bytes 196640 | tf_op jit(solution)/shard_map/ppermute | solution.py:177
  21.8 3.3 %collective-permute-done.3.refs_2_ = bf16[6,64,512]{2,1,0:T(8,128)(2,1)S(1)} collective-permute-done((bf16[6,64,512]{2,1,0:T(8,128)(2,1)S(1)}, bf16[6,64,512]{2,1,0:T(8,128)(2,1)S(1)}, u32[]{:S(2)}, u32[]{:S(2)}) %collective-permute-start.3) | collective-permute-done | bytes 393248 | tf_op jit(solution)/shard_map/ppermute | solution.py:171
  25.1 1.9 %collective-permute-start.10 = (bf16[6,64,512]{2,1,0:T(8,128)(2,1)S(1)}, bf16[6,64,512]{2,1,0:T(8,128)(2,1)S(1)}, u32[]{:S(2)}, u32[]{:S(2)}) collective-permute-start(bf16[6,64,512]{2,1,0:T(8,128)(2,1)S(1)} %collective-permute-done.2.refs_1_), channel_id=1, source_target_pairs={{0,1},{1,0},{2,3},{3,2},{4,5},{5,4},{6,7},{7,6},{8,9},{9,8},{10,11... | collective-permute-start | bytes 1179656 | tf_op jit(solution)/shard_map/ppermute | solution.py:171
  27.1 1.5 %collective-permute-start.13 = (bf16[3,64,512]{2,1,0:T(8,128)(2,1)S(1)}, bf16[3,64,512]{2,1,0:T(8,128)(2,1)S(1)}, u32[]{:S(2)}, u32[]{:S(2)}) collective-permute-start(bf16[3,64,512]{2,1,0:T(8,128)(2,1)S(1)} %slice.23), channel_id=1, source_target_pairs={{0,2},{1,3},{2,0},{3,1},{4,6},{5,7},{6,4},{7,5},{8,10},{9,11},{10,... | collective-permute-start | bytes 589832 | tf_op jit(solution)/shard_map/ppermute | solution.py:171
  28.6 1.3 %collective-permute-start.12 = (bf16[3,64,512]{2,1,0:T(8,128)(2,1)S(1)}, bf16[3,64,512]{2,1,0:T(8,128)(2,1)S(1)}, u32[]{:S(2)}, u32[]{:S(2)}) collective-permute-start(bf16[3,64,512]{2,1,0:T(8,128)(2,1)S(1)} %slice.22), channel_id=1, source_target_pairs={{0,4},{1,5},{2,6},{3,7},{4,0},{5,1},{6,2},{7,3},{8,12},{9,13},{10,... | collective-permute-start | bytes 589832 | tf_op jit(solution)/shard_map/ppermute | solution.py:171
  29.9 3.2 %collective-permute-done.13 = bf16[3,64,512]{2,1,0:T(8,128)(2,1)S(1)} collective-permute-done((bf16[3,64,512]{2,1,0:T(8,128)(2,1)S(1)}, bf16[3,64,512]{2,1,0:T(8,128)(2,1)S(1)}, u32[]{:S(2)}, u32[]{:S(2)}) %collective-permute-start.13) | collective-permute-done | bytes 196640 | tf_op jit(solution)/shard_map/ppermute | solution.py:171
  33.1 1.1 %collective-permute-done.12 = bf16[3,64,512]{2,1,0:T(8,128)(2,1)S(1)} collective-permute-done((bf16[3,64,512]{2,1,0:T(8,128)(2,1)S(1)}, bf16[3,64,512]{2,1,0:T(8,128)(2,1)S(1)}, u32[]{:S(2)}, u32[]{:S(2)}) %collective-permute-start.12) | collective-permute-done | bytes 196640 | tf_op jit(solution)/shard_map/ppermute | solution.py:171
  34.3 2.7 %collective-permute-start.14 = (bf16[6,64,512]{2,1,0:T(8,128)(2,1)S(1)}, bf16[6,64,512]{2,1,0:T(8,128)(2,1)S(1)}, u32[]{:S(2)}, u32[]{:S(2)}) collective-permute-start(bf16[6,64,512]{2,1,0:T(8,128)(2,1)S(1)} %constant_dynamic-update-slice_fusion.2.refs_3_), channel_id=1, source_target_pairs={{0,1},{1,0},{2,3},{3,2},{4,5},{5,4},{6,7},{7,6},{8,9},{9,8},{10,11... | collective-permute-start | bytes 1179656 | tf_op jit(solution)/shard_map/ppermute | solution.py:171
  37.1 1.3 %collective-permute-done.14.refs_7_ = bf16[6,64,512]{2,1,0:T(8,128)(2,1)S(1)} collective-permute-done((bf16[6,64,512]{2,1,0:T(8,128)(2,1)S(1)}, bf16[6,64,512]{2,1,0:T(8,128)(2,1)S(1)}, u32[]{:S(2)}, u32[]{:S(2)}) %collective-permute-start.14) | collective-permute-done | bytes 393248 | tf_op jit(solution)/shard_map/ppermute | solution.py:171
  38.4 3.1 %shard_map.64 = bf16[16,2,4,64,128]{4,3,2,1,0:T(8,128)(2,1)S(1)} custom-call(s32[6]{0:T(128)S(1)} %copy-done, s32[16]{0:T(128)S(1)} %copy-done.1, s32[8]{0:T(128)S(1)} %copy-done.2, s32[8]{0:T(128)S(1)} %copy-done.3, bf16[6,64,512]{2,1,0:T(8,128)(2,1)S(1)} %constant_dynamic-update-slice_fusion.refs_0_, ...), custom_call_target="tpu_custom_call" | custom-call | flops 805306368 | bytes 8388608 | tf_op jit(solution)/shard_map/pallas_call | solution.py:207
  41.5 52.7 %all_to_all.5 = bf16[16,2,4,64,128]{4,3,2,1,0:T(8,128)(2,1)S(1)} all-to-all(bf16[16,2,4,64,128]{4,3,2,1,0:T(8,128)(2,1)S(1)} %shard_map.64), channel_id=1, replica_groups=mesh['batch'=2,'grp'=16] {'grp'}, dimensions={0} | all-to-all | bytes 4194304 | tf_op jit(solution)/shard_map/all_to_all | solution.py:216
  94.3 0.5 convert_element_type.11
  94.8 1.4 %fusion = bf16[8,2,4,64,128]{4,3,2,1,0:T(8,128)(2,1)} fusion(f32[16,2,4,64,128]{4,3,2,1,0:T(8,128)S(1)} %convert_element_type.11), kind=kLoop, calls=%fused_computation.1 | loop fusion | flops 1048576 | bytes 5242880 | tf_op jit(solution)/shard_map/convert_element_type | solution.py:218
  (27 shorter events, 0.2 us)
Async XLA Ops:
  0.0 1.4 %copy-start.4 = (bf16[3,64,8,128]{3,2,1,0:T(8,128)(2,1)S(1)}, bf16[3,64,8,128]{3,2,1,0:T(8,128)(2,1)}, u32[]{:S(2)}) copy-start(bf16[3,64,8,128]{3,2,1,0:T(8,128)(2,1)} %param.7) | copy-start | bytes 1179652
  1.3 1.8 %collective-permute-start = (bf16[3,4,2,64,128]{4,3,2,0,1:T(8,128)(2,1)S(1)}, bf16[3,4,2,64,128]{4,3,2,0,1:T(8,128)(2,1)S(1)}, u32[]{:S(2)}, u32[]{:S(2)}) collective-permute-start(bf16[3,4,2,64,128]{4,3,2,0,1:T(8,128)(2,1)S(1)} %bitcast.25), channel_id=1, source_target_pairs={{0,1},{1,0},{2,3},{3,2},{4,5},{5,4},{6,7},{7,6},{8,9},{9,8},{10,11... | collective-permute-start | bytes 1179656 | tf_op jit(solution)/shard_map/ppermute | solution.py:171
  3.1 7.4 %collective-permute-start.1 = (bf16[3,64,512]{2,1,0:T(8,128)(2,1)S(1)}, bf16[3,64,512]{2,1,0:T(8,128)(2,1)S(1)}, u32[]{:S(2)}, u32[]{:S(2)}) collective-permute-start(bf16[3,64,512]{2,1,0:T(8,128)(2,1)S(1)} %reshape.20), channel_id=1, source_target_pairs={{0,16},{16,0},{1,17},{17,1},{2,18},{18,2},{3,19},{19,3},{4,20},{20... | collective-permute-start | bytes 589832 | tf_op jit(solution)/shard_map/ppermute | solution.py:177
  5.6 32.8 %copy-start = (s32[6]{0:T(128)S(1)}, s32[6]{0:T(128)}, u32[]{:S(2)}) copy-start(s32[6]{0:T(128)} %k_irrep.1) | copy-start | bytes 76
  5.7 32.7 %copy-start.1 = (s32[16]{0:T(128)S(1)}, s32[16]{0:T(128)}, u32[]{:S(2)}) copy-start(s32[16]{0:T(128)} %i_irrep.1) | copy-start | bytes 196
  5.7 32.7 %copy-start.2 = (s32[8]{0:T(128)S(1)}, s32[8]{0:T(128)}, u32[]{:S(2)}) copy-start(s32[8]{0:T(128)} %j_irrep.1) | copy-start | bytes 100
  5.7 32.7 %copy-start.3 = (s32[8]{0:T(128)S(1)}, s32[8]{0:T(128)}, u32[]{:S(2)}) copy-start(s32[8]{0:T(128)} %virt_count.1) | copy-start | bytes 100
  5.7 9.6 %collective-permute-start.6 = (bf16[2,3,2,64,128]{4,3,2,1,0:T(8,128)(2,1)S(1)}, bf16[2,3,2,64,128]{4,3,2,1,0:T(8,128)(2,1)S(1)}, u32[]{:S(2)}, u32[]{:S(2)}) collective-permute-start(bf16[2,3,2,64,128]{4,3,2,1,0:T(8,128)(2,1)S(1)} %get-tuple-element.29), channel_id=1, source_target_pairs={{0,2},{1,3},{2,0},{3,1},{4,6},{5,7},{6,4},{7,5},{8,10},{9,11},{10,... | collective-permute-start | bytes 589832 | tf_op jit(solution)/shard_map/ppermute | solution.py:171
  7.0 10.0 %collective-permute-start.8 = (bf16[2,3,2,64,128]{4,3,2,1,0:T(8,128)(2,1)S(1)}, bf16[2,3,2,64,128]{4,3,2,1,0:T(8,128)(2,1)S(1)}, u32[]{:S(2)}, u32[]{:S(2)}) collective-permute-start(bf16[2,3,2,64,128]{4,3,2,1,0:T(8,128)(2,1)S(1)} %get-tuple-element.30), channel_id=1, source_target_pairs={{0,6},{1,7},{2,4},{3,5},{4,2},{5,3},{6,0},{7,1},{8,14},{9,15},{10,... | collective-permute-start | bytes 589832 | tf_op jit(solution)/shard_map/ppermute | solution.py:171
  8.2 9.0 %collective-permute-start.7 = (bf16[2,3,2,64,128]{4,3,2,1,0:T(8,128)(2,1)S(1)}, bf16[2,3,2,64,128]{4,3,2,1,0:T(8,128)(2,1)S(1)}, u32[]{:S(2)}, u32[]{:S(2)}) collective-permute-start(bf16[2,3,2,64,128]{4,3,2,1,0:T(8,128)(2,1)S(1)} %get-tuple-element.31), channel_id=1, source_target_pairs={{0,4},{1,5},{2,6},{3,7},{4,0},{5,1},{6,2},{7,3},{8,12},{9,13},{10,... | collective-permute-start | bytes 589832 | tf_op jit(solution)/shard_map/ppermute | solution.py:171
  10.6 11.2 %collective-permute-start.4 = (bf16[6,64,512]{2,1,0:T(8,128)(2,1)S(1)}, bf16[6,64,512]{2,1,0:T(8,128)(2,1)S(1)}, u32[]{:S(2)}, u32[]{:S(2)}) collective-permute-start(bf16[6,64,512]{2,1,0:T(8,128)(2,1)S(1)} %constant_dynamic-update-slice_fusion.refs_0_), channel_id=1, source_target_pairs={{0,1},{1,0},{2,3},{3,2},{4,5},{5,4},{6,7},{7,6},{8,9},{9,8},{10,11... | collective-permute-start | bytes 1179656 | tf_op jit(solution)/shard_map/ppermute | solution.py:171
  11.5 13.6 %collective-permute-start.3 = (bf16[6,64,512]{2,1,0:T(8,128)(2,1)S(1)}, bf16[6,64,512]{2,1,0:T(8,128)(2,1)S(1)}, u32[]{:S(2)}, u32[]{:S(2)}) collective-permute-start(bf16[6,64,512]{2,1,0:T(8,128)(2,1)S(1)} %constant_dynamic-update-slice_fusion.refs_0_), channel_id=1, source_target_pairs={{0,4},{1,5},{2,6},{3,7},{4,0},{5,1},{6,2},{7,3},{8,12},{9,13},{10,... | collective-permute-start | bytes 1179656 | tf_op jit(solution)/shard_map/ppermute | solution.py:171
  15.3 9.9 %collective-permute-start.2 = (bf16[6,64,512]{2,1,0:T(8,128)(2,1)S(1)}, bf16[6,64,512]{2,1,0:T(8,128)(2,1)S(1)}, u32[]{:S(2)}, u32[]{:S(2)}) collective-permute-start(bf16[6,64,512]{2,1,0:T(8,128)(2,1)S(1)} %constant_dynamic-update-slice_fusion.refs_0_), channel_id=1, source_target_pairs={{0,2},{1,3},{2,0},{3,1},{4,6},{5,7},{6,4},{7,5},{8,10},{9,11},{10,... | collective-permute-start | bytes 1179656 | tf_op jit(solution)/shard_map/ppermute | solution.py:171
  17.0 4.8 %collective-permute-start.5 = (bf16[2,3,2,64,128]{4,3,2,1,0:T(8,128)(2,1)S(1)}, bf16[2,3,2,64,128]{4,3,2,1,0:T(8,128)(2,1)S(1)}, u32[]{:S(2)}, u32[]{:S(2)}) collective-permute-start(bf16[2,3,2,64,128]{4,3,2,1,0:T(8,128)(2,1)S(1)} %get-tuple-element.32.refs_8_), channel_id=1, source_target_pairs={{0,16},{16,0},{1,17},{17,1},{2,18},{18,2},{3,19},{19,3},{4,20},{20... | collective-permute-start | bytes 589832 | tf_op jit(solution)/shard_map/ppermute | solution.py:177
  17.3 17.0 %collective-permute-start.9 = (bf16[3,2,3,2,64,128]{5,4,3,2,1,0:T(8,128)(2,1)S(1)}, bf16[3,2,3,2,64,128]{5,4,3,2,1,0:T(8,128)(2,1)S(1)}, u32[]{:S(2)}, u32[]{:S(2)}) collective-permute-start(bf16[3,2,3,2,64,128]{5,4,3,2,1,0:T(8,128)(2,1)S(1)} %pad_maximum_fusion.1), channel_id=1, source_target_pairs={{0,16},{16,0},{1,17},{17,1},{2,18},{18,2},{3,19},{19,3},{4,20},{20... | collective-permute-start | bytes 1769480 | tf_op jit(solution)/shard_map/ppermute | solution.py:177
  25.1 9.1 %collective-permute-start.10 = (bf16[6,64,512]{2,1,0:T(8,128)(2,1)S(1)}, bf16[6,64,512]{2,1,0:T(8,128)(2,1)S(1)}, u32[]{:S(2)}, u32[]{:S(2)}) collective-permute-start(bf16[6,64,512]{2,1,0:T(8,128)(2,1)S(1)} %collective-permute-done.2.refs_1_), channel_id=1, source_target_pairs={{0,1},{1,0},{2,3},{3,2},{4,5},{5,4},{6,7},{7,6},{8,9},{9,8},{10,11... | collective-permute-start | bytes 1179656 | tf_op jit(solution)/shard_map/ppermute | solution.py:171
  27.0 7.2 %collective-permute-start.11 = (bf16[6,64,512]{2,1,0:T(8,128)(2,1)S(1)}, bf16[6,64,512]{2,1,0:T(8,128)(2,1)S(1)}, u32[]{:S(2)}, u32[]{:S(2)}) collective-permute-start(bf16[6,64,512]{2,1,0:T(8,128)(2,1)S(1)} %collective-permute-done.3.refs_2_), channel_id=1, source_target_pairs={{0,1},{1,0},{2,3},{3,2},{4,5},{5,4},{6,7},{7,6},{8,9},{9,8},{10,11... | collective-permute-start | bytes 1179656 | tf_op jit(solution)/shard_map/ppermute | solution.py:171
  27.1 6.0 %collective-permute-start.13 = (bf16[3,64,512]{2,1,0:T(8,128)(2,1)S(1)}, bf16[3,64,512]{2,1,0:T(8,128)(2,1)S(1)}, u32[]{:S(2)}, u32[]{:S(2)}) collective-permute-start(bf16[3,64,512]{2,1,0:T(8,128)(2,1)S(1)} %slice.23), channel_id=1, source_target_pairs={{0,2},{1,3},{2,0},{3,1},{4,6},{5,7},{6,4},{7,5},{8,10},{9,11},{10,... | collective-permute-start | bytes 589832 | tf_op jit(solution)/shard_map/ppermute | solution.py:171
  28.6 5.6 %collective-permute-start.12 = (bf16[3,64,512]{2,1,0:T(8,128)(2,1)S(1)}, bf16[3,64,512]{2,1,0:T(8,128)(2,1)S(1)}, u32[]{:S(2)}, u32[]{:S(2)}) collective-permute-start(bf16[3,64,512]{2,1,0:T(8,128)(2,1)S(1)} %slice.22), channel_id=1, source_target_pairs={{0,4},{1,5},{2,6},{3,7},{4,0},{5,1},{6,2},{7,3},{8,12},{9,13},{10,... | collective-permute-start | bytes 589832 | tf_op jit(solution)/shard_map/ppermute | solution.py:171
  34.3 4.1 %collective-permute-start.14 = (bf16[6,64,512]{2,1,0:T(8,128)(2,1)S(1)}, bf16[6,64,512]{2,1,0:T(8,128)(2,1)S(1)}, u32[]{:S(2)}, u32[]{:S(2)}) collective-permute-start(bf16[6,64,512]{2,1,0:T(8,128)(2,1)S(1)} %constant_dynamic-update-slice_fusion.2.refs_3_), channel_id=1, source_target_pairs={{0,1},{1,0},{2,3},{3,2},{4,5},{5,4},{6,7},{7,6},{8,9},{9,8},{10,11... | collective-permute-start | bytes 1179656 | tf_op jit(solution)/shard_map/ppermute | solution.py:171

commit v4 on v3

--- a/solution.py
+++ b/solution.py
@@ -187,14 +187,15 @@
     def i_part(at):
         return lax.dynamic_index_in_dim(i_parts, at, 2, keepdims=False)
 
-    i_parts, away, mine = hold(i_parts, away, mine)
     other = over(away)
     near0, near1, near2, near3 = i_part(place), *(flip(i_part(place ^ m), 2 * m) for m in range(1, n_place))
     far0 = over(near0)
+    other, near1 = hold(other, near1)
+    near1, near2, near3, far0 = hold(near1, near2, near3, far0)
     own0 = jnp.concatenate([mine, other])
     own1, own2, twin0 = flip(own0, 2), flip(own0, 4), flip(own0, 1)
     far123 = over(jnp.stack([near1, near2, near3]))
-    own1, own2, twin0, far0 = hold(own1, own2, twin0, far0)
+    own1, own2, twin0 = hold(own1, own2, twin0)
     own3 = flip(own1[:k_half], 4), flip(own2[k_half:], 2)
     twin1, twin2 = flip(own1, 1), flip(own2, 1)
     far123, twin1, twin2, *own3 = hold(far123, twin1, twin2, *own3)
@@ -214,8 +215,8 @@
         cost_estimate=pl.CostEstimate(flops=flops, bytes_accessed=8 * 2 ** 20, transcendentals=0),
     )(k_irrep, i_irrep, j_irrep, virt_count, *own, *twin, *near, *far)
     result = lax.all_to_all(tile, "grp", split_axis=0, concat_axis=0, tiled=True)
-    result = result.reshape(2, i_total, j_count, slab, width).astype(jnp.float32)
-    return (result[0] + result[1]).astype(jnp.bfloat16)
+    result = result.reshape(2, i_total, j_count, slab, width)
+    return result[0] + result[1]
 
 
 def shards(n_batch, n_grp, amps, cycle_inter, k_irrep, i_irrep, j_irrep, virt_count):

time: 96.4 us -> 93.3 us (0.968)
  starting transfers between devices: 18.4 us -> 16.7 us
    ppermute x3, waiting for transfers between devices: 5.34 us -> 1.28 us  [over(): return lax.ppermute(x, 'batch', swap)]
    ppermute x12, waiting for transfers between devices: 12.5 us -> 16.1 us  [flip(): return lax.ppermute(x, 'grp', [(d, d ^ bits) for d in range(n_grp)])]
    ppermute x12, starting transfers between devices: 14.5 us -> 12.1 us  [flip(): return lax.ppermute(x, 'grp', [(d, d ^ bits) for d in range(n_grp)])]
    convert_element_type x2 -> x0, other arithmetic: 1.92 us -> none  [the longest x1 1.45 us: shards_tiled(): return (result[0] + result[1]).astype(jnp.bfloat16)]
    dynamic_slice x2 -> x1, local copies, waits for them, and re-layouts: 1.26 us -> 0.03 us  [shards_tiled(): keep = lax.dynamic_index_in_dim(parts, core, 2, keepdims=False)]
    dynamic_slice x1 -> x2, local copies, waits for them, and re-layouts: 0.03 us -> 1.26 us  [shards_tiled(): take = flip(lax.dynamic_index_in_dim(parts, 1 - core, 2, keepdims=False), 1)]
    add x0 -> x1, other arithmetic: none -> 1.08 us  [shards_tiled(): return result[0] + result[1]]
where the time goes in v4:
time: 93.3 us; the launch traced here: 93.1 us
  blocking collectives  52.7 us (56%)
  waiting for transfers between devices  17.4 us (19%)
  starting transfers between devices  16.7 us (18%)
  Pallas kernels  3.13 us (3%)
  local copies, waits for them, and re-layouts  1.56 us (2%)
  other arithmetic  1.44 us (2%)
    all_to_all x1, blocking collectives, shards_tiled(): lax.all_to_all(tile, 'grp', split_axis=0, concat_axis=0, tiled=True)  52.7 us
    ppermute x12, waiting for transfers between devices, flip(): return lax.ppermute(x, 'grp', [(d, d ^ bits) for d in range(n_grp)])  16.1 us
    ppermute x12, starting transfers between devices, flip(): return lax.ppermute(x, 'grp', [(d, d ^ bits) for d in range(n_grp)])  12.1 us
    ppermute x3, starting transfers between devices, over(): return lax.ppermute(x, 'batch', swap)  4.54 us
    pallas_call x1, Pallas kernels, shards_tiled(): pl.pallas_call(functools.partial(tile_kernel, n_place, k_half, width, j_c...  3.13 us
  transfers between devices with their start and end apart: 15, of which 8 were waited for; matrix products, arithmetic and copies ran while one was open for 1% of the time, Pallas kernels for 0%

profile of v4, /device:TPU:1, one launch (start us, length us, event | category | flops | bytes accessed | tf_op | source)
XLA Modules:
  0.0 93.1 jit_solution(10228903112329350838)
XLA Ops:
  0.0 1.2 %constant_dynamic-slice_fusion = (bf16[3,4,1,2,64,128]{5,4,3,2,1,0:T(8,128)(2,1)S(1)}, bf16[3,4,1,2,64,128]{5,4,3,2,1,0:T(8,128)(2,1)S(1)}) fusion(bf16[3,4,2,2,64,128]{5,4,3,2,1,0:T(8,128)(2,1)} %bitcast.24, s32[]{:T(128)S(6)} %select_n.52, s32[]{:T(128)S(6)} %select_n.51), kind=kLoop, calls=%fused_computation.26 | loop fusion | bytes 1572872 | tf_op jit(solution)/shard_map/jit(dynamic_index_in_dim)/dynamic_slice | solution.py:184
  1.3 0.1 collective-permute-start.1
  1.4 0.2 broadcast_select_fusion
  1.6 0.1 reshape.17
  1.7 2.8 %collective-permute-start = (bf16[3,64,512]{2,1,0:T(8,128)(2,1)S(1)}, bf16[3,64,512]{2,1,0:T(8,128)(2,1)S(1)}, u32[]{:S(2)}, u32[]{:S(2)}) collective-permute-start(bf16[3,64,512]{2,1,0:T(8,128)(2,1)S(1)} %reshape.17), channel_id=1, source_target_pairs={{0,16},{16,0},{1,17},{17,1},{2,18},{18,2},{3,19},{19,3},{4,20},{20... | collective-permute-start | bytes 589832 | tf_op jit(solution)/shard_map/ppermute | solution.py:177
  4.5 0.1 fusion.1
  4.6 0.0 copy-start.2
  4.7 1.3 %collective-permute-start.2 = (bf16[2,3,2,64,128]{4,3,2,1,0:T(8,128)(2,1)S(1)}, bf16[2,3,2,64,128]{4,3,2,1,0:T(8,128)(2,1)S(1)}, u32[]{:S(2)}, u32[]{:S(2)}) collective-permute-start(bf16[2,3,2,64,128]{4,3,2,1,0:T(8,128)(2,1)S(1)} %get-tuple-element.34), channel_id=1, source_target_pairs={{0,2},{1,3},{2,0},{3,1},{4,6},{5,7},{6,4},{7,5},{8,10},{9,11},{10,... | collective-permute-start | bytes 589832 | tf_op jit(solution)/shard_map/ppermute | solution.py:171
  5.9 0.1 reshape.16
  6.0 1.4 %collective-permute-start.6 = (bf16[2,3,2,64,128]{4,3,2,1,0:T(8,128)(2,1)S(1)}, bf16[2,3,2,64,128]{4,3,2,1,0:T(8,128)(2,1)S(1)}, u32[]{:S(2)}, u32[]{:S(2)}) collective-permute-start(bf16[2,3,2,64,128]{4,3,2,1,0:T(8,128)(2,1)S(1)} %get-tuple-element.35), channel_id=1, source_target_pairs={{0,4},{1,5},{2,6},{3,7},{4,0},{5,1},{6,2},{7,3},{8,12},{9,13},{10,... | collective-permute-start | bytes 589832 | tf_op jit(solution)/shard_map/ppermute | solution.py:171
  7.4 0.1 collective-permute-start.7
  7.5 0.9 collective-permute-start.8
  8.4 1.3 %collective-permute-done = bf16[3,64,512]{2,1,0:T(8,128)(2,1)S(1)} collective-permute-done((bf16[3,64,512]{2,1,0:T(8,128)(2,1)S(1)}, bf16[3,64,512]{2,1,0:T(8,128)(2,1)S(1)}, u32[]{:S(2)}, u32[]{:S(2)}) %collective-permute-start) | collective-permute-done | bytes 196640 | tf_op jit(solution)/shard_map/ppermute | solution.py:177
  9.7 1.2 %collective-permute-done.2.refs_9_ = bf16[2,3,2,64,128]{4,3,2,1,0:T(8,128)(2,1)S(1)} collective-permute-done((bf16[2,3,2,64,128]{4,3,2,1,0:T(8,128)(2,1)S(1)}, bf16[2,3,2,64,128]{4,3,2,1,0:T(8,128)(2,1)S(1)}, u32[]{:S(2)}, u32[]{:S(2)}) %collective-permute-start.2) | collective-permute-done | bytes 196640 | tf_op jit(solution)/shard_map/ppermute | solution.py:171
  10.9 1.2 %collective-permute-start.5 = (bf16[6,64,512]{2,1,0:T(8,128)(2,1)S(1)}, bf16[6,64,512]{2,1,0:T(8,128)(2,1)S(1)}, u32[]{:S(2)}, u32[]{:S(2)}) collective-permute-start(bf16[6,64,512]{2,1,0:T(8,128)(2,1)S(1)} %constant_dynamic-update-slice_fusion.refs_0_), channel_id=1, source_target_pairs={{0,1},{1,0},{2,3},{3,2},{4,5},{5,4},{6,7},{7,6},{8,9},{9,8},{10,11... | collective-permute-start | bytes 1179656 | tf_op jit(solution)/shard_map/ppermute | solution.py:171
  12.1 1.3 %collective-permute-start.4 = (bf16[6,64,512]{2,1,0:T(8,128)(2,1)S(1)}, bf16[6,64,512]{2,1,0:T(8,128)(2,1)S(1)}, u32[]{:S(2)}, u32[]{:S(2)}) collective-permute-start(bf16[6,64,512]{2,1,0:T(8,128)(2,1)S(1)} %constant_dynamic-update-slice_fusion.refs_0_), channel_id=1, source_target_pairs={{0,4},{1,5},{2,6},{3,7},{4,0},{5,1},{6,2},{7,3},{8,12},{9,13},{10,... | collective-permute-start | bytes 1179656 | tf_op jit(solution)/shard_map/ppermute | solution.py:171
  13.4 1.2 %collective-permute-start.3 = (bf16[6,64,512]{2,1,0:T(8,128)(2,1)S(1)}, bf16[6,64,512]{2,1,0:T(8,128)(2,1)S(1)}, u32[]{:S(2)}, u32[]{:S(2)}) collective-permute-start(bf16[6,64,512]{2,1,0:T(8,128)(2,1)S(1)} %constant_dynamic-update-slice_fusion.refs_0_), channel_id=1, source_target_pairs={{0,2},{1,3},{2,0},{3,1},{4,6},{5,7},{6,4},{7,5},{8,10},{9,11},{10,... | collective-permute-start | bytes 1179656 | tf_op jit(solution)/shard_map/ppermute | solution.py:171
  14.7 1.5 %collective-permute-done.7.refs_11_ = bf16[2,3,2,64,128]{4,3,2,1,0:T(8,128)(2,1)S(1)} collective-permute-done((bf16[2,3,2,64,128]{4,3,2,1,0:T(8,128)(2,1)S(1)}, bf16[2,3,2,64,128]{4,3,2,1,0:T(8,128)(2,1)S(1)}, u32[]{:S(2)}, u32[]{:S(2)}) %collective-permute-start.7) | collective-permute-done | bytes 196640 | tf_op jit(solution)/shard_map/ppermute | solution.py:171
  16.1 0.1 pad_maximum_fusion
  16.2 0.9 collective-permute-start.9
  17.1 7.5 %collective-permute-done.4.refs_2_ = bf16[6,64,512]{2,1,0:T(8,128)(2,1)S(1)} collective-permute-done((bf16[6,64,512]{2,1,0:T(8,128)(2,1)S(1)}, bf16[6,64,512]{2,1,0:T(8,128)(2,1)S(1)}, u32[]{:S(2)}, u32[]{:S(2)}) %collective-permute-start.4) | collective-permute-done | bytes 393248 | tf_op jit(solution)/shard_map/ppermute | solution.py:171
  24.6 0.2 collective-permute-done.3.refs_1_
  24.8 1.2 %collective-permute-start.10 = (bf16[6,64,512]{2,1,0:T(8,128)(2,1)S(1)}, bf16[6,64,512]{2,1,0:T(8,128)(2,1)S(1)}, u32[]{:S(2)}, u32[]{:S(2)}) collective-permute-start(bf16[6,64,512]{2,1,0:T(8,128)(2,1)S(1)} %collective-permute-done.3.refs_1_), channel_id=1, source_target_pairs={{0,1},{1,0},{2,3},{3,2},{4,5},{5,4},{6,7},{7,6},{8,9},{9,8},{10,11... | collective-permute-start | bytes 1179656 | tf_op jit(solution)/shard_map/ppermute | solution.py:171
  26.1 1.2 %collective-permute-start.13 = (bf16[3,64,512]{2,1,0:T(8,128)(2,1)S(1)}, bf16[3,64,512]{2,1,0:T(8,128)(2,1)S(1)}, u32[]{:S(2)}, u32[]{:S(2)}) collective-permute-start(bf16[3,64,512]{2,1,0:T(8,128)(2,1)S(1)} %slice.23), channel_id=1, source_target_pairs={{0,2},{1,3},{2,0},{3,1},{4,6},{5,7},{6,4},{7,5},{8,10},{9,11},{10,... | collective-permute-start | bytes 589832 | tf_op jit(solution)/shard_map/ppermute | solution.py:171
  27.3 1.3 %collective-permute-start.12 = (bf16[3,64,512]{2,1,0:T(8,128)(2,1)S(1)}, bf16[3,64,512]{2,1,0:T(8,128)(2,1)S(1)}, u32[]{:S(2)}, u32[]{:S(2)}) collective-permute-start(bf16[3,64,512]{2,1,0:T(8,128)(2,1)S(1)} %slice.22), channel_id=1, source_target_pairs={{0,4},{1,5},{2,6},{3,7},{4,0},{5,1},{6,2},{7,3},{8,12},{9,13},{10,... | collective-permute-start | bytes 589832 | tf_op jit(solution)/shard_map/ppermute | solution.py:171
  28.6 3.5 %collective-permute-done.13 = bf16[3,64,512]{2,1,0:T(8,128)(2,1)S(1)} collective-permute-done((bf16[3,64,512]{2,1,0:T(8,128)(2,1)S(1)}, bf16[3,64,512]{2,1,0:T(8,128)(2,1)S(1)}, u32[]{:S(2)}, u32[]{:S(2)}) %collective-permute-start.13) | collective-permute-done | bytes 196640 | tf_op jit(solution)/shard_map/ppermute | solution.py:171
  32.1 0.9 collective-permute-done.12
  33.0 1.7 %collective-permute-start.14 = (bf16[6,64,512]{2,1,0:T(8,128)(2,1)S(1)}, bf16[6,64,512]{2,1,0:T(8,128)(2,1)S(1)}, u32[]{:S(2)}, u32[]{:S(2)}) collective-permute-start(bf16[6,64,512]{2,1,0:T(8,128)(2,1)S(1)} %constant_dynamic-update-slice_fusion.2.refs_3_), channel_id=1, source_target_pairs={{0,1},{1,0},{2,3},{3,2},{4,5},{5,4},{6,7},{7,6},{8,9},{9,8},{10,11... | collective-permute-start | bytes 1179656 | tf_op jit(solution)/shard_map/ppermute | solution.py:171
  34.8 1.3 %collective-permute-done.14.refs_7_ = bf16[6,64,512]{2,1,0:T(8,128)(2,1)S(1)} collective-permute-done((bf16[6,64,512]{2,1,0:T(8,128)(2,1)S(1)}, bf16[6,64,512]{2,1,0:T(8,128)(2,1)S(1)}, u32[]{:S(2)}, u32[]{:S(2)}) %collective-permute-start.14) | collective-permute-done | bytes 393248 | tf_op jit(solution)/shard_map/ppermute | solution.py:171
  36.1 3.1 %shard_map.64 = bf16[16,2,4,64,128]{4,3,2,1,0:T(8,128)(2,1)S(1)} custom-call(s32[6]{0:T(128)S(1)} %copy-done, s32[16]{0:T(128)S(1)} %copy-done.1, s32[8]{0:T(128)S(1)} %copy-done.2, s32[8]{0:T(128)S(1)} %copy-done.3, bf16[6,64,512]{2,1,0:T(8,128)(2,1)S(1)} %constant_dynamic-update-slice_fusion.refs_0_, ...), custom_call_target="tpu_custom_call" | custom-call | flops 805306368 | bytes 8388608 | tf_op jit(solution)/shard_map/pallas_call | solution.py:208
  39.3 52.7 %all_to_all.5 = bf16[16,2,4,64,128]{4,3,2,1,0:T(8,128)(2,1)S(1)} all-to-all(bf16[16,2,4,64,128]{4,3,2,1,0:T(8,128)(2,1)S(1)} %shard_map.64), channel_id=1, replica_groups=mesh['batch'=2,'grp'=16] {'grp'}, dimensions={0} | all-to-all | bytes 4194304 | tf_op jit(solution)/shard_map/all_to_all | solution.py:217
  92.0 1.1 %slice_add_fusion = bf16[8,2,4,64,128]{4,3,2,1,0:T(8,128)(2,1)} fusion(bf16[16,2,4,64,128]{4,3,2,1,0:T(8,128)(2,1)S(1)} %all_to_all.5), kind=kLoop, calls=%fused_computation.8 | loop fusion | flops 524288 | bytes 3145728 | tf_op jit(solution)/shard_map/add | solution.py:219
  (25 shorter events, 0.2 us)
Async XLA Ops:
  0.0 1.4 %copy-start.4 = (bf16[3,64,8,128]{3,2,1,0:T(8,128)(2,1)S(1)}, bf16[3,64,8,128]{3,2,1,0:T(8,128)(2,1)}, u32[]{:S(2)}) copy-start(bf16[3,64,8,128]{3,2,1,0:T(8,128)(2,1)} %param.7) | copy-start | bytes 1179652
  1.3 3.2 %collective-permute-start.1 = (bf16[3,4,2,64,128]{4,3,2,0,1:T(8,128)(2,1)S(1)}, bf16[3,4,2,64,128]{4,3,2,0,1:T(8,128)(2,1)S(1)}, u32[]{:S(2)}, u32[]{:S(2)}) collective-permute-start(bf16[3,4,2,64,128]{4,3,2,0,1:T(8,128)(2,1)S(1)} %bitcast.25), channel_id=1, source_target_pairs={{0,1},{1,0},{2,3},{3,2},{4,5},{5,4},{6,7},{7,6},{8,9},{9,8},{10,11... | collective-permute-start | bytes 1179656 | tf_op jit(solution)/shard_map/ppermute | solution.py:171
  1.7 8.0 %collective-permute-start = (bf16[3,64,512]{2,1,0:T(8,128)(2,1)S(1)}, bf16[3,64,512]{2,1,0:T(8,128)(2,1)S(1)}, u32[]{:S(2)}, u32[]{:S(2)}) collective-permute-start(bf16[3,64,512]{2,1,0:T(8,128)(2,1)S(1)} %reshape.17), channel_id=1, source_target_pairs={{0,16},{16,0},{1,17},{17,1},{2,18},{18,2},{3,19},{19,3},{4,20},{20... | collective-permute-start | bytes 589832 | tf_op jit(solution)/shard_map/ppermute | solution.py:177
  4.6 31.5 %copy-start = (s32[6]{0:T(128)S(1)}, s32[6]{0:T(128)}, u32[]{:S(2)}) copy-start(s32[6]{0:T(128)} %k_irrep.1) | copy-start | bytes 76
  4.6 31.5 %copy-start.1 = (s32[16]{0:T(128)S(1)}, s32[16]{0:T(128)}, u32[]{:S(2)}) copy-start(s32[16]{0:T(128)} %i_irrep.1) | copy-start | bytes 196
  4.6 31.5 %copy-start.2 = (s32[8]{0:T(128)S(1)}, s32[8]{0:T(128)}, u32[]{:S(2)}) copy-start(s32[8]{0:T(128)} %j_irrep.1) | copy-start | bytes 100
  4.6 31.5 %copy-start.3 = (s32[8]{0:T(128)S(1)}, s32[8]{0:T(128)}, u32[]{:S(2)}) copy-start(s32[8]{0:T(128)} %virt_count.1) | copy-start | bytes 100
  4.7 6.2 %collective-permute-start.2 = (bf16[2,3,2,64,128]{4,3,2,1,0:T(8,128)(2,1)S(1)}, bf16[2,3,2,64,128]{4,3,2,1,0:T(8,128)(2,1)S(1)}, u32[]{:S(2)}, u32[]{:S(2)}) collective-permute-start(bf16[2,3,2,64,128]{4,3,2,1,0:T(8,128)(2,1)S(1)} %get-tuple-element.34), channel_id=1, source_target_pairs={{0,2},{1,3},{2,0},{3,1},{4,6},{5,7},{6,4},{7,5},{8,10},{9,11},{10,... | collective-permute-start | bytes 589832 | tf_op jit(solution)/shard_map/ppermute | solution.py:171
  6.0 7.4 %collective-permute-start.6 = (bf16[2,3,2,64,128]{4,3,2,1,0:T(8,128)(2,1)S(1)}, bf16[2,3,2,64,128]{4,3,2,1,0:T(8,128)(2,1)S(1)}, u32[]{:S(2)}, u32[]{:S(2)}) collective-permute-start(bf16[2,3,2,64,128]{4,3,2,1,0:T(8,128)(2,1)S(1)} %get-tuple-element.35), channel_id=1, source_target_pairs={{0,4},{1,5},{2,6},{3,7},{4,0},{5,1},{6,2},{7,3},{8,12},{9,13},{10,... | collective-permute-start | bytes 589832 | tf_op jit(solution)/shard_map/ppermute | solution.py:171
  7.4 8.8 %collective-permute-start.7 = (bf16[2,3,2,64,128]{4,3,2,1,0:T(8,128)(2,1)S(1)}, bf16[2,3,2,64,128]{4,3,2,1,0:T(8,128)(2,1)S(1)}, u32[]{:S(2)}, u32[]{:S(2)}) collective-permute-start(bf16[2,3,2,64,128]{4,3,2,1,0:T(8,128)(2,1)S(1)} %get-tuple-element.36), channel_id=1, source_target_pairs={{0,6},{1,7},{2,4},{3,5},{4,2},{5,3},{6,0},{7,1},{8,14},{9,15},{10,... | collective-permute-start | bytes 589832 | tf_op jit(solution)/shard_map/ppermute | solution.py:171
  7.5 8.6 %collective-permute-start.8 = (bf16[2,3,2,64,128]{4,3,2,1,0:T(8,128)(2,1)S(1)}, bf16[2,3,2,64,128]{4,3,2,1,0:T(8,128)(2,1)S(1)}, u32[]{:S(2)}, u32[]{:S(2)}) collective-permute-start(bf16[2,3,2,64,128]{4,3,2,1,0:T(8,128)(2,1)S(1)} %get-tuple-element.33.refs_8_), channel_id=1, source_target_pairs={{0,16},{16,0},{1,17},{17,1},{2,18},{18,2},{3,19},{19,3},{4,20},{20... | collective-permute-start | bytes 589832 | tf_op jit(solution)/shard_map/ppermute | solution.py:177
  10.9 6.2 %collective-permute-start.5 = (bf16[6,64,512]{2,1,0:T(8,128)(2,1)S(1)}, bf16[6,64,512]{2,1,0:T(8,128)(2,1)S(1)}, u32[]{:S(2)}, u32[]{:S(2)}) collective-permute-start(bf16[6,64,512]{2,1,0:T(8,128)(2,1)S(1)} %constant_dynamic-update-slice_fusion.refs_0_), channel_id=1, source_target_pairs={{0,1},{1,0},{2,3},{3,2},{4,5},{5,4},{6,7},{7,6},{8,9},{9,8},{10,11... | collective-permute-start | bytes 1179656 | tf_op jit(solution)/shard_map/ppermute | solution.py:171
  12.1 12.5 %collective-permute-start.4 = (bf16[6,64,512]{2,1,0:T(8,128)(2,1)S(1)}, bf16[6,64,512]{2,1,0:T(8,128)(2,1)S(1)}, u32[]{:S(2)}, u32[]{:S(2)}) collective-permute-start(bf16[6,64,512]{2,1,0:T(8,128)(2,1)S(1)} %constant_dynamic-update-slice_fusion.refs_0_), channel_id=1, source_target_pairs={{0,4},{1,5},{2,6},{3,7},{4,0},{5,1},{6,2},{7,3},{8,12},{9,13},{10,... | collective-permute-start | bytes 1179656 | tf_op jit(solution)/shard_map/ppermute | solution.py:171
  13.4 11.4 %collective-permute-start.3 = (bf16[6,64,512]{2,1,0:T(8,128)(2,1)S(1)}, bf16[6,64,512]{2,1,0:T(8,128)(2,1)S(1)}, u32[]{:S(2)}, u32[]{:S(2)}) collective-permute-start(bf16[6,64,512]{2,1,0:T(8,128)(2,1)S(1)} %constant_dynamic-update-slice_fusion.refs_0_), channel_id=1, source_target_pairs={{0,2},{1,3},{2,0},{3,1},{4,6},{5,7},{6,4},{7,5},{8,10},{9,11},{10,... | collective-permute-start | bytes 1179656 | tf_op jit(solution)/shard_map/ppermute | solution.py:171
  16.2 16.8 %collective-permute-start.9 = (bf16[3,2,3,2,64,128]{5,4,3,2,1,0:T(8,128)(2,1)S(1)}, bf16[3,2,3,2,64,128]{5,4,3,2,1,0:T(8,128)(2,1)S(1)}, u32[]{:S(2)}, u32[]{:S(2)}) collective-permute-start(bf16[3,2,3,2,64,128]{5,4,3,2,1,0:T(8,128)(2,1)S(1)} %pad_maximum_fusion), channel_id=1, source_target_pairs={{0,16},{16,0},{1,17},{17,1},{2,18},{18,2},{3,19},{19,3},{4,20},{20... | collective-permute-start | bytes 1769480 | tf_op jit(solution)/shard_map/ppermute | solution.py:177
  24.8 8.2 %collective-permute-start.10 = (bf16[6,64,512]{2,1,0:T(8,128)(2,1)S(1)}, bf16[6,64,512]{2,1,0:T(8,128)(2,1)S(1)}, u32[]{:S(2)}, u32[]{:S(2)}) collective-permute-start(bf16[6,64,512]{2,1,0:T(8,128)(2,1)S(1)} %collective-permute-done.3.refs_1_), channel_id=1, source_target_pairs={{0,1},{1,0},{2,3},{3,2},{4,5},{5,4},{6,7},{7,6},{8,9},{9,8},{10,11... | collective-permute-start | bytes 1179656 | tf_op jit(solution)/shard_map/ppermute | solution.py:171
  26.0 6.9 %collective-permute-start.11 = (bf16[6,64,512]{2,1,0:T(8,128)(2,1)S(1)}, bf16[6,64,512]{2,1,0:T(8,128)(2,1)S(1)}, u32[]{:S(2)}, u32[]{:S(2)}) collective-permute-start(bf16[6,64,512]{2,1,0:T(8,128)(2,1)S(1)} %collective-permute-done.4.refs_2_), channel_id=1, source_target_pairs={{0,1},{1,0},{2,3},{3,2},{4,5},{5,4},{6,7},{7,6},{8,9},{9,8},{10,11... | collective-permute-start | bytes 1179656 | tf_op jit(solution)/shard_map/ppermute | solution.py:171
  26.1 6.0 %collective-permute-start.13 = (bf16[3,64,512]{2,1,0:T(8,128)(2,1)S(1)}, bf16[3,64,512]{2,1,0:T(8,128)(2,1)S(1)}, u32[]{:S(2)}, u32[]{:S(2)}) collective-permute-start(bf16[3,64,512]{2,1,0:T(8,128)(2,1)S(1)} %slice.23), channel_id=1, source_target_pairs={{0,2},{1,3},{2,0},{3,1},{4,6},{5,7},{6,4},{7,5},{8,10},{9,11},{10,... | collective-permute-start | bytes 589832 | tf_op jit(solution)/shard_map/ppermute | solution.py:171
  27.3 5.6 %collective-permute-start.12 = (bf16[3,64,512]{2,1,0:T(8,128)(2,1)S(1)}, bf16[3,64,512]{2,1,0:T(8,128)(2,1)S(1)}, u32[]{:S(2)}, u32[]{:S(2)}) collective-permute-start(bf16[3,64,512]{2,1,0:T(8,128)(2,1)S(1)} %slice.22), channel_id=1, source_target_pairs={{0,4},{1,5},{2,6},{3,7},{4,0},{5,1},{6,2},{7,3},{8,12},{9,13},{10,... | collective-permute-start | bytes 589832 | tf_op jit(solution)/shard_map/ppermute | solution.py:171
  33.0 3.1 %collective-permute-start.14 = (bf16[6,64,512]{2,1,0:T(8,128)(2,1)S(1)}, bf16[6,64,512]{2,1,0:T(8,128)(2,1)S(1)}, u32[]{:S(2)}, u32[]{:S(2)}) collective-permute-start(bf16[6,64,512]{2,1,0:T(8,128)(2,1)S(1)} %constant_dynamic-update-slice_fusion.2.refs_3_), channel_id=1, source_target_pairs={{0,1},{1,0},{2,3},{3,2},{4,5},{5,4},{6,7},{7,6},{8,9},{9,8},{10,11... | collective-permute-start | bytes 1179656 | tf_op jit(solution)/shard_map/ppermute | solution.py:171

commit v5 on v4

--- a/solution.py
+++ b/solution.py
@@ -113,36 +113,54 @@
     return result.reshape(i_total, j_count, slab, width)
 
 
-def tile_kernel(n_place, k_half, width, j_count, k_irrep, i_irrep, j_irrep, virt_count, *refs):
-    own, twin, near = refs[:n_place], refs[n_place:2 * n_place], refs[2 * n_place:3 * n_place]
-    far_first, far_rest, out_ref, total = refs[3 * n_place:]
-    far = [far_first] + [far_rest.at[at] for at in range(n_place - 1)]
-    n_irrep = total.shape[1]
+def device_labels(n_place, k_half, k_irrep, i_irrep):
     me_b, me_g = lax.axis_index("batch"), lax.axis_index("grp")
-    core, first_c = me_g % 2, me_g // 2
     i_labels = [i_irrep[2 * (me_g % (2 * n_place)) + i] for i in range(2)]
     k_labels = [k_irrep[(me_b ^ half) * k_half + k] for half in range(2) for k in range(k_half)]
+    return me_b, me_g % 2, me_g // 2, k_labels, i_labels
+
+
+def add_terms(n_place, k_half, pieces, k_irrep, i_irrep, virt_count, total):
+    width = total.shape[2]
+    _, core, first_c, k_labels, i_labels = device_labels(n_place, k_half, k_irrep, i_irrep)
+    row = lax.broadcasted_iota(jnp.int32, (width, width), 0)
+    slot = (row + core * (width // 2)) & (width - 1)
+    for at, half, side, own, twin in pieces:
+        c = first_c ^ at
+        live = slot < virt_count[c]
+        for k in range(k_half):
+            amps = []
+            for i in range(2):
+                amp = side[:, k, i].reshape(width, width)
+                amps.append(jnp.where(live, amp, jnp.zeros((), amp.dtype)))
+            inter = jnp.concatenate([own[half * k_half + k], twin[half * k_half + k]], axis=0)
+            term = lax.dot_general(
+                jnp.concatenate(amps, axis=1), inter, (((0,), (0,)), ((), ())), preferred_element_type=jnp.float32
+            )
+            for i in range(2):
+                p = c ^ k_labels[half * k_half + k] ^ i_labels[i]
+                total[i, p] += term[i * width:(i + 1) * width]
+
+
+def early_kernel(n_place, k_half, k_irrep, i_irrep, virt_count, *refs):
+    m = n_place - 1
+    own, twin, near, (far, total) = refs[:m], refs[m:2 * m], refs[2 * m:3 * m], refs[3 * m:]
     total[...] = jnp.zeros_like(total)
+    pieces = [(at, 0, near[at], own[at], twin[at]) for at in range(m)] + [(0, 1, far, own[0], twin[0])]
+    add_terms(n_place, k_half, pieces, k_irrep, i_irrep, virt_count, total)
+
+
+def late_kernel(n_place, k_half, k_irrep, i_irrep, virt_count, j_irrep, *refs):
+    m = n_place - 1
+    own, twin, (near, far, _, out_ref, total) = refs[:m], refs[m:2 * m], refs[2 * m:]
+    n_irrep, width = total.shape[1:3]
+    j_count = out_ref.shape[2]
+    pieces = [(at, 1, far.at[at - 1], own[at - 1], twin[at - 1]) for at in range(1, n_place)]
+    pieces.append((m, 0, near, own[m - 1], twin[m - 1]))
+    add_terms(n_place, k_half, pieces, k_irrep, i_irrep, virt_count, total)
+    me_b, _, _, _, i_labels = device_labels(n_place, k_half, k_irrep, i_irrep)
     row = lax.broadcasted_iota(jnp.int32, (width, width), 0)
     col = lax.broadcasted_iota(jnp.int32, (width, width), 1)
-    slot = (row + core * (width // 2)) & (width - 1)
-    for at in range(n_place):
-        c = first_c ^ at
-        live = slot < virt_count[c]
-        for half, side in enumerate((near, far)):
-            for k in range(k_half):
-                amps = []
-                for i in range(2):
-                    amp = side[at][:, k, i].reshape(width, width)
-                    amps.append(jnp.where(live, amp, jnp.zeros((), amp.dtype)))
-                inter = jnp.concatenate([own[at][half * k_half + k], twin[at][half * k_half + k]], axis=0)
-                term = lax.dot_general(
-                    jnp.concatenate(amps, axis=1), inter,
-                    (((0,), (0,)), ((), ())), preferred_element_type=jnp.float32,
-                )
-                for i in range(2):
-                    p = c ^ k_labels[half * k_half + k] ^ i_labels[i]
-                    total[i, p] += term[i * width:(i + 1) * width]
 
     @pl.loop(0, n_irrep)
     def _(p):
@@ -198,22 +216,33 @@
     own1, own2, twin0 = hold(own1, own2, twin0)
     own3 = flip(own1[:k_half], 4), flip(own2[k_half:], 2)
     twin1, twin2 = flip(own1, 1), flip(own2, 1)
-    far123, twin1, twin2, *own3 = hold(far123, twin1, twin2, *own3)
+    here, scalars = pl.BlockSpec(memory_space=pltpu.VMEM), pl.BlockSpec(memory_space=pltpu.SMEM)
+    terms = jax.ShapeDtypeStruct((2, n_irrep, width, j_count * width), jnp.float32)
+    flops = 2 * k_half * 2 * n_place * width ** 3 * j_count
+    cost = pl.CostEstimate(flops=flops, bytes_accessed=2 ** 20, transcendentals=0)
+    params = pltpu.CompilerParams(vmem_limit_bytes=16 * 2 ** 20)
+    operands = [own0, own1, own2, twin0, twin1, twin2, near0, near1, near2, far0]
+    early = pl.pallas_call(
+        functools.partial(early_kernel, n_place, k_half),
+        in_specs=[scalars] * 3 + [here] * len(operands),
+        out_specs=here,
+        out_shape=terms,
+        compiler_params=params,
+        cost_estimate=cost,
+    )(k_irrep, i_irrep, virt_count, *operands)
+    far123, early, *own3 = hold(far123, early, *own3)
     own3 = jnp.concatenate(own3)
-    near, far = [near0, near1, near2, near3], [far0, far123]
-    own, twin = [own0, own1, own2, own3], [twin0, twin1, twin2, flip(own3, 1)]
-
-    here = pl.BlockSpec(memory_space=pltpu.VMEM)
-    flops = 2 * 2 * k_half * 2 * n_place * width ** 3 * j_count
-    tile = pl.pallas_call(
-        functools.partial(tile_kernel, n_place, k_half, width, j_count),
-        in_specs=[pl.BlockSpec(memory_space=pltpu.SMEM)] * 4 + [here] * (3 * n_place + 2),
-        out_specs=here,
-        out_shape=jax.ShapeDtypeStruct((n_grp, 2, j_count, slab, width), jnp.bfloat16),
-        scratch_shapes=[pltpu.VMEM((2, n_irrep, width, j_count * width), jnp.float32)],
-        compiler_params=pltpu.CompilerParams(vmem_limit_bytes=16 * 2 ** 20),
-        cost_estimate=pl.CostEstimate(flops=flops, bytes_accessed=8 * 2 ** 20, transcendentals=0),
-    )(k_irrep, i_irrep, j_irrep, virt_count, *own, *twin, *near, *far)
+    twin3 = flip(own3, 1)
+    operands = [own1, own2, own3, twin1, twin2, twin3, near3, far123, early]
+    tile, _ = pl.pallas_call(
+        functools.partial(late_kernel, n_place, k_half),
+        in_specs=[scalars] * 4 + [here] * len(operands),
+        out_specs=[here, here],
+        out_shape=[jax.ShapeDtypeStruct((n_grp, 2, j_count, slab, width), jnp.bfloat16), terms],
+        input_output_aliases={3 + len(operands): 1},
+        compiler_params=params,
+        cost_estimate=cost,
+    )(k_irrep, i_irrep, virt_count, j_irrep, *operands)
     result = lax.all_to_all(tile, "grp", split_axis=0, concat_axis=0, tiled=True)
     result = result.reshape(2, i_total, j_count, slab, width)
     return result[0] + result[1]

time: 93.3 us -> 92.2 us (0.988)
  waiting for transfers between devices: 17.4 us -> 15.5 us
    ppermute x12, waiting for transfers between devices: 16.1 us -> 14.2 us  [flip(): return lax.ppermute(x, 'grp', [(d, d ^ bits) for d in range(n_grp)])]
    pallas_call x1 -> x2, Pallas kernels: 3.13 us -> 3.94 us  [the longest x1 2.08 us: shards_tiled(): pl.pallas_call(functools.partial(late_kernel, n_place, k_half), in_specs=...]
  transfers between devices with their start and end apart: 15 -> 15, of which waited for: 8 -> 8; matrix products, arithmetic and copies ran while one was open for 1% -> 1% of each run, Pallas kernels for 0% -> 2%
where the time goes in v5:
time: 92.2 us; the launch traced here: 92 us
  blocking collectives  52.7 us (57%)
  starting transfers between devices  16.7 us (18%)
  waiting for transfers between devices  15.5 us (17%)
  Pallas kernels  3.94 us (4%)
  local copies, waits for them, and re-layouts  1.56 us (2%)
  other arithmetic  1.44 us (2%)
    all_to_all x1, blocking collectives, shards_tiled(): lax.all_to_all(tile, 'grp', split_axis=0, concat_axis=0, tiled=True)  52.7 us
    ppermute x12, waiting for transfers between devices, flip(): return lax.ppermute(x, 'grp', [(d, d ^ bits) for d in range(n_grp)])  14.2 us
    ppermute x12, starting transfers between devices, flip(): return lax.ppermute(x, 'grp', [(d, d ^ bits) for d in range(n_grp)])  12.2 us
    ppermute x3, starting transfers between devices, over(): return lax.ppermute(x, 'batch', swap)  4.47 us
    pallas_call x1, Pallas kernels, shards_tiled(): pl.pallas_call(functools.partial(late_kernel, n_place, k_half), in_specs=...  2.08 us
    pallas_call x1, Pallas kernels, shards_tiled(): pl.pallas_call(functools.partial(early_kernel, n_place, k_half), in_specs...  1.86 us
  transfers between devices with their start and end apart: 15, of which 8 were waited for; matrix products, arithmetic and copies ran while one was open for 1% of the time, Pallas kernels for 2%

profile of v5, /device:TPU:1, one launch (start us, length us, event | category | flops | bytes accessed | tf_op | source)
XLA Modules:
  0.0 92.0 jit_solution(14989934368122601698)
XLA Ops:
  0.0 1.2 %constant_dynamic-slice_fusion = (bf16[3,4,1,2,64,128]{5,4,3,2,1,0:T(8,128)(2,1)S(1)}, bf16[3,4,1,2,64,128]{5,4,3,2,1,0:T(8,128)(2,1)S(1)}) fusion(bf16[3,4,2,2,64,128]{5,4,3,2,1,0:T(8,128)(2,1)} %bitcast.24, s32[]{:T(128)S(6)} %select_n.52, s32[]{:T(128)S(6)} %select_n.51), kind=kLoop, calls=%fused_computation.26 | loop fusion | bytes 1572872 | tf_op jit(solution)/shard_map/jit(dynamic_index_in_dim)/dynamic_slice | solution.py:202
  1.3 0.1 collective-permute-start.1
  1.4 0.2 broadcast_select_fusion
  1.6 0.1 reshape.17
  1.7 2.8 %collective-permute-start = (bf16[3,64,512]{2,1,0:T(8,128)(2,1)S(1)}, bf16[3,64,512]{2,1,0:T(8,128)(2,1)S(1)}, u32[]{:S(2)}, u32[]{:S(2)}) collective-permute-start(bf16[3,64,512]{2,1,0:T(8,128)(2,1)S(1)} %reshape.17), channel_id=1, source_target_pairs={{0,16},{16,0},{1,17},{17,1},{2,18},{18,2},{3,19},{19,3},{4,20},{20... | collective-permute-start | bytes 589832 | tf_op jit(solution)/shard_map/ppermute | solution.py:195
  4.6 0.1 fusion.1
  4.7 1.3 %collective-permute-start.2 = (bf16[2,3,2,64,128]{4,3,2,1,0:T(8,128)(2,1)S(1)}, bf16[2,3,2,64,128]{4,3,2,1,0:T(8,128)(2,1)S(1)}, u32[]{:S(2)}, u32[]{:S(2)}) collective-permute-start(bf16[2,3,2,64,128]{4,3,2,1,0:T(8,128)(2,1)S(1)} %get-tuple-element.34), channel_id=1, source_target_pairs={{0,2},{1,3},{2,0},{3,1},{4,6},{5,7},{6,4},{7,5},{8,10},{9,11},{10,... | collective-permute-start | bytes 589832 | tf_op jit(solution)/shard_map/ppermute | solution.py:189
  5.9 0.1 reshape.16
  6.0 1.4 %collective-permute-start.6 = (bf16[2,3,2,64,128]{4,3,2,1,0:T(8,128)(2,1)S(1)}, bf16[2,3,2,64,128]{4,3,2,1,0:T(8,128)(2,1)S(1)}, u32[]{:S(2)}, u32[]{:S(2)}) collective-permute-start(bf16[2,3,2,64,128]{4,3,2,1,0:T(8,128)(2,1)S(1)} %get-tuple-element.35), channel_id=1, source_target_pairs={{0,4},{1,5},{2,6},{3,7},{4,0},{5,1},{6,2},{7,3},{8,12},{9,13},{10,... | collective-permute-start | bytes 589832 | tf_op jit(solution)/shard_map/ppermute | solution.py:189
  7.4 0.2 collective-permute-start.7
  7.6 0.9 collective-permute-start.8
  8.5 1.2 %collective-permute-done = bf16[3,64,512]{2,1,0:T(8,128)(2,1)S(1)} collective-permute-done((bf16[3,64,512]{2,1,0:T(8,128)(2,1)S(1)}, bf16[3,64,512]{2,1,0:T(8,128)(2,1)S(1)}, u32[]{:S(2)}, u32[]{:S(2)}) %collective-permute-start) | collective-permute-done | bytes 196640 | tf_op jit(solution)/shard_map/ppermute | solution.py:195
  9.7 1.2 %collective-permute-done.2.refs_7_ = bf16[2,3,2,64,128]{4,3,2,1,0:T(8,128)(2,1)S(1)} collective-permute-done((bf16[2,3,2,64,128]{4,3,2,1,0:T(8,128)(2,1)S(1)}, bf16[2,3,2,64,128]{4,3,2,1,0:T(8,128)(2,1)S(1)}, u32[]{:S(2)}, u32[]{:S(2)}) %collective-permute-start.2) | collective-permute-done | bytes 196640 | tf_op jit(solution)/shard_map/ppermute | solution.py:189
  10.9 1.2 %collective-permute-start.5 = (bf16[6,64,512]{2,1,0:T(8,128)(2,1)S(1)}, bf16[6,64,512]{2,1,0:T(8,128)(2,1)S(1)}, u32[]{:S(2)}, u32[]{:S(2)}) collective-permute-start(bf16[6,64,512]{2,1,0:T(8,128)(2,1)S(1)} %constant_dynamic-update-slice_fusion.refs_0_), channel_id=1, source_target_pairs={{0,1},{1,0},{2,3},{3,2},{4,5},{5,4},{6,7},{7,6},{8,9},{9,8},{10,11... | collective-permute-start | bytes 1179656 | tf_op jit(solution)/shard_map/ppermute | solution.py:189
  12.1 1.3 %collective-permute-start.4 = (bf16[6,64,512]{2,1,0:T(8,128)(2,1)S(1)}, bf16[6,64,512]{2,1,0:T(8,128)(2,1)S(1)}, u32[]{:S(2)}, u32[]{:S(2)}) collective-permute-start(bf16[6,64,512]{2,1,0:T(8,128)(2,1)S(1)} %constant_dynamic-update-slice_fusion.refs_0_), channel_id=1, source_target_pairs={{0,4},{1,5},{2,6},{3,7},{4,0},{5,1},{6,2},{7,3},{8,12},{9,13},{10,... | collective-permute-start | bytes 1179656 | tf_op jit(solution)/shard_map/ppermute | solution.py:189
  13.4 1.2 %collective-permute-start.3 = (bf16[6,64,512]{2,1,0:T(8,128)(2,1)S(1)}, bf16[6,64,512]{2,1,0:T(8,128)(2,1)S(1)}, u32[]{:S(2)}, u32[]{:S(2)}) collective-permute-start(bf16[6,64,512]{2,1,0:T(8,128)(2,1)S(1)} %constant_dynamic-update-slice_fusion.refs_0_), channel_id=1, source_target_pairs={{0,2},{1,3},{2,0},{3,1},{4,6},{5,7},{6,4},{7,5},{8,10},{9,11},{10,... | collective-permute-start | bytes 1179656 | tf_op jit(solution)/shard_map/ppermute | solution.py:189
  14.6 1.5 %collective-permute-done.7.refs_6_ = bf16[2,3,2,64,128]{4,3,2,1,0:T(8,128)(2,1)S(1)} collective-permute-done((bf16[2,3,2,64,128]{4,3,2,1,0:T(8,128)(2,1)S(1)}, bf16[2,3,2,64,128]{4,3,2,1,0:T(8,128)(2,1)S(1)}, u32[]{:S(2)}, u32[]{:S(2)}) %collective-permute-start.7) | collective-permute-done | bytes 196640 | tf_op jit(solution)/shard_map/ppermute | solution.py:189
  16.1 0.1 pad_maximum_fusion
  16.2 0.9 collective-permute-start.9
  17.1 7.5 %collective-permute-done.4.refs_2_.refs_1_ = bf16[6,64,512]{2,1,0:T(8,128)(2,1)S(1)} collective-permute-done((bf16[6,64,512]{2,1,0:T(8,128)(2,1)S(1)}, bf16[6,64,512]{2,1,0:T(8,128)(2,1)S(1)}, u32[]{:S(2)}, u32[]{:S(2)}) %collective-permute-start.4) | collective-permute-done | bytes 393248 | tf_op jit(solution)/shard_map/ppermute | solution.py:189
  24.6 0.2 collective-permute-done.3.refs_1_.refs_0_
  24.8 1.2 %collective-permute-start.10 = (bf16[6,64,512]{2,1,0:T(8,128)(2,1)S(1)}, bf16[6,64,512]{2,1,0:T(8,128)(2,1)S(1)}, u32[]{:S(2)}, u32[]{:S(2)}) collective-permute-start(bf16[6,64,512]{2,1,0:T(8,128)(2,1)S(1)} %collective-permute-done.3.refs_1_.refs_0_), channel_id=1, source_target_pairs={{0,1},{1,0},{2,3},{3,2},{4,5},{5,4},{6,7},{7,6},{8,9},{9,8},{10,11... | collective-permute-start | bytes 1179656 | tf_op jit(solution)/shard_map/ppermute | solution.py:189
  26.1 1.2 %collective-permute-start.13 = (bf16[3,64,512]{2,1,0:T(8,128)(2,1)S(1)}, bf16[3,64,512]{2,1,0:T(8,128)(2,1)S(1)}, u32[]{:S(2)}, u32[]{:S(2)}) collective-permute-start(bf16[3,64,512]{2,1,0:T(8,128)(2,1)S(1)} %slice.23), channel_id=1, source_target_pairs={{0,2},{1,3},{2,0},{3,1},{4,6},{5,7},{6,4},{7,5},{8,10},{9,11},{10,... | collective-permute-start | bytes 589832 | tf_op jit(solution)/shard_map/ppermute | solution.py:189
  27.3 1.3 %collective-permute-start.12 = (bf16[3,64,512]{2,1,0:T(8,128)(2,1)S(1)}, bf16[3,64,512]{2,1,0:T(8,128)(2,1)S(1)}, u32[]{:S(2)}, u32[]{:S(2)}) collective-permute-start(bf16[3,64,512]{2,1,0:T(8,128)(2,1)S(1)} %slice.22), channel_id=1, source_target_pairs={{0,4},{1,5},{2,6},{3,7},{4,0},{5,1},{6,2},{7,3},{8,12},{9,13},{10,... | collective-permute-start | bytes 589832 | tf_op jit(solution)/shard_map/ppermute | solution.py:189
  28.7 1.9 %shard_map.64.refs_8_ = f32[2,8,128,512]{3,2,1,0:T(8,128)S(1)} custom-call(s32[6]{0:T(128)S(1)} %copy-done, s32[16]{0:T(128)S(1)} %copy-done.1, s32[8]{0:T(128)S(1)} %copy-done.2, bf16[6,64,512]{2,1,0:T(8,128)(2,1)S(1)} %constant_dynamic-update-slice_fusion.refs_0_, bf16[6,64,512]{2,1,0:T(8,128)(2,1)S(1)} %collective-permute-done.3.refs_1_.refs_0_, ...), custom_call_target="tpu_custom_call" | custom-call | flops 402653184 | bytes 1048576 | tf_op jit(solution)/shard_map/pallas_call | solution.py:225
  30.5 1.6 %collective-permute-done.13 = bf16[3,64,512]{2,1,0:T(8,128)(2,1)S(1)} collective-permute-done((bf16[3,64,512]{2,1,0:T(8,128)(2,1)S(1)}, bf16[3,64,512]{2,1,0:T(8,128)(2,1)S(1)}, u32[]{:S(2)}, u32[]{:S(2)}) %collective-permute-start.13) | collective-permute-done | bytes 196640 | tf_op jit(solution)/shard_map/ppermute | solution.py:189
  32.1 0.9 collective-permute-done.12
  33.0 1.7 %collective-permute-start.14 = (bf16[6,64,512]{2,1,0:T(8,128)(2,1)S(1)}, bf16[6,64,512]{2,1,0:T(8,128)(2,1)S(1)}, u32[]{:S(2)}, u32[]{:S(2)}) collective-permute-start(bf16[6,64,512]{2,1,0:T(8,128)(2,1)S(1)} %constant_dynamic-update-slice_fusion.2.refs_2_), channel_id=1, source_target_pairs={{0,1},{1,0},{2,3},{3,2},{4,5},{5,4},{6,7},{7,6},{8,9},{9,8},{10,11... | collective-permute-start | bytes 1179656 | tf_op jit(solution)/shard_map/ppermute | solution.py:189
  34.8 1.3 %collective-permute-done.14.refs_5_ = bf16[6,64,512]{2,1,0:T(8,128)(2,1)S(1)} collective-permute-done((bf16[6,64,512]{2,1,0:T(8,128)(2,1)S(1)}, bf16[6,64,512]{2,1,0:T(8,128)(2,1)S(1)}, u32[]{:S(2)}, u32[]{:S(2)}) %collective-permute-start.14) | collective-permute-done | bytes 393248 | tf_op jit(solution)/shard_map/ppermute | solution.py:189
  36.1 2.1 %shard_map.65 = (bf16[16,2,4,64,128]{4,3,2,1,0:T(8,128)(2,1)S(1)}, f32[2,8,128,512]{3,2,1,0:T(8,128)S(1)}) custom-call(s32[6]{0:T(128)S(1)} %copy-done, s32[16]{0:T(128)S(1)} %copy-done.1, s32[8]{0:T(128)S(1)} %copy-done.2, s32[8]{0:T(128)S(1)} %copy-done.3, ...), custom_call_target="tpu_custom_call", output_to_operand_aliasing={{1}: (12, {})} | custom-call | flops 402653184 | bytes 1048576 | tf_op jit(solution)/shard_map/pallas_call | solution.py:237
  38.2 52.7 %all_to_all.5 = bf16[16,2,4,64,128]{4,3,2,1,0:T(8,128)(2,1)S(1)} all-to-all(bf16[16,2,4,64,128]{4,3,2,1,0:T(8,128)(2,1)S(1)} %get-tuple-element.32), channel_id=1, replica_groups=mesh['batch'=2,'grp'=16] {'grp'}, dimensions={0} | all-to-all | bytes 4194304 | tf_op jit(solution)/shard_map/all_to_all | solution.py:246
  90.9 1.1 %slice_add_fusion = bf16[8,2,4,64,128]{4,3,2,1,0:T(8,128)(2,1)} fusion(bf16[16,2,4,64,128]{4,3,2,1,0:T(8,128)(2,1)S(1)} %all_to_all.5), kind=kLoop, calls=%fused_computation.8 | loop fusion | flops 524288 | bytes 3145728 | tf_op jit(solution)/shard_map/add | solution.py:248
  (26 shorter events, 0.2 us)
Async XLA Ops:
  0.0 1.4 %copy-start.4 = (bf16[3,64,8,128]{3,2,1,0:T(8,128)(2,1)S(1)}, bf16[3,64,8,128]{3,2,1,0:T(8,128)(2,1)}, u32[]{:S(2)}) copy-start(bf16[3,64,8,128]{3,2,1,0:T(8,128)(2,1)} %param.7) | copy-start | bytes 1179652
  1.3 3.2 %collective-permute-start.1 = (bf16[3,4,2,64,128]{4,3,2,0,1:T(8,128)(2,1)S(1)}, bf16[3,4,2,64,128]{4,3,2,0,1:T(8,128)(2,1)S(1)}, u32[]{:S(2)}, u32[]{:S(2)}) collective-permute-start(bf16[3,4,2,64,128]{4,3,2,0,1:T(8,128)(2,1)S(1)} %bitcast.25), channel_id=1, source_target_pairs={{0,1},{1,0},{2,3},{3,2},{4,5},{5,4},{6,7},{7,6},{8,9},{9,8},{10,11... | collective-permute-start | bytes 1179656 | tf_op jit(solution)/shard_map/ppermute | solution.py:189
  1.7 8.0 %collective-permute-start = (bf16[3,64,512]{2,1,0:T(8,128)(2,1)S(1)}, bf16[3,64,512]{2,1,0:T(8,128)(2,1)S(1)}, u32[]{:S(2)}, u32[]{:S(2)}) collective-permute-start(bf16[3,64,512]{2,1,0:T(8,128)(2,1)S(1)} %reshape.17), channel_id=1, source_target_pairs={{0,16},{16,0},{1,17},{17,1},{2,18},{18,2},{3,19},{19,3},{4,20},{20... | collective-permute-start | bytes 589832 | tf_op jit(solution)/shard_map/ppermute | solution.py:195
  4.5 24.1 %copy-start = (s32[6]{0:T(128)S(1)}, s32[6]{0:T(128)}, u32[]{:S(2)}) copy-start(s32[6]{0:T(128)} %k_irrep.3) | copy-start | bytes 76
  4.5 24.1 %copy-start.1 = (s32[16]{0:T(128)S(1)}, s32[16]{0:T(128)}, u32[]{:S(2)}) copy-start(s32[16]{0:T(128)} %i_irrep.3) | copy-start | bytes 196
  4.6 24.1 %copy-start.2 = (s32[8]{0:T(128)S(1)}, s32[8]{0:T(128)}, u32[]{:S(2)}) copy-start(s32[8]{0:T(128)} %virt_count.3) | copy-start | bytes 100
  4.7 6.2 %collective-permute-start.2 = (bf16[2,3,2,64,128]{4,3,2,1,0:T(8,128)(2,1)S(1)}, bf16[2,3,2,64,128]{4,3,2,1,0:T(8,128)(2,1)S(1)}, u32[]{:S(2)}, u32[]{:S(2)}) collective-permute-start(bf16[2,3,2,64,128]{4,3,2,1,0:T(8,128)(2,1)S(1)} %get-tuple-element.34), channel_id=1, source_target_pairs={{0,2},{1,3},{2,0},{3,1},{4,6},{5,7},{6,4},{7,5},{8,10},{9,11},{10,... | collective-permute-start | bytes 589832 | tf_op jit(solution)/shard_map/ppermute | solution.py:189
  6.0 7.4 %collective-permute-start.6 = (bf16[2,3,2,64,128]{4,3,2,1,0:T(8,128)(2,1)S(1)}, bf16[2,3,2,64,128]{4,3,2,1,0:T(8,128)(2,1)S(1)}, u32[]{:S(2)}, u32[]{:S(2)}) collective-permute-start(bf16[2,3,2,64,128]{4,3,2,1,0:T(8,128)(2,1)S(1)} %get-tuple-element.35), channel_id=1, source_target_pairs={{0,4},{1,5},{2,6},{3,7},{4,0},{5,1},{6,2},{7,3},{8,12},{9,13},{10,... | collective-permute-start | bytes 589832 | tf_op jit(solution)/shard_map/ppermute | solution.py:189
  7.4 8.7 %collective-permute-start.7 = (bf16[2,3,2,64,128]{4,3,2,1,0:T(8,128)(2,1)S(1)}, bf16[2,3,2,64,128]{4,3,2,1,0:T(8,128)(2,1)S(1)}, u32[]{:S(2)}, u32[]{:S(2)}) collective-permute-start(bf16[2,3,2,64,128]{4,3,2,1,0:T(8,128)(2,1)S(1)} %get-tuple-element.36), channel_id=1, source_target_pairs={{0,6},{1,7},{2,4},{3,5},{4,2},{5,3},{6,0},{7,1},{8,14},{9,15},{10,... | collective-permute-start | bytes 589832 | tf_op jit(solution)/shard_map/ppermute | solution.py:189
  7.6 8.5 %collective-permute-start.8 = (bf16[2,3,2,64,128]{4,3,2,1,0:T(8,128)(2,1)S(1)}, bf16[2,3,2,64,128]{4,3,2,1,0:T(8,128)(2,1)S(1)}, u32[]{:S(2)}, u32[]{:S(2)}) collective-permute-start(bf16[2,3,2,64,128]{4,3,2,1,0:T(8,128)(2,1)S(1)} %get-tuple-element.33.refs_6_), channel_id=1, source_target_pairs={{0,16},{16,0},{1,17},{17,1},{2,18},{18,2},{3,19},{19,3},{4,20},{20... | collective-permute-start | bytes 589832 | tf_op jit(solution)/shard_map/ppermute | solution.py:195
  10.9 6.1 %collective-permute-start.5 = (bf16[6,64,512]{2,1,0:T(8,128)(2,1)S(1)}, bf16[6,64,512]{2,1,0:T(8,128)(2,1)S(1)}, u32[]{:S(2)}, u32[]{:S(2)}) collective-permute-start(bf16[6,64,512]{2,1,0:T(8,128)(2,1)S(1)} %constant_dynamic-update-slice_fusion.refs_0_), channel_id=1, source_target_pairs={{0,1},{1,0},{2,3},{3,2},{4,5},{5,4},{6,7},{7,6},{8,9},{9,8},{10,11... | collective-permute-start | bytes 1179656 | tf_op jit(solution)/shard_map/ppermute | solution.py:189
  12.1 12.5 %collective-permute-start.4 = (bf16[6,64,512]{2,1,0:T(8,128)(2,1)S(1)}, bf16[6,64,512]{2,1,0:T(8,128)(2,1)S(1)}, u32[]{:S(2)}, u32[]{:S(2)}) collective-permute-start(bf16[6,64,512]{2,1,0:T(8,128)(2,1)S(1)} %constant_dynamic-update-slice_fusion.refs_0_), channel_id=1, source_target_pairs={{0,4},{1,5},{2,6},{3,7},{4,0},{5,1},{6,2},{7,3},{8,12},{9,13},{10,... | collective-permute-start | bytes 1179656 | tf_op jit(solution)/shard_map/ppermute | solution.py:189
  13.4 11.4 %collective-permute-start.3 = (bf16[6,64,512]{2,1,0:T(8,128)(2,1)S(1)}, bf16[6,64,512]{2,1,0:T(8,128)(2,1)S(1)}, u32[]{:S(2)}, u32[]{:S(2)}) collective-permute-start(bf16[6,64,512]{2,1,0:T(8,128)(2,1)S(1)} %constant_dynamic-update-slice_fusion.refs_0_), channel_id=1, source_target_pairs={{0,2},{1,3},{2,0},{3,1},{4,6},{5,7},{6,4},{7,5},{8,10},{9,11},{10,... | collective-permute-start | bytes 1179656 | tf_op jit(solution)/shard_map/ppermute | solution.py:189
  16.2 16.8 %collective-permute-start.9 = (bf16[3,2,3,2,64,128]{5,4,3,2,1,0:T(8,128)(2,1)S(1)}, bf16[3,2,3,2,64,128]{5,4,3,2,1,0:T(8,128)(2,1)S(1)}, u32[]{:S(2)}, u32[]{:S(2)}) collective-permute-start(bf16[3,2,3,2,64,128]{5,4,3,2,1,0:T(8,128)(2,1)S(1)} %pad_maximum_fusion), channel_id=1, source_target_pairs={{0,16},{16,0},{1,17},{17,1},{2,18},{18,2},{3,19},{19,3},{4,20},{20... | collective-permute-start | bytes 1769480 | tf_op jit(solution)/shard_map/ppermute | solution.py:195
  24.8 3.8 %collective-permute-start.10 = (bf16[6,64,512]{2,1,0:T(8,128)(2,1)S(1)}, bf16[6,64,512]{2,1,0:T(8,128)(2,1)S(1)}, u32[]{:S(2)}, u32[]{:S(2)}) collective-permute-start(bf16[6,64,512]{2,1,0:T(8,128)(2,1)S(1)} %collective-permute-done.3.refs_1_.refs_0_), channel_id=1, source_target_pairs={{0,1},{1,0},{2,3},{3,2},{4,5},{5,4},{6,7},{7,6},{8,9},{9,8},{10,11... | collective-permute-start | bytes 1179656 | tf_op jit(solution)/shard_map/ppermute | solution.py:189
  26.0 2.6 %collective-permute-start.11 = (bf16[6,64,512]{2,1,0:T(8,128)(2,1)S(1)}, bf16[6,64,512]{2,1,0:T(8,128)(2,1)S(1)}, u32[]{:S(2)}, u32[]{:S(2)}) collective-permute-start(bf16[6,64,512]{2,1,0:T(8,128)(2,1)S(1)} %collective-permute-done.4.refs_2_.refs_1_), channel_id=1, source_target_pairs={{0,1},{1,0},{2,3},{3,2},{4,5},{5,4},{6,7},{7,6},{8,9},{9,8},{10,11... | collective-permute-start | bytes 1179656 | tf_op jit(solution)/shard_map/ppermute | solution.py:189
  26.1 10.0 %copy-start.3 = (s32[8]{0:T(128)S(1)}, s32[8]{0:T(128)}, u32[]{:S(2)}) copy-start(s32[8]{0:T(128)} %j_irrep.1) | copy-start | bytes 100
  26.1 6.0 %collective-permute-start.13 = (bf16[3,64,512]{2,1,0:T(8,128)(2,1)S(1)}, bf16[3,64,512]{2,1,0:T(8,128)(2,1)S(1)}, u32[]{:S(2)}, u32[]{:S(2)}) collective-permute-start(bf16[3,64,512]{2,1,0:T(8,128)(2,1)S(1)} %slice.23), channel_id=1, source_target_pairs={{0,2},{1,3},{2,0},{3,1},{4,6},{5,7},{6,4},{7,5},{8,10},{9,11},{10,... | collective-permute-start | bytes 589832 | tf_op jit(solution)/shard_map/ppermute | solution.py:189
  27.3 5.6 %collective-permute-start.12 = (bf16[3,64,512]{2,1,0:T(8,128)(2,1)S(1)}, bf16[3,64,512]{2,1,0:T(8,128)(2,1)S(1)}, u32[]{:S(2)}, u32[]{:S(2)}) collective-permute-start(bf16[3,64,512]{2,1,0:T(8,128)(2,1)S(1)} %slice.22), channel_id=1, source_target_pairs={{0,4},{1,5},{2,6},{3,7},{4,0},{5,1},{6,2},{7,3},{8,12},{9,13},{10,... | collective-permute-start | bytes 589832 | tf_op jit(solution)/shard_map/ppermute | solution.py:189
  33.0 3.1 %collective-permute-start.14 = (bf16[6,64,512]{2,1,0:T(8,128)(2,1)S(1)}, bf16[6,64,512]{2,1,0:T(8,128)(2,1)S(1)}, u32[]{:S(2)}, u32[]{:S(2)}) collective-permute-start(bf16[6,64,512]{2,1,0:T(8,128)(2,1)S(1)} %constant_dynamic-update-slice_fusion.2.refs_2_), channel_id=1, source_target_pairs={{0,1},{1,0},{2,3},{3,2},{4,5},{5,4},{6,7},{7,6},{8,9},{9,8},{10,11... | collective-permute-start | bytes 1179656 | tf_op jit(solution)/shard_map/ppermute | solution.py:189

commit v6 on v5

--- a/solution.py
+++ b/solution.py
@@ -133,7 +133,7 @@
             for i in range(2):
                 amp = side[:, k, i].reshape(width, width)
                 amps.append(jnp.where(live, amp, jnp.zeros((), amp.dtype)))
-            inter = jnp.concatenate([own[half * k_half + k], twin[half * k_half + k]], axis=0)
+            inter = jnp.concatenate([own[k], twin[k]], axis=0)
             term = lax.dot_general(
                 jnp.concatenate(amps, axis=1), inter, (((0,), (0,)), ((), ())), preferred_element_type=jnp.float32
             )
@@ -146,17 +146,19 @@
     m = n_place - 1
     own, twin, near, (far, total) = refs[:m], refs[m:2 * m], refs[2 * m:3 * m], refs[3 * m:]
     total[...] = jnp.zeros_like(total)
-    pieces = [(at, 0, near[at], own[at], twin[at]) for at in range(m)] + [(0, 1, far, own[0], twin[0])]
+    pieces = [(at, 0, near[at], own[at], twin[at]) for at in range(m)]
+    pieces.append((0, 1, far, own[0].at[pl.ds(k_half, k_half)], twin[0].at[pl.ds(k_half, k_half)]))
     add_terms(n_place, k_half, pieces, k_irrep, i_irrep, virt_count, total)
 
 
 def late_kernel(n_place, k_half, k_irrep, i_irrep, virt_count, j_irrep, *refs):
     m = n_place - 1
-    own, twin, (near, far, _, out_ref, total) = refs[:m], refs[m:2 * m], refs[2 * m:]
+    own, twin, (near, far, _, out_ref, total) = refs[:m + 1], refs[m + 1:2 * m + 2], refs[2 * m + 2:]
     n_irrep, width = total.shape[1:3]
     j_count = out_ref.shape[2]
-    pieces = [(at, 1, far.at[at - 1], own[at - 1], twin[at - 1]) for at in range(1, n_place)]
-    pieces.append((m, 0, near, own[m - 1], twin[m - 1]))
+    later = pl.ds(k_half, k_half)
+    pieces = [(at, 1, far.at[at - 1], own[at - 1].at[later], twin[at - 1].at[later]) for at in range(1, m)]
+    pieces += [(m, 0, near, own[m - 1], twin[m - 1]), (m, 1, far.at[m - 1], own[m], twin[m])]
     add_terms(n_place, k_half, pieces, k_irrep, i_irrep, virt_count, total)
     me_b, _, _, _, i_labels = device_labels(n_place, k_half, k_irrep, i_irrep)
     row = lax.broadcasted_iota(jnp.int32, (width, width), 0)
@@ -208,7 +210,6 @@
     other = over(away)
     near0, near1, near2, near3 = i_part(place), *(flip(i_part(place ^ m), 2 * m) for m in range(1, n_place))
     far0 = over(near0)
-    other, near1 = hold(other, near1)
     near1, near2, near3, far0 = hold(near1, near2, near3, far0)
     own0 = jnp.concatenate([mine, other])
     own1, own2, twin0 = flip(own0, 2), flip(own0, 4), flip(own0, 1)
@@ -231,9 +232,8 @@
         cost_estimate=cost,
     )(k_irrep, i_irrep, virt_count, *operands)
     far123, early, *own3 = hold(far123, early, *own3)
-    own3 = jnp.concatenate(own3)
-    twin3 = flip(own3, 1)
-    operands = [own1, own2, own3, twin1, twin2, twin3, near3, far123, early]
+    twin3 = [flip(x, 1) for x in own3]
+    operands = [own1, own2, *own3, twin1, twin2, *twin3, near3, far123, early]
     tile, _ = pl.pallas_call(
         functools.partial(late_kernel, n_place, k_half),
         in_specs=[scalars] * 4 + [here] * len(operands),

time: 92.2 us -> 92.1 us (level)
    ppermute x12 -> x13, starting transfers between devices: 12.2 us -> 11.5 us  [flip(): return lax.ppermute(x, 'grp', [(d, d ^ bits) for d in range(n_grp)])]
    ppermute x12 -> x13, waiting for transfers between devices: 14.2 us -> 14.9 us  [flip(): return lax.ppermute(x, 'grp', [(d, d ^ bits) for d in range(n_grp)])]
  transfers between devices with their start and end apart: 15 -> 16, of which waited for: 8 -> 9; matrix products, arithmetic and copies ran while one was open for 1% -> 1% of each run, Pallas kernels for 2% -> 2%
where the time goes in v6:
time: 92.1 us; the launch traced here: 91.9 us
  blocking collectives  52.7 us (57%)
  waiting for transfers between devices  16.3 us (18%)
  starting transfers between devices  15.8 us (17%)
  Pallas kernels  3.94 us (4%)
  local copies, waits for them, and re-layouts  1.53 us (2%)
  other arithmetic  1.44 us (2%)
    all_to_all x1, blocking collectives, shards_tiled(): lax.all_to_all(tile, 'grp', split_axis=0, concat_axis=0, tiled=True)  52.7 us
    ppermute x13, waiting for transfers between devices, flip(): return lax.ppermute(x, 'grp', [(d, d ^ bits) for d in range(n_grp)])  14.9 us
    ppermute x13, starting transfers between devices, flip(): return lax.ppermute(x, 'grp', [(d, d ^ bits) for d in range(n_grp)])  11.5 us
    ppermute x3, starting transfers between devices, over(): return lax.ppermute(x, 'batch', swap)  4.3 us
    pallas_call x1, Pallas kernels, shards_tiled(): pl.pallas_call(functools.partial(late_kernel, n_place, k_half), in_specs=...  2.08 us
    pallas_call x1, Pallas kernels, shards_tiled(): pl.pallas_call(functools.partial(early_kernel, n_place, k_half), in_specs...  1.87 us
  transfers between devices with their start and end apart: 16, of which 9 were waited for; matrix products, arithmetic and copies ran while one was open for 1% of the time, Pallas kernels for 2%

profile of v6, /device:TPU:1, one launch (start us, length us, event | category | flops | bytes accessed | tf_op | source)
XLA Modules:
  0.0 91.9 jit_solution(2788475608150836415)
XLA Ops:
  0.0 1.2 %constant_dynamic-slice_fusion = (bf16[3,4,1,2,64,128]{5,4,3,2,1,0:T(8,128)(2,1)S(1)}, bf16[3,4,1,2,64,128]{5,4,3,2,1,0:T(8,128)(2,1)S(1)}) fusion(bf16[3,4,2,2,64,128]{5,4,3,2,1,0:T(8,128)(2,1)} %bitcast.24, s32[]{:T(128)S(6)} %select_n.52, s32[]{:T(128)S(6)} %select_n.51), kind=kLoop, calls=%fused_computation.24 | loop fusion | bytes 1572872 | tf_op jit(solution)/shard_map/jit(dynamic_index_in_dim)/dynamic_slice | solution.py:204
  1.3 0.1 collective-permute-start.4
  1.4 0.2 broadcast_select_fusion
  1.6 0.1 reshape.17
  1.7 2.8 %collective-permute-start = (bf16[3,64,512]{2,1,0:T(8,128)(2,1)S(1)}, bf16[3,64,512]{2,1,0:T(8,128)(2,1)S(1)}, u32[]{:S(2)}, u32[]{:S(2)}) collective-permute-start(bf16[3,64,512]{2,1,0:T(8,128)(2,1)S(1)} %reshape.17), channel_id=1, source_target_pairs={{0,16},{16,0},{1,17},{17,1},{2,18},{18,2},{3,19},{19,3},{4,20},{20... | collective-permute-start | bytes 589832 | tf_op jit(solution)/shard_map/ppermute | solution.py:197
  4.5 0.1 reshape.16
  4.6 0.1 fusion.1
  4.7 1.3 %collective-permute-start.5 = (bf16[2,3,2,64,128]{4,3,2,1,0:T(8,128)(2,1)S(1)}, bf16[2,3,2,64,128]{4,3,2,1,0:T(8,128)(2,1)S(1)}, u32[]{:S(2)}, u32[]{:S(2)}) collective-permute-start(bf16[2,3,2,64,128]{4,3,2,1,0:T(8,128)(2,1)S(1)} %get-tuple-element.30), channel_id=1, source_target_pairs={{0,2},{1,3},{2,0},{3,1},{4,6},{5,7},{6,4},{7,5},{8,10},{9,11},{10,... | collective-permute-start | bytes 589832 | tf_op jit(solution)/shard_map/ppermute | solution.py:191
  6.0 1.3 %collective-permute-start.6 = (bf16[2,3,2,64,128]{4,3,2,1,0:T(8,128)(2,1)S(1)}, bf16[2,3,2,64,128]{4,3,2,1,0:T(8,128)(2,1)S(1)}, u32[]{:S(2)}, u32[]{:S(2)}) collective-permute-start(bf16[2,3,2,64,128]{4,3,2,1,0:T(8,128)(2,1)S(1)} %get-tuple-element.31), channel_id=1, source_target_pairs={{0,4},{1,5},{2,6},{3,7},{4,0},{5,1},{6,2},{7,3},{8,12},{9,13},{10,... | collective-permute-start | bytes 589832 | tf_op jit(solution)/shard_map/ppermute | solution.py:191
  7.3 0.2 collective-permute-start.7
  7.5 0.8 collective-permute-start.8
  8.3 1.4 %collective-permute-done = bf16[3,64,512]{2,1,0:T(8,128)(2,1)S(1)} collective-permute-done((bf16[3,64,512]{2,1,0:T(8,128)(2,1)S(1)}, bf16[3,64,512]{2,1,0:T(8,128)(2,1)S(1)}, u32[]{:S(2)}, u32[]{:S(2)}) %collective-permute-start) | collective-permute-done | bytes 196640 | tf_op jit(solution)/shard_map/ppermute | solution.py:197
  9.7 0.7 collective-permute-start.3
  10.4 0.6 collective-permute-done.5.refs_7_
  11.0 1.3 %collective-permute-start.2 = (bf16[6,64,512]{2,1,0:T(8,128)(2,1)S(1)}, bf16[6,64,512]{2,1,0:T(8,128)(2,1)S(1)}, u32[]{:S(2)}, u32[]{:S(2)}) collective-permute-start(bf16[6,64,512]{2,1,0:T(8,128)(2,1)S(1)} %constant_dynamic-update-slice_fusion.refs_0_), channel_id=1, source_target_pairs={{0,4},{1,5},{2,6},{3,7},{4,0},{5,1},{6,2},{7,3},{8,12},{9,13},{10,... | collective-permute-start | bytes 1179656 | tf_op jit(solution)/shard_map/ppermute | solution.py:191
  12.3 1.2 %collective-permute-start.1 = (bf16[6,64,512]{2,1,0:T(8,128)(2,1)S(1)}, bf16[6,64,512]{2,1,0:T(8,128)(2,1)S(1)}, u32[]{:S(2)}, u32[]{:S(2)}) collective-permute-start(bf16[6,64,512]{2,1,0:T(8,128)(2,1)S(1)} %constant_dynamic-update-slice_fusion.refs_0_), channel_id=1, source_target_pairs={{0,2},{1,3},{2,0},{3,1},{4,6},{5,7},{6,4},{7,5},{8,10},{9,11},{10,... | collective-permute-start | bytes 1179656 | tf_op jit(solution)/shard_map/ppermute | solution.py:191
  13.5 2.6 %collective-permute-done.7.refs_8_ = bf16[2,3,2,64,128]{4,3,2,1,0:T(8,128)(2,1)S(1)} collective-permute-done((bf16[2,3,2,64,128]{4,3,2,1,0:T(8,128)(2,1)S(1)}, bf16[2,3,2,64,128]{4,3,2,1,0:T(8,128)(2,1)S(1)}, u32[]{:S(2)}, u32[]{:S(2)}) %collective-permute-start.7) | collective-permute-done | bytes 196640 | tf_op jit(solution)/shard_map/ppermute | solution.py:191
  16.1 0.8 collective-permute-start.9
  16.9 7.6 %collective-permute-done.2.refs_2_.refs_1_ = bf16[6,64,512]{2,1,0:T(8,128)(2,1)S(1)} collective-permute-done((bf16[6,64,512]{2,1,0:T(8,128)(2,1)S(1)}, bf16[6,64,512]{2,1,0:T(8,128)(2,1)S(1)}, u32[]{:S(2)}, u32[]{:S(2)}) %collective-permute-start.2) | collective-permute-done | bytes 393248 | tf_op jit(solution)/shard_map/ppermute | solution.py:191
  24.5 0.2 collective-permute-done.1.refs_1_.refs_0_
  24.7 1.2 %collective-permute-start.10 = (bf16[6,64,512]{2,1,0:T(8,128)(2,1)S(1)}, bf16[6,64,512]{2,1,0:T(8,128)(2,1)S(1)}, u32[]{:S(2)}, u32[]{:S(2)}) collective-permute-start(bf16[6,64,512]{2,1,0:T(8,128)(2,1)S(1)} %collective-permute-done.1.refs_1_.refs_0_), channel_id=1, source_target_pairs={{0,1},{1,0},{2,3},{3,2},{4,5},{5,4},{6,7},{7,6},{8,9},{9,8},{10,11... | collective-permute-start | bytes 1179656 | tf_op jit(solution)/shard_map/ppermute | solution.py:191
  26.0 1.2 %collective-permute-start.13 = (bf16[3,64,512]{2,1,0:T(8,128)(2,1)S(1)}, bf16[3,64,512]{2,1,0:T(8,128)(2,1)S(1)}, u32[]{:S(2)}, u32[]{:S(2)}) collective-permute-start(bf16[3,64,512]{2,1,0:T(8,128)(2,1)S(1)} %slice.23), channel_id=1, source_target_pairs={{0,2},{1,3},{2,0},{3,1},{4,6},{5,7},{6,4},{7,5},{8,10},{9,11},{10,... | collective-permute-start | bytes 589832 | tf_op jit(solution)/shard_map/ppermute | solution.py:191
  27.3 1.2 %collective-permute-start.12 = (bf16[3,64,512]{2,1,0:T(8,128)(2,1)S(1)}, bf16[3,64,512]{2,1,0:T(8,128)(2,1)S(1)}, u32[]{:S(2)}, u32[]{:S(2)}) collective-permute-start(bf16[3,64,512]{2,1,0:T(8,128)(2,1)S(1)} %slice.22), channel_id=1, source_target_pairs={{0,4},{1,5},{2,6},{3,7},{4,0},{5,1},{6,2},{7,3},{8,12},{9,13},{10,... | collective-permute-start | bytes 589832 | tf_op jit(solution)/shard_map/ppermute | solution.py:191
  28.6 1.9 %shard_map.64.refs_10_ = f32[2,8,128,512]{3,2,1,0:T(8,128)S(1)} custom-call(s32[6]{0:T(128)S(1)} %copy-done, s32[16]{0:T(128)S(1)} %copy-done.1, s32[8]{0:T(128)S(1)} %copy-done.2, bf16[6,64,512]{2,1,0:T(8,128)(2,1)S(1)} %constant_dynamic-update-slice_fusion.refs_0_, bf16[6,64,512]{2,1,0:T(8,128)(2,1)S(1)} %collective-permute-done.1.refs_1_.refs_0_, ...), custom_call_target="tpu_custom_call" | custom-call | flops 402653184 | bytes 1048576 | tf_op jit(solution)/shard_map/pallas_call | solution.py:226
  30.4 1.6 %collective-permute-done.13.refs_3_ = bf16[3,64,512]{2,1,0:T(8,128)(2,1)S(1)} collective-permute-done((bf16[3,64,512]{2,1,0:T(8,128)(2,1)S(1)}, bf16[3,64,512]{2,1,0:T(8,128)(2,1)S(1)}, u32[]{:S(2)}, u32[]{:S(2)}) %collective-permute-start.13) | collective-permute-done | bytes 196640 | tf_op jit(solution)/shard_map/ppermute | solution.py:191
  32.1 0.9 collective-permute-done.12.refs_2_
  32.9 1.7 %collective-permute-start.14 = (bf16[3,64,512]{2,1,0:T(8,128)(2,1)S(1)}, bf16[3,64,512]{2,1,0:T(8,128)(2,1)S(1)}, u32[]{:S(2)}, u32[]{:S(2)}) collective-permute-start(bf16[3,64,512]{2,1,0:T(8,128)(2,1)S(1)} %collective-permute-done.12.refs_2_), channel_id=1, source_target_pairs={{0,1},{1,0},{2,3},{3,2},{4,5},{5,4},{6,7},{7,6},{8,9},{9,8},{10,11... | collective-permute-start | bytes 589832 | tf_op jit(solution)/shard_map/ppermute | solution.py:191
  34.6 1.1 %collective-permute-done.14.refs_6_ = bf16[3,64,512]{2,1,0:T(8,128)(2,1)S(1)} collective-permute-done((bf16[3,64,512]{2,1,0:T(8,128)(2,1)S(1)}, bf16[3,64,512]{2,1,0:T(8,128)(2,1)S(1)}, u32[]{:S(2)}, u32[]{:S(2)}) %collective-permute-start.14) | collective-permute-done | bytes 196640 | tf_op jit(solution)/shard_map/ppermute | solution.py:191
  35.7 0.4 collective-permute-done.15.refs_7_
  36.0 2.1 %shard_map.65 = (bf16[16,2,4,64,128]{4,3,2,1,0:T(8,128)(2,1)S(1)}, f32[2,8,128,512]{3,2,1,0:T(8,128)S(1)}) custom-call(s32[6]{0:T(128)S(1)} %copy-done, s32[16]{0:T(128)S(1)} %copy-done.1, s32[8]{0:T(128)S(1)} %copy-done.2, s32[8]{0:T(128)S(1)} %copy-done.3, ...), custom_call_target="tpu_custom_call", output_to_operand_aliasing={{1}: (14, {})} | custom-call | flops 402653184 | bytes 1048576 | tf_op jit(solution)/shard_map/pallas_call | solution.py:237
  38.1 52.7 %all_to_all.5 = bf16[16,2,4,64,128]{4,3,2,1,0:T(8,128)(2,1)S(1)} all-to-all(bf16[16,2,4,64,128]{4,3,2,1,0:T(8,128)(2,1)S(1)} %get-tuple-element.28), channel_id=1, replica_groups=mesh['batch'=2,'grp'=16] {'grp'}, dimensions={0} | all-to-all | bytes 4194304 | tf_op jit(solution)/shard_map/all_to_all | solution.py:246
  90.8 1.1 %slice_add_fusion = bf16[8,2,4,64,128]{4,3,2,1,0:T(8,128)(2,1)} fusion(bf16[16,2,4,64,128]{4,3,2,1,0:T(8,128)(2,1)S(1)} %all_to_all.5), kind=kLoop, calls=%fused_computation.8 | loop fusion | flops 524288 | bytes 3145728 | tf_op jit(solution)/shard_map/add | solution.py:248
  (26 shorter events, 0.2 us)
Async XLA Ops:
  0.0 1.4 %copy-start.4 = (bf16[3,64,8,128]{3,2,1,0:T(8,128)(2,1)S(1)}, bf16[3,64,8,128]{3,2,1,0:T(8,128)(2,1)}, u32[]{:S(2)}) copy-start(bf16[3,64,8,128]{3,2,1,0:T(8,128)(2,1)} %param.7) | copy-start | bytes 1179652
  1.3 3.3 %collective-permute-start.4 = (bf16[3,4,2,64,128]{4,3,2,0,1:T(8,128)(2,1)S(1)}, bf16[3,4,2,64,128]{4,3,2,0,1:T(8,128)(2,1)S(1)}, u32[]{:S(2)}, u32[]{:S(2)}) collective-permute-start(bf16[3,4,2,64,128]{4,3,2,0,1:T(8,128)(2,1)S(1)} %bitcast.25), channel_id=1, source_target_pairs={{0,1},{1,0},{2,3},{3,2},{4,5},{5,4},{6,7},{7,6},{8,9},{9,8},{10,11... | collective-permute-start | bytes 1179656 | tf_op jit(solution)/shard_map/ppermute | solution.py:191
  1.7 8.0 %collective-permute-start = (bf16[3,64,512]{2,1,0:T(8,128)(2,1)S(1)}, bf16[3,64,512]{2,1,0:T(8,128)(2,1)S(1)}, u32[]{:S(2)}, u32[]{:S(2)}) collective-permute-start(bf16[3,64,512]{2,1,0:T(8,128)(2,1)S(1)} %reshape.17), channel_id=1, source_target_pairs={{0,16},{16,0},{1,17},{17,1},{2,18},{18,2},{3,19},{19,3},{4,20},{20... | collective-permute-start | bytes 589832 | tf_op jit(solution)/shard_map/ppermute | solution.py:197
  4.6 23.9 %copy-start = (s32[6]{0:T(128)S(1)}, s32[6]{0:T(128)}, u32[]{:S(2)}) copy-start(s32[6]{0:T(128)} %k_irrep.3) | copy-start | bytes 76
  4.6 23.9 %copy-start.1 = (s32[16]{0:T(128)S(1)}, s32[16]{0:T(128)}, u32[]{:S(2)}) copy-start(s32[16]{0:T(128)} %i_irrep.3) | copy-start | bytes 196
  4.6 23.9 %copy-start.2 = (s32[8]{0:T(128)S(1)}, s32[8]{0:T(128)}, u32[]{:S(2)}) copy-start(s32[8]{0:T(128)} %virt_count.3) | copy-start | bytes 100
  4.7 6.2 %collective-permute-start.5 = (bf16[2,3,2,64,128]{4,3,2,1,0:T(8,128)(2,1)S(1)}, bf16[2,3,2,64,128]{4,3,2,1,0:T(8,128)(2,1)S(1)}, u32[]{:S(2)}, u32[]{:S(2)}) collective-permute-start(bf16[2,3,2,64,128]{4,3,2,1,0:T(8,128)(2,1)S(1)} %get-tuple-element.30), channel_id=1, source_target_pairs={{0,2},{1,3},{2,0},{3,1},{4,6},{5,7},{6,4},{7,5},{8,10},{9,11},{10,... | collective-permute-start | bytes 589832 | tf_op jit(solution)/shard_map/ppermute | solution.py:191
  6.0 6.3 %collective-permute-start.6 = (bf16[2,3,2,64,128]{4,3,2,1,0:T(8,128)(2,1)S(1)}, bf16[2,3,2,64,128]{4,3,2,1,0:T(8,128)(2,1)S(1)}, u32[]{:S(2)}, u32[]{:S(2)}) collective-permute-start(bf16[2,3,2,64,128]{4,3,2,1,0:T(8,128)(2,1)S(1)} %get-tuple-element.31), channel_id=1, source_target_pairs={{0,4},{1,5},{2,6},{3,7},{4,0},{5,1},{6,2},{7,3},{8,12},{9,13},{10,... | collective-permute-start | bytes 589832 | tf_op jit(solution)/shard_map/ppermute | solution.py:191
  7.3 8.7 %collective-permute-start.7 = (bf16[2,3,2,64,128]{4,3,2,1,0:T(8,128)(2,1)S(1)}, bf16[2,3,2,64,128]{4,3,2,1,0:T(8,128)(2,1)S(1)}, u32[]{:S(2)}, u32[]{:S(2)}) collective-permute-start(bf16[2,3,2,64,128]{4,3,2,1,0:T(8,128)(2,1)S(1)} %get-tuple-element.32), channel_id=1, source_target_pairs={{0,6},{1,7},{2,4},{3,5},{4,2},{5,3},{6,0},{7,1},{8,14},{9,15},{10,... | collective-permute-start | bytes 589832 | tf_op jit(solution)/shard_map/ppermute | solution.py:191
  7.5 8.5 %collective-permute-start.8 = (bf16[2,3,2,64,128]{4,3,2,1,0:T(8,128)(2,1)S(1)}, bf16[2,3,2,64,128]{4,3,2,1,0:T(8,128)(2,1)S(1)}, u32[]{:S(2)}, u32[]{:S(2)}) collective-permute-start(bf16[2,3,2,64,128]{4,3,2,1,0:T(8,128)(2,1)S(1)} %get-tuple-element.29.refs_6_), channel_id=1, source_target_pairs={{0,16},{16,0},{1,17},{17,1},{2,18},{18,2},{3,19},{19,3},{4,20},{20... | collective-permute-start | bytes 589832 | tf_op jit(solution)/shard_map/ppermute | solution.py:197
  9.7 7.2 %collective-permute-start.3 = (bf16[6,64,512]{2,1,0:T(8,128)(2,1)S(1)}, bf16[6,64,512]{2,1,0:T(8,128)(2,1)S(1)}, u32[]{:S(2)}, u32[]{:S(2)}) collective-permute-start(bf16[6,64,512]{2,1,0:T(8,128)(2,1)S(1)} %constant_dynamic-update-slice_fusion.refs_0_), channel_id=1, source_target_pairs={{0,1},{1,0},{2,3},{3,2},{4,5},{5,4},{6,7},{7,6},{8,9},{9,8},{10,11... | collective-permute-start | bytes 1179656 | tf_op jit(solution)/shard_map/ppermute | solution.py:191
  11.0 13.5 %collective-permute-start.2 = (bf16[6,64,512]{2,1,0:T(8,128)(2,1)S(1)}, bf16[6,64,512]{2,1,0:T(8,128)(2,1)S(1)}, u32[]{:S(2)}, u32[]{:S(2)}) collective-permute-start(bf16[6,64,512]{2,1,0:T(8,128)(2,1)S(1)} %constant_dynamic-update-slice_fusion.refs_0_), channel_id=1, source_target_pairs={{0,4},{1,5},{2,6},{3,7},{4,0},{5,1},{6,2},{7,3},{8,12},{9,13},{10,... | collective-permute-start | bytes 1179656 | tf_op jit(solution)/shard_map/ppermute | solution.py:191
  12.3 12.5 %collective-permute-start.1 = (bf16[6,64,512]{2,1,0:T(8,128)(2,1)S(1)}, bf16[6,64,512]{2,1,0:T(8,128)(2,1)S(1)}, u32[]{:S(2)}, u32[]{:S(2)}) collective-permute-start(bf16[6,64,512]{2,1,0:T(8,128)(2,1)S(1)} %constant_dynamic-update-slice_fusion.refs_0_), channel_id=1, source_target_pairs={{0,2},{1,3},{2,0},{3,1},{4,6},{5,7},{6,4},{7,5},{8,10},{9,11},{10,... | collective-permute-start | bytes 1179656 | tf_op jit(solution)/shard_map/ppermute | solution.py:191
  16.1 16.8 %collective-permute-start.9 = (bf16[3,2,3,2,64,128]{5,4,3,2,1,0:T(8,128)(2,1)S(1)}, bf16[3,2,3,2,64,128]{5,4,3,2,1,0:T(8,128)(2,1)S(1)}, u32[]{:S(2)}, u32[]{:S(2)}) collective-permute-start(bf16[3,2,3,2,64,128]{5,4,3,2,1,0:T(8,128)(2,1)S(1)} %pad_maximum_fusion), channel_id=1, source_target_pairs={{0,16},{16,0},{1,17},{17,1},{2,18},{18,2},{3,19},{19,3},{4,20},{20... | collective-permute-start | bytes 1769480 | tf_op jit(solution)/shard_map/ppermute | solution.py:197
  24.7 3.8 %collective-permute-start.10 = (bf16[6,64,512]{2,1,0:T(8,128)(2,1)S(1)}, bf16[6,64,512]{2,1,0:T(8,128)(2,1)S(1)}, u32[]{:S(2)}, u32[]{:S(2)}) collective-permute-start(bf16[6,64,512]{2,1,0:T(8,128)(2,1)S(1)} %collective-permute-done.1.refs_1_.refs_0_), channel_id=1, source_target_pairs={{0,1},{1,0},{2,3},{3,2},{4,5},{5,4},{6,7},{7,6},{8,9},{9,8},{10,11... | collective-permute-start | bytes 1179656 | tf_op jit(solution)/shard_map/ppermute | solution.py:191
  26.0 2.6 %collective-permute-start.11 = (bf16[6,64,512]{2,1,0:T(8,128)(2,1)S(1)}, bf16[6,64,512]{2,1,0:T(8,128)(2,1)S(1)}, u32[]{:S(2)}, u32[]{:S(2)}) collective-permute-start(bf16[6,64,512]{2,1,0:T(8,128)(2,1)S(1)} %collective-permute-done.2.refs_2_.refs_1_), channel_id=1, source_target_pairs={{0,1},{1,0},{2,3},{3,2},{4,5},{5,4},{6,7},{7,6},{8,9},{9,8},{10,11... | collective-permute-start | bytes 1179656 | tf_op jit(solution)/shard_map/ppermute | solution.py:191
  26.0 10.0 %copy-start.3 = (s32[8]{0:T(128)S(1)}, s32[8]{0:T(128)}, u32[]{:S(2)}) copy-start(s32[8]{0:T(128)} %j_irrep.1) | copy-start | bytes 100
  26.0 6.0 %collective-permute-start.13 = (bf16[3,64,512]{2,1,0:T(8,128)(2,1)S(1)}, bf16[3,64,512]{2,1,0:T(8,128)(2,1)S(1)}, u32[]{:S(2)}, u32[]{:S(2)}) collective-permute-start(bf16[3,64,512]{2,1,0:T(8,128)(2,1)S(1)} %slice.23), channel_id=1, source_target_pairs={{0,2},{1,3},{2,0},{3,1},{4,6},{5,7},{6,4},{7,5},{8,10},{9,11},{10,... | collective-permute-start | bytes 589832 | tf_op jit(solution)/shard_map/ppermute | solution.py:191
  27.3 5.6 %collective-permute-start.12 = (bf16[3,64,512]{2,1,0:T(8,128)(2,1)S(1)}, bf16[3,64,512]{2,1,0:T(8,128)(2,1)S(1)}, u32[]{:S(2)}, u32[]{:S(2)}) collective-permute-start(bf16[3,64,512]{2,1,0:T(8,128)(2,1)S(1)} %slice.22), channel_id=1, source_target_pairs={{0,4},{1,5},{2,6},{3,7},{4,0},{5,1},{6,2},{7,3},{8,12},{9,13},{10,... | collective-permute-start | bytes 589832 | tf_op jit(solution)/shard_map/ppermute | solution.py:191
  32.9 2.8 %collective-permute-start.14 = (bf16[3,64,512]{2,1,0:T(8,128)(2,1)S(1)}, bf16[3,64,512]{2,1,0:T(8,128)(2,1)S(1)}, u32[]{:S(2)}, u32[]{:S(2)}) collective-permute-start(bf16[3,64,512]{2,1,0:T(8,128)(2,1)S(1)} %collective-permute-done.12.refs_2_), channel_id=1, source_target_pairs={{0,1},{1,0},{2,3},{3,2},{4,5},{5,4},{6,7},{7,6},{8,9},{9,8},{10,11... | collective-permute-start | bytes 589832 | tf_op jit(solution)/shard_map/ppermute | solution.py:191
  34.6 1.4 %collective-permute-start.15 = (bf16[3,64,512]{2,1,0:T(8,128)(2,1)S(1)}, bf16[3,64,512]{2,1,0:T(8,128)(2,1)S(1)}, u32[]{:S(2)}, u32[]{:S(2)}) collective-permute-start(bf16[3,64,512]{2,1,0:T(8,128)(2,1)S(1)} %collective-permute-done.13.refs_3_), channel_id=1, source_target_pairs={{0,1},{1,0},{2,3},{3,2},{4,5},{5,4},{6,7},{7,6},{8,9},{9,8},{10,11... | collective-permute-start | bytes 589832 | tf_op jit(solution)/shard_map/ppermute | solution.py:191

commit v7 on v6

--- a/solution.py
+++ b/solution.py
@@ -200,8 +200,9 @@
     mine = jnp.where(me_b == 0, low, high).reshape(k_half, slab, j_count * width)
     away = jnp.where(me_b == 0, high, low).reshape(k_half, slab, j_count * width)
     parts = amps.reshape(k_half, n_place, 2, 2, slab, width)
+    take = flip(lax.dynamic_index_in_dim(parts, 1 - core, 2, keepdims=False), 1)
+    parts, away = hold(parts, away)
     keep = lax.dynamic_index_in_dim(parts, core, 2, keepdims=False)
-    take = flip(lax.dynamic_index_in_dim(parts, 1 - core, 2, keepdims=False), 1)
     i_parts = jnp.stack([keep, take])
 
     def i_part(at):

time: 92.1 us -> 93.1 us (1.011)
  other arithmetic: 1.44 us -> 2.57 us
    dynamic_slice x3 -> x0, local copies, waits for them, and re-layouts: 1.28 us -> none  [the longest x2 1.26 us: shards_tiled(): take = flip(lax.dynamic_index_in_dim(parts, 1 - core, 2, keepdims=False), 1)]
    unnamed x11, local copies, waits for them, and re-layouts: 0.04 us -> 1.17 us
    select_n x1, other arithmetic: 0.22 us -> 1.34 us  [shards_tiled(): jnp.where(me_b == 0, high, low).reshape(k_half, slab, j_count * width)]
  transfers between devices with their start and end apart: 16 -> 16, of which waited for: 9 -> 9; matrix products, arithmetic and copies ran while one was open for 1% -> 2% of each run, Pallas kernels for 2% -> 2%
where the time goes in v7:
time: 93.1 us; the launch traced here: 92.9 us
  blocking collectives  52.7 us (57%)
  waiting for transfers between devices  17.2 us (18%)
  starting transfers between devices  14.9 us (16%)
  Pallas kernels  3.94 us (4%)
  other arithmetic  2.57 us (3%)
  local copies, waits for them, and re-layouts  1.43 us (2%)
    all_to_all x1, blocking collectives, shards_tiled(): lax.all_to_all(tile, 'grp', split_axis=0, concat_axis=0, tiled=True)  52.7 us
    ppermute x13, waiting for transfers between devices, flip(): return lax.ppermute(x, 'grp', [(d, d ^ bits) for d in range(n_grp)])  15.2 us
    ppermute x13, starting transfers between devices, flip(): return lax.ppermute(x, 'grp', [(d, d ^ bits) for d in range(n_grp)])  11.5 us
    ppermute x3, starting transfers between devices, over(): return lax.ppermute(x, 'batch', swap)  3.37 us
    pallas_call x1, Pallas kernels, shards_tiled(): pl.pallas_call(functools.partial(late_kernel, n_place, k_half), in_specs=...  2.08 us
    ppermute x3, waiting for transfers between devices, over(): return lax.ppermute(x, 'batch', swap)  2.01 us
    pallas_call x1, Pallas kernels, shards_tiled(): pl.pallas_call(functools.partial(early_kernel, n_place, k_half), in_specs...  1.86 us
  transfers between devices with their start and end apart: 16, of which 9 were waited for; matrix products, arithmetic and copies ran while one was open for 2% of the time, Pallas kernels for 2%

profile of v7, /device:TPU:1, one launch (start us, length us, event | category | flops | bytes accessed | tf_op | source)
XLA Modules:
  0.0 92.9 jit_solution(2816175015959489622)
XLA Ops:
  0.0 1.1 %copy-done = bf16[3,16,64,128]{3,2,1,0:T(8,128)(2,1)S(1)} copy-done((bf16[3,16,64,128]{3,2,1,0:T(8,128)(2,1)S(1)}, bf16[3,16,64,128]{3,2,1,0:T(8,128)(2,1)}, u32[]{:S(2)}) %copy-start) | copy-done | bytes 786456
  1.2 0.1 collective-permute-start.4
  1.3 1.3 %broadcast_select_fusion = (bf16[3,64,4,128]{3,2,1,0:T(4,128)(2,1)S(1)}, bf16[3,64,4,128]{3,2,1,0:T(4,128)(2,1)S(1)}) fusion(pred[]{:T(512)S(6)} %eq.7, bf16[3,64,8,128]{3,2,1,0:T(8,128)(2,1)} %param.7), kind=kLoop, calls=%fused_computation.20 | loop fusion | flops 196608 | bytes 786433 | tf_op jit(solution)/shard_map/jit(_where)/select_n | solution.py:201
  2.6 0.1 reshape.18
  2.7 2.8 %collective-permute-start = (bf16[3,64,512]{2,1,0:T(8,128)(2,1)S(1)}, bf16[3,64,512]{2,1,0:T(8,128)(2,1)S(1)}, u32[]{:S(2)}, u32[]{:S(2)}) collective-permute-start(bf16[3,64,512]{2,1,0:T(8,128)(2,1)S(1)} %reshape.18), channel_id=1, source_target_pairs={{0,16},{16,0},{1,17},{17,1},{2,18},{18,2},{3,19},{19,3},{4,20},{20... | collective-permute-start | bytes 589832 | tf_op jit(solution)/shard_map/ppermute | solution.py:197
  5.5 0.1 reshape.16
  5.7 0.1 fusion.1
  5.8 1.3 %collective-permute-start.5 = (bf16[2,3,2,64,128]{4,3,2,1,0:T(8,128)(2,1)S(1)}, bf16[2,3,2,64,128]{4,3,2,1,0:T(8,128)(2,1)S(1)}, u32[]{:S(2)}, u32[]{:S(2)}) collective-permute-start(bf16[2,3,2,64,128]{4,3,2,1,0:T(8,128)(2,1)S(1)} %get-tuple-element.34), channel_id=1, source_target_pairs={{0,2},{1,3},{2,0},{3,1},{4,6},{5,7},{6,4},{7,5},{8,10},{9,11},{10,... | collective-permute-start | bytes 589832 | tf_op jit(solution)/shard_map/ppermute | solution.py:191
  7.0 1.3 %collective-permute-start.6 = (bf16[2,3,2,64,128]{4,3,2,1,0:T(8,128)(2,1)S(1)}, bf16[2,3,2,64,128]{4,3,2,1,0:T(8,128)(2,1)S(1)}, u32[]{:S(2)}, u32[]{:S(2)}) collective-permute-start(bf16[2,3,2,64,128]{4,3,2,1,0:T(8,128)(2,1)S(1)} %get-tuple-element.35), channel_id=1, source_target_pairs={{0,4},{1,5},{2,6},{3,7},{4,0},{5,1},{6,2},{7,3},{8,12},{9,13},{10,... | collective-permute-start | bytes 589832 | tf_op jit(solution)/shard_map/ppermute | solution.py:191
  8.4 0.2 collective-permute-start.7
  8.6 0.2 collective-permute-start.8
  8.7 2.0 %collective-permute-done = bf16[3,64,512]{2,1,0:T(8,128)(2,1)S(1)} collective-permute-done((bf16[3,64,512]{2,1,0:T(8,128)(2,1)S(1)}, bf16[3,64,512]{2,1,0:T(8,128)(2,1)S(1)}, u32[]{:S(2)}, u32[]{:S(2)}) %collective-permute-start) | collective-permute-done | bytes 196640 | tf_op jit(solution)/shard_map/ppermute | solution.py:197
  10.7 0.7 collective-permute-start.3
  11.4 0.6 collective-permute-done.5.refs_7_
  12.0 1.3 %collective-permute-start.2 = (bf16[6,64,512]{2,1,0:T(8,128)(2,1)S(1)}, bf16[6,64,512]{2,1,0:T(8,128)(2,1)S(1)}, u32[]{:S(2)}, u32[]{:S(2)}) collective-permute-start(bf16[6,64,512]{2,1,0:T(8,128)(2,1)S(1)} %constant_dynamic-update-slice_fusion.refs_0_), channel_id=1, source_target_pairs={{0,4},{1,5},{2,6},{3,7},{4,0},{5,1},{6,2},{7,3},{8,12},{9,13},{10,... | collective-permute-start | bytes 1179656 | tf_op jit(solution)/shard_map/ppermute | solution.py:191
  13.3 1.2 %collective-permute-start.1 = (bf16[6,64,512]{2,1,0:T(8,128)(2,1)S(1)}, bf16[6,64,512]{2,1,0:T(8,128)(2,1)S(1)}, u32[]{:S(2)}, u32[]{:S(2)}) collective-permute-start(bf16[6,64,512]{2,1,0:T(8,128)(2,1)S(1)} %constant_dynamic-update-slice_fusion.refs_0_), channel_id=1, source_target_pairs={{0,2},{1,3},{2,0},{3,1},{4,6},{5,7},{6,4},{7,5},{8,10},{9,11},{10,... | collective-permute-start | bytes 1179656 | tf_op jit(solution)/shard_map/ppermute | solution.py:191
  14.5 2.6 %collective-permute-done.7.refs_8_ = bf16[2,3,2,64,128]{4,3,2,1,0:T(8,128)(2,1)S(1)} collective-permute-done((bf16[2,3,2,64,128]{4,3,2,1,0:T(8,128)(2,1)S(1)}, bf16[2,3,2,64,128]{4,3,2,1,0:T(8,128)(2,1)S(1)}, u32[]{:S(2)}, u32[]{:S(2)}) %collective-permute-start.7) | collective-permute-done | bytes 196640 | tf_op jit(solution)/shard_map/ppermute | solution.py:191
  17.2 0.5 collective-permute-start.9
  17.6 7.9 %collective-permute-done.2.refs_2_.refs_1_ = bf16[6,64,512]{2,1,0:T(8,128)(2,1)S(1)} collective-permute-done((bf16[6,64,512]{2,1,0:T(8,128)(2,1)S(1)}, bf16[6,64,512]{2,1,0:T(8,128)(2,1)S(1)}, u32[]{:S(2)}, u32[]{:S(2)}) %collective-permute-start.2) | collective-permute-done | bytes 393248 | tf_op jit(solution)/shard_map/ppermute | solution.py:191
  25.6 0.2 collective-permute-done.1.refs_1_.refs_0_
  25.8 1.2 %collective-permute-start.10 = (bf16[6,64,512]{2,1,0:T(8,128)(2,1)S(1)}, bf16[6,64,512]{2,1,0:T(8,128)(2,1)S(1)}, u32[]{:S(2)}, u32[]{:S(2)}) collective-permute-start(bf16[6,64,512]{2,1,0:T(8,128)(2,1)S(1)} %collective-permute-done.1.refs_1_.refs_0_), channel_id=1, source_target_pairs={{0,1},{1,0},{2,3},{3,2},{4,5},{5,4},{6,7},{7,6},{8,9},{9,8},{10,11... | collective-permute-start | bytes 1179656 | tf_op jit(solution)/shard_map/ppermute | solution.py:191
  27.1 1.2 %collective-permute-start.13 = (bf16[3,64,512]{2,1,0:T(8,128)(2,1)S(1)}, bf16[3,64,512]{2,1,0:T(8,128)(2,1)S(1)}, u32[]{:S(2)}, u32[]{:S(2)}) collective-permute-start(bf16[3,64,512]{2,1,0:T(8,128)(2,1)S(1)} %slice.23), channel_id=1, source_target_pairs={{0,2},{1,3},{2,0},{3,1},{4,6},{5,7},{6,4},{7,5},{8,10},{9,11},{10,... | collective-permute-start | bytes 589832 | tf_op jit(solution)/shard_map/ppermute | solution.py:191
  28.3 1.3 %collective-permute-start.12 = (bf16[3,64,512]{2,1,0:T(8,128)(2,1)S(1)}, bf16[3,64,512]{2,1,0:T(8,128)(2,1)S(1)}, u32[]{:S(2)}, u32[]{:S(2)}) collective-permute-start(bf16[3,64,512]{2,1,0:T(8,128)(2,1)S(1)} %slice.22), channel_id=1, source_target_pairs={{0,4},{1,5},{2,6},{3,7},{4,0},{5,1},{6,2},{7,3},{8,12},{9,13},{10,... | collective-permute-start | bytes 589832 | tf_op jit(solution)/shard_map/ppermute | solution.py:191
  29.6 1.9 %shard_map.64.refs_10_ = f32[2,8,128,512]{3,2,1,0:T(8,128)S(1)} custom-call(s32[6]{0:T(128)S(1)} %copy-done.1, s32[16]{0:T(128)S(1)} %copy-done.2, s32[8]{0:T(128)S(1)} %copy-done.3, bf16[6,64,512]{2,1,0:T(8,128)(2,1)S(1)} %constant_dynamic-update-slice_fusion.refs_0_, bf16[6,64,512]{2,1,0:T(8,128)(2,1)S(1)} %collective-permute-done.1.refs_1_.refs_0_, ...), custom_call_target="tpu_custom_call" | custom-call | flops 402653184 | bytes 1048576 | tf_op jit(solution)/shard_map/pallas_call | solution.py:227
  31.5 1.6 %collective-permute-done.13.refs_3_ = bf16[3,64,512]{2,1,0:T(8,128)(2,1)S(1)} collective-permute-done((bf16[3,64,512]{2,1,0:T(8,128)(2,1)S(1)}, bf16[3,64,512]{2,1,0:T(8,128)(2,1)S(1)}, u32[]{:S(2)}, u32[]{:S(2)}) %collective-permute-start.13) | collective-permute-done | bytes 196640 | tf_op jit(solution)/shard_map/ppermute | solution.py:191
  33.1 0.9 collective-permute-done.12.refs_2_
  33.9 1.7 %collective-permute-start.14 = (bf16[3,64,512]{2,1,0:T(8,128)(2,1)S(1)}, bf16[3,64,512]{2,1,0:T(8,128)(2,1)S(1)}, u32[]{:S(2)}, u32[]{:S(2)}) collective-permute-start(bf16[3,64,512]{2,1,0:T(8,128)(2,1)S(1)} %collective-permute-done.12.refs_2_), channel_id=1, source_target_pairs={{0,1},{1,0},{2,3},{3,2},{4,5},{5,4},{6,7},{7,6},{8,9},{9,8},{10,11... | collective-permute-start | bytes 589832 | tf_op jit(solution)/shard_map/ppermute | solution.py:191
  35.6 1.1 %collective-permute-done.14.refs_6_ = bf16[3,64,512]{2,1,0:T(8,128)(2,1)S(1)} collective-permute-done((bf16[3,64,512]{2,1,0:T(8,128)(2,1)S(1)}, bf16[3,64,512]{2,1,0:T(8,128)(2,1)S(1)}, u32[]{:S(2)}, u32[]{:S(2)}) %collective-permute-start.14) | collective-permute-done | bytes 196640 | tf_op jit(solution)/shard_map/ppermute | solution.py:191
  36.7 0.4 collective-permute-done.15.refs_7_
  37.1 2.1 %shard_map.65 = (bf16[16,2,4,64,128]{4,3,2,1,0:T(8,128)(2,1)S(1)}, f32[2,8,128,512]{3,2,1,0:T(8,128)S(1)}) custom-call(s32[6]{0:T(128)S(1)} %copy-done.1, s32[16]{0:T(128)S(1)} %copy-done.2, s32[8]{0:T(128)S(1)} %copy-done.3, s32[8]{0:T(128)S(1)} %copy-done.4, ...), custom_call_target="tpu_custom_call", output_to_operand_aliasing={{1}: (14, {})} | custom-call | flops 402653184 | bytes 1048576 | tf_op jit(solution)/shard_map/pallas_call | solution.py:238
  39.2 52.7 %all_to_all.5 = bf16[16,2,4,64,128]{4,3,2,1,0:T(8,128)(2,1)S(1)} all-to-all(bf16[16,2,4,64,128]{4,3,2,1,0:T(8,128)(2,1)S(1)} %get-tuple-element.32), channel_id=1, replica_groups=mesh['batch'=2,'grp'=16] {'grp'}, dimensions={0} | all-to-all | bytes 4194304 | tf_op jit(solution)/shard_map/all_to_all | solution.py:247
  91.9 1.1 %slice_add_fusion = bf16[8,2,4,64,128]{4,3,2,1,0:T(8,128)(2,1)} fusion(bf16[16,2,4,64,128]{4,3,2,1,0:T(8,128)(2,1)S(1)} %all_to_all.5), kind=kLoop, calls=%fused_computation.8 | loop fusion | flops 524288 | bytes 3145728 | tf_op jit(solution)/shard_map/add | solution.py:249
  (25 shorter events, 0.2 us)
Async XLA Ops:
  0.0 1.1 %copy-start = (bf16[3,16,64,128]{3,2,1,0:T(8,128)(2,1)S(1)}, bf16[3,16,64,128]{3,2,1,0:T(8,128)(2,1)}, u32[]{:S(2)}) copy-start(bf16[3,16,64,128]{3,2,1,0:T(8,128)(2,1)} %param.6) | copy-start | bytes 2359300
  1.2 4.5 %collective-permute-start.4 = (bf16[3,4,2,64,128]{4,3,2,0,1:T(8,128)(2,1)S(1)}, bf16[3,4,2,64,128]{4,3,2,0,1:T(8,128)(2,1)S(1)}, u32[]{:S(2)}, u32[]{:S(2)}) collective-permute-start(bf16[3,4,2,64,128]{4,3,2,0,1:T(8,128)(2,1)S(1)} %copy_bitcast_fusion), channel_id=1, source_target_pairs={{0,1},{1,0},{2,3},{3,2},{4,5},{5,4},{6,7},{7,6},{8,9},{9,8},{10,11... | collective-permute-start | bytes 1179656 | tf_op jit(solution)/shard_map/ppermute | solution.py:191
  2.7 8.0 %collective-permute-start = (bf16[3,64,512]{2,1,0:T(8,128)(2,1)S(1)}, bf16[3,64,512]{2,1,0:T(8,128)(2,1)S(1)}, u32[]{:S(2)}, u32[]{:S(2)}) collective-permute-start(bf16[3,64,512]{2,1,0:T(8,128)(2,1)S(1)} %reshape.18), channel_id=1, source_target_pairs={{0,16},{16,0},{1,17},{17,1},{2,18},{18,2},{3,19},{19,3},{4,20},{20... | collective-permute-start | bytes 589832 | tf_op jit(solution)/shard_map/ppermute | solution.py:197
  5.6 23.9 %copy-start.1 = (s32[6]{0:T(128)S(1)}, s32[6]{0:T(128)}, u32[]{:S(2)}) copy-start(s32[6]{0:T(128)} %k_irrep.3) | copy-start | bytes 76
  5.6 23.9 %copy-start.2 = (s32[16]{0:T(128)S(1)}, s32[16]{0:T(128)}, u32[]{:S(2)}) copy-start(s32[16]{0:T(128)} %i_irrep.3) | copy-start | bytes 196
  5.7 23.9 %copy-start.3 = (s32[8]{0:T(128)S(1)}, s32[8]{0:T(128)}, u32[]{:S(2)}) copy-start(s32[8]{0:T(128)} %virt_count.3) | copy-start | bytes 100
  5.8 6.3 %collective-permute-start.5 = (bf16[2,3,2,64,128]{4,3,2,1,0:T(8,128)(2,1)S(1)}, bf16[2,3,2,64,128]{4,3,2,1,0:T(8,128)(2,1)S(1)}, u32[]{:S(2)}, u32[]{:S(2)}) collective-permute-start(bf16[2,3,2,64,128]{4,3,2,1,0:T(8,128)(2,1)S(1)} %get-tuple-element.34), channel_id=1, source_target_pairs={{0,2},{1,3},{2,0},{3,1},{4,6},{5,7},{6,4},{7,5},{8,10},{9,11},{10,... | collective-permute-start | bytes 589832 | tf_op jit(solution)/shard_map/ppermute | solution.py:191
  7.0 6.3 %collective-permute-start.6 = (bf16[2,3,2,64,128]{4,3,2,1,0:T(8,128)(2,1)S(1)}, bf16[2,3,2,64,128]{4,3,2,1,0:T(8,128)(2,1)S(1)}, u32[]{:S(2)}, u32[]{:S(2)}) collective-permute-start(bf16[2,3,2,64,128]{4,3,2,1,0:T(8,128)(2,1)S(1)} %get-tuple-element.35), channel_id=1, source_target_pairs={{0,4},{1,5},{2,6},{3,7},{4,0},{5,1},{6,2},{7,3},{8,12},{9,13},{10,... | collective-permute-start | bytes 589832 | tf_op jit(solution)/shard_map/ppermute | solution.py:191
  8.4 8.7 %collective-permute-start.7 = (bf16[2,3,2,64,128]{4,3,2,1,0:T(8,128)(2,1)S(1)}, bf16[2,3,2,64,128]{4,3,2,1,0:T(8,128)(2,1)S(1)}, u32[]{:S(2)}, u32[]{:S(2)}) collective-permute-start(bf16[2,3,2,64,128]{4,3,2,1,0:T(8,128)(2,1)S(1)} %get-tuple-element.36), channel_id=1, source_target_pairs={{0,6},{1,7},{2,4},{3,5},{4,2},{5,3},{6,0},{7,1},{8,14},{9,15},{10,... | collective-permute-start | bytes 589832 | tf_op jit(solution)/shard_map/ppermute | solution.py:191
  8.6 8.5 %collective-permute-start.8 = (bf16[2,3,2,64,128]{4,3,2,1,0:T(8,128)(2,1)S(1)}, bf16[2,3,2,64,128]{4,3,2,1,0:T(8,128)(2,1)S(1)}, u32[]{:S(2)}, u32[]{:S(2)}) collective-permute-start(bf16[2,3,2,64,128]{4,3,2,1,0:T(8,128)(2,1)S(1)} %get-tuple-element.33.refs_6_), channel_id=1, source_target_pairs={{0,16},{16,0},{1,17},{17,1},{2,18},{18,2},{3,19},{19,3},{4,20},{20... | collective-permute-start | bytes 589832 | tf_op jit(solution)/shard_map/ppermute | solution.py:197
  10.7 6.9 %collective-permute-start.3 = (bf16[6,64,512]{2,1,0:T(8,128)(2,1)S(1)}, bf16[6,64,512]{2,1,0:T(8,128)(2,1)S(1)}, u32[]{:S(2)}, u32[]{:S(2)}) collective-permute-start(bf16[6,64,512]{2,1,0:T(8,128)(2,1)S(1)} %constant_dynamic-update-slice_fusion.refs_0_), channel_id=1, source_target_pairs={{0,1},{1,0},{2,3},{3,2},{4,5},{5,4},{6,7},{7,6},{8,9},{9,8},{10,11... | collective-permute-start | bytes 1179656 | tf_op jit(solution)/shard_map/ppermute | solution.py:191
  12.0 13.5 %collective-permute-start.2 = (bf16[6,64,512]{2,1,0:T(8,128)(2,1)S(1)}, bf16[6,64,512]{2,1,0:T(8,128)(2,1)S(1)}, u32[]{:S(2)}, u32[]{:S(2)}) collective-permute-start(bf16[6,64,512]{2,1,0:T(8,128)(2,1)S(1)} %constant_dynamic-update-slice_fusion.refs_0_), channel_id=1, source_target_pairs={{0,4},{1,5},{2,6},{3,7},{4,0},{5,1},{6,2},{7,3},{8,12},{9,13},{10,... | collective-permute-start | bytes 1179656 | tf_op jit(solution)/shard_map/ppermute | solution.py:191
  13.3 12.4 %collective-permute-start.1 = (bf16[6,64,512]{2,1,0:T(8,128)(2,1)S(1)}, bf16[6,64,512]{2,1,0:T(8,128)(2,1)S(1)}, u32[]{:S(2)}, u32[]{:S(2)}) collective-permute-start(bf16[6,64,512]{2,1,0:T(8,128)(2,1)S(1)} %constant_dynamic-update-slice_fusion.refs_0_), channel_id=1, source_target_pairs={{0,2},{1,3},{2,0},{3,1},{4,6},{5,7},{6,4},{7,5},{8,10},{9,11},{10,... | collective-permute-start | bytes 1179656 | tf_op jit(solution)/shard_map/ppermute | solution.py:191
  17.2 16.8 %collective-permute-start.9 = (bf16[3,2,3,2,64,128]{5,4,3,2,1,0:T(8,128)(2,1)S(1)}, bf16[3,2,3,2,64,128]{5,4,3,2,1,0:T(8,128)(2,1)S(1)}, u32[]{:S(2)}, u32[]{:S(2)}) collective-permute-start(bf16[3,2,3,2,64,128]{5,4,3,2,1,0:T(8,128)(2,1)S(1)} %pad_maximum_fusion), channel_id=1, source_target_pairs={{0,16},{16,0},{1,17},{17,1},{2,18},{18,2},{3,19},{19,3},{4,20},{20... | collective-permute-start | bytes 1769480 | tf_op jit(solution)/shard_map/ppermute | solution.py:197
  25.8 3.8 %collective-permute-start.10 = (bf16[6,64,512]{2,1,0:T(8,128)(2,1)S(1)}, bf16[6,64,512]{2,1,0:T(8,128)(2,1)S(1)}, u32[]{:S(2)}, u32[]{:S(2)}) collective-permute-start(bf16[6,64,512]{2,1,0:T(8,128)(2,1)S(1)} %collective-permute-done.1.refs_1_.refs_0_), channel_id=1, source_target_pairs={{0,1},{1,0},{2,3},{3,2},{4,5},{5,4},{6,7},{7,6},{8,9},{9,8},{10,11... | collective-permute-start | bytes 1179656 | tf_op jit(solution)/shard_map/ppermute | solution.py:191
  27.0 2.6 %collective-permute-start.11 = (bf16[6,64,512]{2,1,0:T(8,128)(2,1)S(1)}, bf16[6,64,512]{2,1,0:T(8,128)(2,1)S(1)}, u32[]{:S(2)}, u32[]{:S(2)}) collective-permute-start(bf16[6,64,512]{2,1,0:T(8,128)(2,1)S(1)} %collective-permute-done.2.refs_2_.refs_1_), channel_id=1, source_target_pairs={{0,1},{1,0},{2,3},{3,2},{4,5},{5,4},{6,7},{7,6},{8,9},{9,8},{10,11... | collective-permute-start | bytes 1179656 | tf_op jit(solution)/shard_map/ppermute | solution.py:191
  27.0 10.0 %copy-start.4 = (s32[8]{0:T(128)S(1)}, s32[8]{0:T(128)}, u32[]{:S(2)}) copy-start(s32[8]{0:T(128)} %j_irrep.1) | copy-start | bytes 100
  27.1 6.0 %collective-permute-start.13 = (bf16[3,64,512]{2,1,0:T(8,128)(2,1)S(1)}, bf16[3,64,512]{2,1,0:T(8,128)(2,1)S(1)}, u32[]{:S(2)}, u32[]{:S(2)}) collective-permute-start(bf16[3,64,512]{2,1,0:T(8,128)(2,1)S(1)} %slice.23), channel_id=1, source_target_pairs={{0,2},{1,3},{2,0},{3,1},{4,6},{5,7},{6,4},{7,5},{8,10},{9,11},{10,... | collective-permute-start | bytes 589832 | tf_op jit(solution)/shard_map/ppermute | solution.py:191
  28.3 5.6 %collective-permute-start.12 = (bf16[3,64,512]{2,1,0:T(8,128)(2,1)S(1)}, bf16[3,64,512]{2,1,0:T(8,128)(2,1)S(1)}, u32[]{:S(2)}, u32[]{:S(2)}) collective-permute-start(bf16[3,64,512]{2,1,0:T(8,128)(2,1)S(1)} %slice.22), channel_id=1, source_target_pairs={{0,4},{1,5},{2,6},{3,7},{4,0},{5,1},{6,2},{7,3},{8,12},{9,13},{10,... | collective-permute-start | bytes 589832 | tf_op jit(solution)/shard_map/ppermute | solution.py:191
  33.9 2.8 %collective-permute-start.14 = (bf16[3,64,512]{2,1,0:T(8,128)(2,1)S(1)}, bf16[3,64,512]{2,1,0:T(8,128)(2,1)S(1)}, u32[]{:S(2)}, u32[]{:S(2)}) collective-permute-start(bf16[3,64,512]{2,1,0:T(8,128)(2,1)S(1)} %collective-permute-done.12.refs_2_), channel_id=1, source_target_pairs={{0,1},{1,0},{2,3},{3,2},{4,5},{5,4},{6,7},{7,6},{8,9},{9,8},{10,11... | collective-permute-start | bytes 589832 | tf_op jit(solution)/shard_map/ppermute | solution.py:191
  35.6 1.4 %collective-permute-start.15 = (bf16[3,64,512]{2,1,0:T(8,128)(2,1)S(1)}, bf16[3,64,512]{2,1,0:T(8,128)(2,1)S(1)}, u32[]{:S(2)}, u32[]{:S(2)}) collective-permute-start(bf16[3,64,512]{2,1,0:T(8,128)(2,1)S(1)} %collective-permute-done.13.refs_3_), channel_id=1, source_target_pairs={{0,1},{1,0},{2,3},{3,2},{4,5},{5,4},{6,7},{7,6},{8,9},{9,8},{10,11... | collective-permute-start | bytes 589832 | tf_op jit(solution)/shard_map/ppermute | solution.py:191
